TPU v7x, 256 devices: a whole 4x4x8 slice. The times are simulated.
256 devices in a mesh: seq: 32 (over y, z_hi, core), mp: 8 (over z_lo, x).
Axes of the slice: x: 4, y: 4, z: 8 (z_hi: 4, z_lo: 2; z = z_hi * 2 + z_lo), core: 2. Of those that a mesh axis runs over, the one named last changes fastest.
Arguments:
- frames_in: bfloat16 [5632, 1536], P(('seq', 'mp')), may hold values from -6 to 6
- attn_gain: float32 [1536], replicated, may hold values from 0.25 to 1.75
- attn_shift: float32 [1536], replicated, may hold values from -3 to 3
- w_qkv: bfloat16 [3, 1536, 1536], P(None, 'mp'), may hold values from -0.76546554 to 0.76546554
- w_attn_out: bfloat16 [1536, 1536], P('mp'), may hold values from -2.5 to 2.5
- conv_gain: float32 [1536], replicated, may hold values from 0.25 to 1.75
- conv_shift: float32 [1536], replicated, may hold values from -3 to 3
- w_pointwise_in: bfloat16 [2, 1536, 1536], P(None, 'mp'), may hold values from -0.15625 to 0.15625
- depth_kernel: float32 [31, 1536], P(None, 'mp'), may hold values from -2 to 2
- norm_scale: float32 [1536], P('mp'), may hold values from 0.5 to 2
- norm_offset: float32 [1536], P('mp'), may hold values from -3 to 3
- w_pointwise_out: bfloat16 [1536, 1536], P('mp'), may hold values from -0.15625 to 0.15625
Outputs:
- block_out: bfloat16 [5632, 1536], P(('seq', 'mp'))
All inputs are finite; a program needn't handle non-finite values.
Results may differ from a plain program's by a relative error of at most 0.018.
The roundings to bfloat16 on the way count: a program that leaves them out, or rounds other values in their place, can miss the bound.
Values may be sent and summed in bfloat16 or wider, within the bound.
No kernel may reach another device: no remote copies, remote signals or barrier semaphores. Data moves between devices by JAX's collectives and lax.ppermute only.
A program may use at most 64 MiB of HBM per device.

v0:
```python
import jax
import jax.numpy as jnp
from jax import lax
from jax.sharding import PartitionSpec as P

D = 1536
HEADS = 16


def padded_2(cells, sides, width):
    for axis, dim in sides:
        count = lax.axis_size(axis)
        ends = count - 1
        head = lax.slice_in_dim(cells, 0, width, axis=dim)
        tail = lax.slice_in_dim(cells, cells.shape[dim] - width, cells.shape[dim], axis=dim)
        cells = jnp.concatenate(
            [
                lax.ppermute(tail, axis, [(i, (i + 1) % count) for i in range(ends)]),
                cells,
                lax.ppermute(head, axis, [((i + 1) % count, i) for i in range(ends)]),
            ],
            axis=dim,
        )
    return cells


def layer_norm(values, gain, shift):
    vf = values.astype(jnp.float32)
    center = vf - jnp.mean(vf, axis=-1, keepdims=True)
    spread = jnp.mean(center * center, axis=-1, keepdims=True)
    return (center * lax.rsqrt(spread + 1e-05) * gain + shift).astype(jnp.bfloat16)


def rotate(tensor, positions):
    half = tensor.shape[-1] // 2
    freq = 10000.0 ** (-jnp.arange(half).astype(jnp.float32) / half)
    angle = positions.astype(jnp.float32)[:, None] * freq[None, :]
    cosine = jnp.cos(angle)[:, None, :]
    sine = jnp.sin(angle)[:, None, :]
    first = tensor[..., :half]
    second = tensor[..., half:]
    return jnp.concatenate(
        [first * cosine - second * sine, first * sine + second * cosine], axis=-1
    )


def project_out_in(inputs, weight):
    return lax.dot_general(
        inputs, weight, (((1,), (1,)), ((), ())), preferred_element_type=jnp.float32
    )


def attend_block(carry, queries, key_block, value_block, scale):
    run_max, run_total, run_acc = carry
    scores = (
        jnp.einsum("qhd,khd->qhk", queries, key_block, preferred_element_type=jnp.float32) * scale
    )
    new_max = jnp.maximum(run_max, jnp.max(scores, axis=-1))
    weights = jnp.exp(scores - new_max[..., None])
    decay = jnp.exp(run_max - new_max)
    new_total = run_total * decay + jnp.sum(weights, axis=-1)
    mixed = jnp.einsum(
        "qhk,khd->qhd",
        weights.astype(jnp.bfloat16),
        value_block,
        preferred_element_type=jnp.float32,
    )
    return (new_max, new_total, run_acc * decay[..., None] + mixed)


def attend(carry, queries, key_piece, value_piece, scale):
    count = key_piece.shape[0]
    blocks = 1
    key_steps = key_piece.reshape(blocks, count // blocks, key_piece.shape[1], key_piece.shape[2])
    value_steps = value_piece.reshape(
        blocks, count // blocks, value_piece.shape[1], value_piece.shape[2]
    )

    def step(state, pair):
        return (attend_block(state, queries, pair[0], pair[1], scale), None)

    result, unused = lax.scan(step, carry, (key_steps, value_steps))
    return result


def local(
    frames_in,
    attn_gain,
    attn_shift,
    w_qkv,
    w_attn_out,
    conv_gain,
    conv_shift,
    w_pointwise_in,
    depth_kernel,
    norm_scale,
    norm_offset,
    w_pointwise_out,
):
    local_width = w_qkv.shape[1]
    local_heads = HEADS // lax.axis_size("mp")
    head_dim = D // HEADS
    scale = 1.0 / head_dim**0.5
    whole_in = lax.all_gather(frames_in, "mp", axis=0, tiled=True)
    frame_count = whole_in.shape[0]
    attn_in = layer_norm(whole_in, attn_gain, attn_shift)
    positions = lax.axis_index("seq") * frame_count + jnp.arange(frame_count)
    projected = [
        project_out_in(attn_in, w_qkv[slot]).reshape(frame_count, local_heads, head_dim)
        for slot in range(3)
    ]
    queries = rotate(projected[0], positions).astype(jnp.bfloat16)
    keys = rotate(projected[1], positions).astype(jnp.bfloat16)
    values = projected[2].astype(jnp.bfloat16)
    start_state = (
        jnp.full((frame_count, local_heads), -1e30, jnp.float32),
        jnp.zeros((frame_count, local_heads), jnp.float32),
        jnp.zeros((frame_count, local_heads, head_dim), jnp.float32),
    )
    run_max, run_total, run_acc = attend(
        start_state,
        queries,
        lax.all_gather(keys, "seq", axis=0, tiled=True),
        lax.all_gather(values, "seq", axis=0, tiled=True),
        scale,
    )
    context = (
        (run_acc / run_total[..., None]).astype(jnp.bfloat16).reshape(frame_count, local_width)
    )
    partial_attn = jnp.dot(context, w_attn_out, preferred_element_type=jnp.float32)
    attn_part = lax.psum_scatter(
        partial_attn.astype(jnp.bfloat16), "mp", scatter_dimension=0, tiled=True
    ).astype(jnp.float32)
    mid = (frames_in.astype(jnp.float32) + attn_part).astype(jnp.bfloat16)
    whole_mid = lax.all_gather(mid, "mp", axis=0, tiled=True)
    conv_in = layer_norm(whole_mid, conv_gain, conv_shift)
    value_half = project_out_in(conv_in, w_pointwise_in[0])
    gate_half = project_out_in(conv_in, w_pointwise_in[1])
    glu = (value_half * jax.nn.sigmoid(gate_half)).astype(jnp.bfloat16)
    taps = depth_kernel.shape[0]
    padded = padded_2(glu, (("seq", 0),), taps // 2)
    depth = jnp.zeros((frame_count, local_width), jnp.float32)
    for tap in range(taps):
        depth = depth + padded[tap : tap + frame_count].astype(jnp.float32) * depth_kernel[tap]
    normed = depth * norm_scale + norm_offset
    swish = (normed * jax.nn.sigmoid(normed)).astype(jnp.bfloat16)
    partial_conv = jnp.dot(swish, w_pointwise_out, preferred_element_type=jnp.float32)
    conv_part = lax.psum_scatter(
        partial_conv.astype(jnp.bfloat16), "mp", scatter_dimension=0, tiled=True
    ).astype(jnp.float32)
    return (mid.astype(jnp.float32) + conv_part).astype(jnp.bfloat16)


def solution(mesh):
    placed = (
        P(("seq", "mp"), None),
        P(),
        P(),
        P(None, "mp", None),
        P("mp", None),
        P(),
        P(),
        P(None, "mp", None),
        P(None, "mp"),
        P("mp"),
        P("mp"),
        P("mp", None),
    )
    return jax.shard_map(
        local, mesh=mesh, in_specs=placed, out_specs=P(("seq", "mp"), None), check_vma=False
    )
```

profile of v0, /device:TPU:24, one launch (start us, length us, event | category | flops | bytes accessed | tf_op | source)
XLA Modules:
  0.0 268.8 jit_solution(18006487947794246170)
XLA Ops:
  6.5 30.3 %all-gather = bf16[8,22,1536]{2,1,0:T(8,128)(2,1)S(1)} all-gather(bf16[1,22,1536]{2,1,0:T(8,128)(2,1)} %bitcast.74), channel_id=1, replica_groups=mesh['seq'=32,'mp'=8] {'mp'}, dimensions={0}, use_global_device_ids=true | all-gather | bytes 608256 | tf_op jit(solution)/shard_map/all_gather | solution.py:104
  36.8 0.1 reshape.125
  36.9 0.2 convert_reduce_fusion.1
  37.1 0.1 reshape.130
  37.2 0.3 multiply_reduce_fusion.1
  37.5 1.5 fusion.65
  39.1 0.3 fusion.28
  39.3 0.4 fusion.70
  39.7 0.4 fusion.71
  40.1 0.4 multiply_cosine_fusion
  40.5 0.2 subtract_convert_fusion
  40.7 0.7 pad_maximum_fusion.2
  41.5 0.0 all-gather.5.cloned.1.call-update
  41.5 0.0 all-gather.7.cloned.1.call-start
  41.5 1.0 convolution_convert_fusion.2
  42.5 0.0 all-gather.7.cloned.1.call-update
  42.6 56.3 %all-gather.5.cloned.1.call-done = bf16[5632,2,96]{2,0,1:T(8,128)(2,1)} async-done(((bf16[176,2,96]{2,0,1:T(8,128)(2,1)}), bf16[5632,2,96]{2,0,1:T(8,128)(2,1)}) %all-gather.5.cloned.1.call-update) | async-done | bytes 2162704 | tf_op jit(solution)/shard_map/all_gather | solution.py:123
  98.9 3.1 %fusion.69 = (f32[176,2]{0,1:T(2,128)S(1)}, f32[176,2,5632]{2,0,1:T(8,128)S(1)}) fusion(bf16[5632,2,96]{2,0,1:T(8,128)(2,1)} %all-gather.5.cloned.1.call-done, bf16[176,2,48]{2,0,1:T(8,128)(2,1)S(1)} %get-tuple-element.28, bf16[176,2,48]{2,0,1:T(8,128)(2,1)S(1)} %get-tuple-element.20), kind=kOutput, calls=%fused_computation.138 | convolution fusion | flops 384732832 | bytes 10161536 | tf_op jit(solution)/shard_map/while/body/eval_jaxpr/qhd,khd->qhk/dot_general | solution.py:56
  102.0 1.2 fusion.3
  103.2 1.9 copy-done.1
  105.1 50.5 %all-gather.7.cloned.1.call-done = bf16[5632,2,96]{2,0,1:T(8,128)(2,1)} async-done(((bf16[176,2,96]{2,0,1:T(8,128)(2,1)}), bf16[5632,2,96]{2,0,1:T(8,128)(2,1)}) %all-gather.7.cloned.1.call-update) | async-done | bytes 2162704 | tf_op jit(solution)/shard_map/all_gather | solution.py:124
  155.6 5.4 %fusion.21 = bf16[176,2,96]{2,0,1:T(8,128)(2,1)S(1)} fusion(bf16[5632,2,96]{2,0,1:T(8,128)(2,1)} %all-gather.7.cloned.1.call-done, f32[176,2,5632]{2,0,1:T(8,128)} %copy-done.1, f32[176,2]{0,1:T(2,128)S(1)} %broadcast_maximum_fusion, f32[176,2]{0,1:T(2,128)S(1)} %get-tuple-element.69, f32[176,2]{0,1:T(2,128)S(1)} %get-tuple-element.68), kind=kOutput, calls=%fused_computation.19 | convolution fusion | flops 384699392 | bytes 10164352 | tf_op jit(solution)/shard_map/while/body/eval_jaxpr/qhk,khd->qhd/dot_general | solution.py:62
  161.1 0.1 copy.14
  161.2 0.1 reshape.120
  161.3 0.3 convolution_convert_fusion.1
  161.6 23.2 %fusion = bf16[24,1536]{1,0:T(8,128)(2,1)S(1)} fusion(bf16[176,1536]{1,0:T(8,128)(2,1)S(1)} %convolution_convert_fusion.1), kind=kCustom, calls=%all-reduce-scatter | all-reduce-scatter fusion | flops 294913 | bytes 615424
  184.8 3.4 %collective-permute-start.2 = (bf16[14,1536]{1,0:T(8,128)(2,1)S(1)}, bf16[14,1536]{1,0:T(8,128)(2,1)S(1)}, u32[]{:S(2)}, u32[]{:S(2)}) collective-permute-start(bf16[14,1536]{1,0:T(8,128)(2,1)S(1)} %slice.380), channel_id=1, source_target_pairs={{0,1},{1,2},{2,3},{3,4},{4,5},{5,6},{6,7},{8,9},{9,10},{10,11},{11... | collective-permute-start | bytes 129032
  188.3 0.6 dynamic-slice.8
  189.5 0.4 collective-permute-done.2
  189.9 0.2 concatenate.47
  190.2 29.3 %all-gather.1 = bf16[8,22,1536]{2,1,0:T(8,128)(2,1)S(1)} all-gather(bf16[1,22,1536]{2,1,0:T(8,128)(2,1)S(1)} %fusion.60), channel_id=1, replica_groups=mesh['seq'=32,'mp'=8] {'mp'}, dimensions={0}, use_global_device_ids=true | all-gather | bytes 608256 | tf_op jit(solution)/shard_map/all_gather | solution.py:135
  219.5 0.1 reshape.126
  219.6 0.2 convert_reduce_fusion
  219.8 0.1 reshape.132
  219.9 0.3 multiply_reduce_fusion
  220.1 0.1 copy-done.9
  220.3 0.0 copy-done.10
  220.3 1.6 fusion.10
  221.9 0.4 fusion.17
  222.3 1.9 collective-permute-start
  224.2 6.7 %collective-permute-start.1 = (bf16[15,192]{1,0:T(8,128)(2,1)S(1)}, bf16[15,192]{1,0:T(8,128)(2,1)S(1)}, u32[]{:S(2)}, u32[]{:S(2)}) collective-permute-start(bf16[15,192]{1,0:T(8,128)(2,1)S(1)} %get-tuple-element.36), channel_id=1, source_target_pairs={{8,0},{16,8},{24,16},{32,24},{40,32},{48,40},{56,48},{64,56},{72,6... | collective-permute-start | bytes 17288 | tf_op jit(solution)/shard_map/ppermute | solution.py:20
  230.9 1.3 collective-permute-done.1
  232.3 1.0 convolution_convert_fusion
  233.3 23.5 %fusion.1 = bf16[24,1536]{1,0:T(8,128)(2,1)S(1)} fusion(bf16[176,1536]{1,0:T(8,128)(2,1)S(1)} %convolution_convert_fusion), kind=kCustom, calls=%all-reduce-scatter.1 | all-reduce-scatter fusion | flops 294913 | bytes 615424
  256.9 2.5 collective-permute-start.3
  259.3 1.7 collective-permute-done.3
  261.1 0.2 concatenate.48
  261.2 0.7 add_convert_fusion.4
  (39 shorter events, 0.2 us)
Async XLA Ops:
  6.5 154.7 %copy-start = (bf16[192,1536]{1,0:T(8,128)(2,1)S(1)}, bf16[192,1536]{1,0:T(8,128)(2,1)}, u32[]{:S(2)}) copy-start(bf16[192,1536]{1,0:T(8,128)(2,1)} %param.16) | copy-start | bytes 1769476
  6.5 92.3 %all-gather.5.cloned.1.call-start = ((), (), s32[]{:S(2)}) async-start(), calls=%async_computation | async-start | bytes 2973696 | tf_op jit(solution)/shard_map/all_gather | solution.py:123
  37.5 1.6 copy-start.4
  37.5 1.6 copy-start.5
  41.5 114.1 %all-gather.7.cloned.1.call-start = ((), (), s32[]{:S(2)}) async-start(), calls=%async_computation.1 | async-start | bytes 2973696 | tf_op jit(solution)/shard_map/all_gather | solution.py:124
  102.0 3.1 %copy-start.1 = (f32[176,2,5632]{2,0,1:T(8,128)}, f32[176,2,5632]{2,0,1:T(8,128)S(1)}, u32[]{:S(2)}) copy-start(f32[176,2,5632]{2,0,1:T(8,128)S(1)} %get-tuple-element.73) | copy-start | bytes 23789572
  161.1 27.1 %copy-start.3 = (f32[31,192]{1,0:T(8,128)S(1)}, f32[31,192]{1,0:T(8,128)}, u32[]{:S(2)}) copy-start(f32[31,192]{1,0:T(8,128)} %param.20) | copy-start | bytes 71428
  161.2 27.1 %copy-start.6 = (u32[256]{0:T(256)S(1)}, u32[256]{0:T(256)}, u32[]{:S(2)}) copy-start(u32[256]{0:T(256)} %constant.48) | copy-start | bytes 3076
  161.3 28.8 %copy-start.2 = (bf16[22,1536]{1,0:T(8,128)(2,1)S(1)}, bf16[22,1536]{1,0:T(8,128)(2,1)}, u32[]{:S(2)}) copy-start(bf16[22,1536]{1,0:T(8,128)(2,1)} %param.12) | copy-start | bytes 202756
  184.8 5.1 %collective-permute-start.2 = (bf16[14,1536]{1,0:T(8,128)(2,1)S(1)}, bf16[14,1536]{1,0:T(8,128)(2,1)S(1)}, u32[]{:S(2)}, u32[]{:S(2)}) collective-permute-start(bf16[14,1536]{1,0:T(8,128)(2,1)S(1)} %slice.380), channel_id=1, source_target_pairs={{0,1},{1,2},{2,3},{3,4},{4,5},{5,6},{6,7},{8,9},{9,10},{10,11},{11... | collective-permute-start | bytes 129032
  219.6 0.7 copy-start.9
  219.6 0.7 copy-start.10
  220.3 1.6 copy-start.7
  221.9 10.4 %copy-start.8 = (bf16[192,1536]{1,0:T(8,128)(2,1)S(1)}, bf16[192,1536]{1,0:T(8,128)(2,1)}, u32[]{:S(2)}) copy-start(bf16[192,1536]{1,0:T(8,128)(2,1)} %param.23) | copy-start | bytes 1769476
  221.9 10.4 %copy-start.11 = (f32[192]{0:T(256)S(1)}, f32[192]{0:T(256)}, u32[]{:S(2)}) copy-start(f32[192]{0:T(256)} %param.22) | copy-start | bytes 2308
  221.9 10.3 %copy-start.12 = (f32[192]{0:T(256)S(1)}, f32[192]{0:T(256)}, u32[]{:S(2)}) copy-start(f32[192]{0:T(256)} %param.21) | copy-start | bytes 2308
  222.3 8.6 %collective-permute-start = (bf16[15,192]{1,0:T(8,128)(2,1)S(1)}, bf16[15,192]{1,0:T(8,128)(2,1)S(1)}, u32[]{:S(2)}, u32[]{:S(2)}) collective-permute-start(bf16[15,192]{1,0:T(8,128)(2,1)S(1)} %get-tuple-element.35), channel_id=1, source_target_pairs={{0,8},{8,16},{16,24},{24,32},{32,40},{40,48},{48,56},{56,64},{64,7... | collective-permute-start | bytes 17288 | tf_op jit(solution)/shard_map/ppermute | solution.py:18
  224.2 8.0 %collective-permute-start.1 = (bf16[15,192]{1,0:T(8,128)(2,1)S(1)}, bf16[15,192]{1,0:T(8,128)(2,1)S(1)}, u32[]{:S(2)}, u32[]{:S(2)}) collective-permute-start(bf16[15,192]{1,0:T(8,128)(2,1)S(1)} %get-tuple-element.36), channel_id=1, source_target_pairs={{8,0},{16,8},{24,16},{32,24},{40,32},{48,40},{56,48},{64,56},{72,6... | collective-permute-start | bytes 17288 | tf_op jit(solution)/shard_map/ppermute | solution.py:20
  256.9 4.2 %collective-permute-start.3 = (bf16[14,1536]{1,0:T(8,128)(2,1)S(1)}, bf16[14,1536]{1,0:T(8,128)(2,1)S(1)}, u32[]{:S(2)}, u32[]{:S(2)}) collective-permute-start(bf16[14,1536]{1,0:T(8,128)(2,1)S(1)} %slice.381), channel_id=1, source_target_pairs={{0,1},{1,2},{2,3},{3,4},{4,5},{5,6},{6,7},{8,9},{9,10},{10,11},{11... | collective-permute-start | bytes 129032
Sparse Core Ops, SparseCore 0:
  41.6 57.2 all-gather.4
  101.5 54.0 all-gather.6
where the time goes:
time: 274 us; the launch traced here: 269 us
  waiting for transfers between devices  110 us (40%)
  blocking collectives  106 us (39%)
  between operations  14.5 us (5%)
  starting transfers between devices  14.4 us (5%)
  matrix products  13.6 us (5%)
  local copies, waits for them, and re-layouts  5.21 us (2%)
  other arithmetic  4.42 us (2%)
    all_gather x1, waiting for transfers between devices, local(): lax.all_gather(keys, 'seq', axis=0, tiled=True)  56.3 us
    all_gather x1, waiting for transfers between devices, local(): lax.all_gather(values, 'seq', axis=0, tiled=True)  50.5 us
    unnamed x2, blocking collectives  46.7 us
    all_gather x1, blocking collectives, local(): whole_in = lax.all_gather(frames_in, 'mp', axis=0, tiled=True)  30.3 us
    all_gather x1, blocking collectives, local(): whole_mid = lax.all_gather(mid, 'mp', axis=0, tiled=True)  29.3 us
    ppermute x1, starting transfers between devices, padded_2(): lax.ppermute(head, axis, [((i + 1) % count, i) for i in range(ends)])  6.65 us
    unnamed x2, starting transfers between devices  5.82 us
  transfers between devices with their start and end apart: 6, of which 5 were waited for; matrix products, arithmetic and copies ran while one was open for 2% of the time, Pallas kernels for 0%

commit v1 on v0

v1 whole, which is shorter than its diff:
```python
import jax
import jax.numpy as jnp
from jax import lax
from jax.sharding import PartitionSpec as P

D = 1536
HEADS = 16
HEAD = D // HEADS
ROWS = 22
PEERS = 8
BLOCK = ROWS * PEERS
TAPS = 31
REACH = TAPS // 2
F32 = jnp.float32
BF16 = jnp.bfloat16


def hop(array, place):
    count = lax.axis_size("seq")
    return lax.ppermute(array, "seq", [(i, place(i)) for i in range(count)])


def along_y(step):
    return lambda i: (i + 8 * step) % 32


def along_z(step):
    return lambda i: (i // 8) * 8 + (i % 8 + 2 * step) % 8


def other_core(i):
    return i ^ 1


def layer_norm(values, gain, shift):
    vf = values.astype(F32)
    center = vf - jnp.mean(vf, axis=-1, keepdims=True)
    spread = jnp.mean(center * center, axis=-1, keepdims=True)
    return (center * lax.rsqrt(spread + 1e-05) * gain + shift).astype(BF16)


def rotate(tensor, cosine, sine):
    half = HEAD // 2
    first = tensor[..., :half]
    second = tensor[..., half:]
    return jnp.concatenate(
        [first * cosine - second * sine, first * sine + second * cosine], axis=-1
    )


def project_out_in(inputs, weight):
    return lax.dot_general(inputs, weight, (((1,), (1,)), ((), ())), preferred_element_type=F32)


def gather_frames(own):
    spread = jnp.broadcast_to(own[None], (PEERS,) + own.shape)
    return lax.all_to_all(spread, "mp", 0, 0, tiled=False).reshape(BLOCK, own.shape[-1])


def scatter_sum(partial):
    sent = partial.astype(BF16).reshape(PEERS, ROWS, D)
    return jnp.sum(lax.all_to_all(sent, "mp", 0, 0, tiled=False).astype(F32), axis=0)


def split3(value):
    high = lax.reduce_precision(value, 8, 7)
    middle = lax.reduce_precision(value - high, 8, 7)
    low = value - high - middle
    return jnp.concatenate([high, middle, low], axis=-1).astype(BF16)


def local(
    frames_in,
    attn_gain,
    attn_shift,
    w_qkv,
    w_attn_out,
    conv_gain,
    conv_shift,
    w_pointwise_in,
    depth_kernel,
    norm_scale,
    norm_offset,
    w_pointwise_out,
):
    width = w_qkv.shape[1]
    heads = width // HEAD
    scale = 1.0 / HEAD**0.5
    attn_in = gather_frames(layer_norm(frames_in, attn_gain, attn_shift))
    positions = lax.axis_index("seq") * BLOCK + jnp.arange(BLOCK)
    half = HEAD // 2
    freq = 10000.0 ** (-jnp.arange(half).astype(F32) / half)
    angle = positions.astype(F32)[:, None] * freq[None, :]
    cosine, sine = jnp.cos(angle)[:, None, :], jnp.sin(angle)[:, None, :]
    projected = [
        project_out_in(attn_in, w_qkv[slot]).reshape(BLOCK, heads, HEAD) for slot in range(3)
    ]
    queries = rotate(projected[0], cosine, sine).astype(BF16).reshape(BLOCK, width)
    keys = rotate(projected[1], cosine, sine).astype(BF16).reshape(BLOCK, width)
    values = projected[2].astype(BF16).reshape(BLOCK, width)

    packed = jnp.concatenate([queries[: BLOCK // 2], queries[BLOCK // 2 :]], axis=1)
    pair = jnp.concatenate([keys, values], axis=1)
    steps = (2, 1, -1)
    q_got = [hop(packed, along_z(step)) for step in steps]
    kv_got = [hop(pair, along_y(step)) for step in steps]
    kv_mine = jnp.stack([pair] + kv_got)
    kv_all = jnp.concatenate([kv_mine, hop(kv_mine, other_core)]).reshape(-1, 2, heads, HEAD)
    q_all = jnp.stack(
        [queries] + [jnp.concatenate([q[:, :width], q[:, width:]], axis=0) for q in q_got]
    ).reshape(-1, heads, HEAD)
    scores = (
        jnp.einsum("qhd,khd->hqk", q_all, kv_all[:, 0], preferred_element_type=F32) * scale
    )
    top = jnp.max(scores, axis=-1, keepdims=True)
    weights = jnp.exp(scores - top)
    total = jnp.sum(weights, axis=-1, keepdims=True)
    mixed = jnp.einsum(
        "hqk,khd->hqd", weights.astype(BF16), kv_all[:, 1], preferred_element_type=F32
    )
    part = (mixed / total).astype(BF16)
    level = top + jnp.log(total)
    part = jnp.transpose(part, (1, 0, 2)).reshape(4, BLOCK, width)
    level = jnp.transpose(level[..., 0]).reshape(4, BLOCK, heads)
    sent = jnp.concatenate([part, split3(level)], axis=-1)
    back = jnp.stack([sent[0]] + [hop(sent[n + 1], along_z(-step)) for n, step in enumerate(steps)])
    level = back[:, :, width:].astype(F32).reshape(4, BLOCK, 3, heads).sum(axis=2)
    share = jnp.exp(level - jnp.max(level, axis=0))
    share = share / jnp.sum(share, axis=0)
    part = back[:, :, :width].astype(F32).reshape(4, BLOCK, heads, HEAD)
    context = jnp.sum(part * share[..., None], axis=0).astype(BF16).reshape(BLOCK, width)

    attn = scatter_sum(jnp.dot(context, w_attn_out, preferred_element_type=F32))
    mid = (frames_in.astype(F32) + attn).astype(BF16)
    conv_in = gather_frames(layer_norm(mid, conv_gain, conv_shift))
    value_half = project_out_in(conv_in, w_pointwise_in[0])
    gate_half = project_out_in(conv_in, w_pointwise_in[1])
    glu = (value_half * jax.nn.sigmoid(gate_half)).astype(BF16)
    count = lax.axis_size("seq")
    ahead = lax.ppermute(glu[-REACH:], "seq", [(i, i + 1) for i in range(count - 1)])
    behind = lax.ppermute(glu[:REACH], "seq", [(i + 1, i) for i in range(count - 1)])
    padded = jnp.concatenate([ahead, glu, behind], axis=0)
    depth = jnp.zeros((BLOCK, width), F32)
    for tap in range(TAPS):
        depth = depth + padded[tap : tap + BLOCK].astype(F32) * depth_kernel[tap]
    normed = depth * norm_scale + norm_offset
    swish = (normed * jax.nn.sigmoid(normed)).astype(BF16)
    conv = scatter_sum(jnp.dot(swish, w_pointwise_out, preferred_element_type=F32))
    return (mid.astype(F32) + conv).astype(BF16)


def solution(mesh):
    placed = (
        P(("seq", "mp"), None),
        P(),
        P(),
        P(None, "mp", None),
        P("mp", None),
        P(),
        P(),
        P(None, "mp", None),
        P(None, "mp"),
        P("mp"),
        P("mp"),
        P("mp", None),
    )
    return jax.shard_map(
        local, mesh=mesh, in_specs=placed, out_specs=P(("seq", "mp"), None), check_vma=False
    )
```

time: 274 us -> 131 us (0.48); the launches traced: 269 us -> 130 us
  waiting for transfers between devices: 110 us -> 31.2 us
  blocking collectives: 106 us -> 27.4 us
  starting transfers between devices: 14.4 us -> 37.4 us
  between operations: 14.5 us -> 0.62 us
  local copies, waits for them, and re-layouts: 5.21 us -> 14.2 us
  other arithmetic: 4.42 us -> 10.1 us
  matrix products: 13.6 us -> 9.25 us
    all_gather x2 -> x0, waiting for transfers between devices: 107 us -> none  [the longest x1 56.3 us: local(): lax.all_gather(keys, 'seq', axis=0, tiled=True)]
    all_gather x2 -> x0, blocking collectives: 59.5 us -> none  [the longest x1 30.3 us: local(): whole_in = lax.all_gather(frames_in, 'mp', axis=0, tiled=True)]
    unnamed x2 -> x0, blocking collectives: 46.7 us -> none
    all_to_all x0 -> x2, blocking collectives: none -> 27.4 us  [scatter_sum(): lax.all_to_all(sent, 'mp', 0, 0, tiled=False).astype(F32)]
    ppermute x2 -> x12, starting transfers between devices: 8.57 us -> 28.1 us  [the longest x10 19.5 us: hop(): return lax.ppermute(array, 'seq', [(i, place(i)) for i in range(count)])]
    all_to_all x0 -> x2, waiting for transfers between devices: none -> 16 us  [gather_frames(): lax.all_to_all(spread, 'mp', 0, 0, tiled=False)]
    ppermute x2 -> x12, waiting for transfers between devices: 1.32 us -> 15.2 us  [the longest x10 13.9 us: hop(): return lax.ppermute(array, 'seq', [(i, place(i)) for i in range(count)])]
    all_to_all x0 -> x2, starting transfers between devices: none -> 9.32 us  [gather_frames(): lax.all_to_all(spread, 'mp', 0, 0, tiled=False)]
  transfers between devices with their start and end apart: 6 -> 14, of which waited for: 5 -> 9; matrix products, arithmetic and copies ran while one was open for 2% -> 5% of each run, Pallas kernels for 0% -> 0%
where the time goes in v1:
time: 131 us; the launch traced here: 130 us
  starting transfers between devices  37.4 us (29%)
  waiting for transfers between devices  31.2 us (24%)
  blocking collectives  27.4 us (21%)
  local copies, waits for them, and re-layouts  14.2 us (11%)
  other arithmetic  10.1 us (8%)
  matrix products  9.25 us (7%)
    all_to_all x2, blocking collectives, scatter_sum(): lax.all_to_all(sent, 'mp', 0, 0, tiled=False).astype(F32)  27.4 us
    ppermute x10, starting transfers between devices, hop(): return lax.ppermute(array, 'seq', [(i, place(i)) for i in range(count)])  19.5 us
    all_to_all x2, waiting for transfers between devices, gather_frames(): lax.all_to_all(spread, 'mp', 0, 0, tiled=False)  16 us
    ppermute x10, waiting for transfers between devices, hop(): return lax.ppermute(array, 'seq', [(i, place(i)) for i in range(count)])  13.9 us
    all_to_all x2, starting transfers between devices, gather_frames(): lax.all_to_all(spread, 'mp', 0, 0, tiled=False)  9.32 us
    ppermute x1, starting transfers between devices, local(): lax.ppermute(glu[:REACH], 'seq', [(i + 1, i) for i in range(count - 1)])  6.65 us
    dot_general x1, matrix products, local(): jnp.einsum('hqk,khd->hqd', weights.astype(BF16), kv_all[:, 1], preferred_...  4.8 us
    unnamed x31, local copies, waits for them, and re-layouts  4.21 us
  transfers between devices with their start and end apart: 14, of which 9 were waited for; matrix products, arithmetic and copies ran while one was open for 5% of the time, Pallas kernels for 0%

profile of v1, /device:TPU:24, one launch (start us, length us, event | category | flops | bytes accessed | tf_op | source)
XLA Modules:
  0.0 130.2 jit_solution(128972270595340048)
XLA Ops:
  0.0 1.1 convert_reduce_fusion.3
  1.1 1.1 fusion.39
  2.2 1.0 fusion.42
  3.2 0.9 broadcast_in_dim.4
  4.0 5.7 %all-to-all-start = ((bf16[8,22,1536]{2,1,0:T(8,128)(2,1)}), bf16[8,22,1536]{2,1,0:T(8,128)(2,1)S(1)}, u32[]{:S(2)}, u32[]{:S(2)}) async-start(bf16[8,22,1536]{2,1,0:T(8,128)(2,1)} %broadcast_in_dim.4), calls=%async_computation | async-start | bytes 1179648 | tf_op jit(solution)/shard_map/all_to_all | solution.py:57
  9.7 1.1 multiply_cosine_fusion
  10.8 1.5 %fusion.79 = (bf16[1,192,1536]{2,1,0:T(8,128)(2,1)S(1)}, bf16[1,192,1536]{2,1,0:T(8,128)(2,1)S(1)}, bf16[1,192,1536]{2,1,0:T(8,128)(2,1)S(1)}) fusion(bf16[3,192,1536]{2,1,0:T(8,128)(2,1)} %param.15), kind=kLoop, calls=%fused_computation.173 | loop fusion | bytes 3538944 | tf_op jit(solution)/shard_map/slice | solution.py:96
  12.3 7.4 %all-to-all-done = bf16[8,22,1536]{2,1,0:T(8,128)(2,1)S(1)} async-done(((bf16[8,22,1536]{2,1,0:T(8,128)(2,1)}), bf16[8,22,1536]{2,1,0:T(8,128)(2,1)S(1)}, u32[]{:S(2)}, u32[]{:S(2)}) %all-to-all-start) | async-done | bytes 540704 | tf_op jit(solution)/shard_map/all_to_all | solution.py:57
  19.9 0.4 fusion.90
  20.3 0.5 copy-done.4
  21.5 5.5 %collective-permute-start.2 = (bf16[88,384]{1,0:T(8,128)(2,1)S(1)}, bf16[88,384]{1,0:T(8,128)(2,1)S(1)}, u32[]{:S(2)}, u32[]{:S(2)}) collective-permute-start(bf16[88,384]{1,0:T(8,128)(2,1)S(1)} %pad_maximum_fusion.8), channel_id=1, source_target_pairs={{0,48},{8,56},{16,0},{24,8},{32,16},{40,24},{48,32},{56,40},{64,11... | collective-permute-start | bytes 202760 | tf_op jit(solution)/shard_map/ppermute | solution.py:20
  27.0 3.8 %collective-permute-start = (bf16[88,384]{1,0:T(8,128)(2,1)S(1)}, bf16[88,384]{1,0:T(8,128)(2,1)S(1)}, u32[]{:S(2)}, u32[]{:S(2)}) collective-permute-start(bf16[88,384]{1,0:T(8,128)(2,1)S(1)} %pad_maximum_fusion.8), channel_id=1, source_target_pairs={{0,32},{8,40},{16,48},{24,56},{32,0},{40,8},{48,16},{56,24},{64,96... | collective-permute-start | bytes 202760 | tf_op jit(solution)/shard_map/ppermute | solution.py:20
  30.8 0.4 convolution_convert_fusion.2
  31.2 0.4 fusion.91
  32.3 0.8 collective-permute-start.5
  33.1 2.5 %collective-permute-start.4 = (bf16[176,384]{1,0:T(8,128)(2,1)S(1)}, bf16[176,384]{1,0:T(8,128)(2,1)S(1)}, u32[]{:S(2)}, u32[]{:S(2)}) collective-permute-start(bf16[176,384]{1,0:T(8,128)(2,1)S(1)} %get-tuple-element.8), channel_id=1, source_target_pairs={{0,64},{8,72},{16,80},{24,88},{32,96},{40,104},{48,112},{56,120},{... | collective-permute-start | bytes 405512 | tf_op jit(solution)/shard_map/ppermute | solution.py:20
  36.3 1.0 reshape.184
  37.2 2.4 %collective-permute-done.5 = bf16[176,384]{1,0:T(8,128)(2,1)S(1)} collective-permute-done((bf16[176,384]{1,0:T(8,128)(2,1)S(1)}, bf16[176,384]{1,0:T(8,128)(2,1)S(1)}, u32[]{:S(2)}, u32[]{:S(2)}) %collective-permute-start.5) | collective-permute-done | bytes 135200 | tf_op jit(solution)/shard_map/ppermute | solution.py:20
  39.7 2.7 %collective-permute-done.3 = bf16[176,384]{1,0:T(8,128)(2,1)S(1)} collective-permute-done((bf16[176,384]{1,0:T(8,128)(2,1)S(1)}, bf16[176,384]{1,0:T(8,128)(2,1)S(1)}, u32[]{:S(2)}, u32[]{:S(2)}) %collective-permute-start.3) | collective-permute-done | bytes 135200 | tf_op jit(solution)/shard_map/ppermute | solution.py:20
  42.8 1.8 %collective-permute-done.6 = bf16[4,176,384]{2,1,0:T(8,128)(2,1)S(1)} collective-permute-done((bf16[4,176,384]{2,1,0:T(8,128)(2,1)S(1)}, bf16[4,176,384]{2,1,0:T(8,128)(2,1)S(1)}, u32[]{:S(2)}, u32[]{:S(2)}) %collective-permute-start.6) | collective-permute-done | bytes 540704 | tf_op jit(solution)/shard_map/ppermute | solution.py:20
  44.7 1.1 reshape.172
  45.8 1.0 fusion.80
  46.9 1.0 copy.95
  47.9 1.0 copy.94
  48.9 1.3 multiply_reduce_fusion
  50.2 1.6 %fusion.1 = f32[2,704]{1,0:T(2,128)S(1)} fusion(f32[2,704,1408]{2,1,0:T(8,128)S(1)} %get-tuple-element.69, f32[2,704]{1,0:T(2,128)S(1)} %get-tuple-element.68), kind=kLoop, calls=%fused_computation.3 | loop fusion | flops 5945984 | bytes 7941120 | tf_op jit(solution)/shard_map/reduce_sum | solution.py:117
  51.8 1.5 %copy-done.1 = f32[2,704,1408]{2,1,0:T(8,128)} copy-done((f32[2,704,1408]{2,1,0:T(8,128)}, f32[2,704,1408]{2,1,0:T(8,128)S(1)}, u32[]{:S(2)}) %copy-start.1) | copy-done | bytes 7929880
  53.4 4.8 %fusion.19 = bf16[704,2,96]{0,2,1:T(8,128)(2,1)S(1)} fusion(f32[2,704,1408]{2,1,0:T(8,128)} %copy-done.1, f32[2,704]{1,0:T(2,128)S(1)} %get-tuple-element.68, bf16[1408,1,2,96]{0,3,2,1:T(8,128)(2,1)S(1)} %copy.95, f32[704,2]{0,1:T(2,128)S(1)} %bitcast.114), kind=kOutput, calls=%fused_computation.23 | convolution fusion | flops 386850816 | bytes 8752128 | tf_op jit(solution)/shard_map/hqk,khd->hqd/dot_general | solution.py:118
  58.5 0.3 pad_maximum_fusion.1
  58.9 0.6 fusion.81
  59.8 2.8 %collective-permute-start.9 = (bf16[176,198]{1,0:T(8,128)(2,1)S(1)}, bf16[176,198]{1,0:T(8,128)(2,1)S(1)}, u32[]{:S(2)}, u32[]{:S(2)}) collective-permute-start(bf16[176,198]{1,0:T(8,128)(2,1)S(1)} %bitcast.108), channel_id=1, source_target_pairs={{0,16},{8,24},{16,32},{24,40},{32,48},{40,56},{48,0},{56,8},{64,80... | collective-permute-start | bytes 209096 | tf_op jit(solution)/shard_map/ppermute | solution.py:20
  62.5 1.5 %collective-permute-start.8 = (bf16[176,198]{1,0:T(8,128)(2,1)S(1)}, bf16[176,198]{1,0:T(8,128)(2,1)S(1)}, u32[]{:S(2)}, u32[]{:S(2)}) collective-permute-start(bf16[176,198]{1,0:T(8,128)(2,1)S(1)} %bitcast.107), channel_id=1, source_target_pairs={{0,48},{8,56},{16,0},{24,8},{32,16},{40,24},{48,32},{56,40},{64,11... | collective-permute-start | bytes 209096 | tf_op jit(solution)/shard_map/ppermute | solution.py:20
  64.1 2.3 %collective-permute-start.7 = (bf16[176,198]{1,0:T(8,128)(2,1)S(1)}, bf16[176,198]{1,0:T(8,128)(2,1)S(1)}, u32[]{:S(2)}, u32[]{:S(2)}) collective-permute-start(bf16[176,198]{1,0:T(8,128)(2,1)S(1)} %bitcast.110), channel_id=1, source_target_pairs={{0,32},{8,40},{16,48},{24,56},{32,0},{40,8},{48,16},{56,24},{64,96... | collective-permute-start | bytes 209096 | tf_op jit(solution)/shard_map/ppermute | solution.py:20
  66.4 2.1 %collective-permute-done.9 = bf16[176,198]{1,0:T(8,128)(2,1)S(1)} collective-permute-done((bf16[176,198]{1,0:T(8,128)(2,1)S(1)}, bf16[176,198]{1,0:T(8,128)(2,1)S(1)}, u32[]{:S(2)}, u32[]{:S(2)}) %collective-permute-start.9) | collective-permute-done | bytes 69728 | tf_op jit(solution)/shard_map/ppermute | solution.py:20
  68.7 1.5 %collective-permute-done.8 = bf16[176,198]{1,0:T(8,128)(2,1)S(1)} collective-permute-done((bf16[176,198]{1,0:T(8,128)(2,1)S(1)}, bf16[176,198]{1,0:T(8,128)(2,1)S(1)}, u32[]{:S(2)}, u32[]{:S(2)}) %collective-permute-start.8) | collective-permute-done | bytes 69728 | tf_op jit(solution)/shard_map/ppermute | solution.py:20
  70.4 3.4 %collective-permute-done.7 = bf16[176,198]{1,0:T(8,128)(2,1)S(1)} collective-permute-done((bf16[176,198]{1,0:T(8,128)(2,1)S(1)}, bf16[176,198]{1,0:T(8,128)(2,1)S(1)}, u32[]{:S(2)}, u32[]{:S(2)}) %collective-permute-start.7) | collective-permute-done | bytes 69728 | tf_op jit(solution)/shard_map/ppermute | solution.py:20
  73.9 1.1 pad_maximum_fusion.2
  75.1 0.6 fusion.22
  76.2 15.3 %all_to_all.20 = bf16[8,22,1536]{2,1,0:T(8,128)(2,1)S(1)} all-to-all(bf16[8,22,1536]{2,1,0:T(8,128)(2,1)S(1)} %reshape.177), channel_id=1, replica_groups=mesh['seq'=32,'mp'=8] {'mp'}, dimensions={0} | all-to-all | bytes 1081344 | tf_op jit(solution)/shard_map/all_to_all | solution.py:62
  92.0 0.9 broadcast_in_dim.5
  92.9 3.7 %all-to-all-start.2 = ((bf16[8,22,1536]{2,1,0:T(8,128)(2,1)}), bf16[8,22,1536]{2,1,0:T(8,128)(2,1)S(1)}, u32[]{:S(2)}, u32[]{:S(2)}) async-start(bf16[8,22,1536]{2,1,0:T(8,128)(2,1)} %broadcast_in_dim.5), calls=%async_computation.2 | async-start | bytes 1179648 | tf_op jit(solution)/shard_map/all_to_all | solution.py:57
  96.6 8.6 %all-to-all-done.2 = bf16[8,22,1536]{2,1,0:T(8,128)(2,1)S(1)} async-done(((bf16[8,22,1536]{2,1,0:T(8,128)(2,1)}), bf16[8,22,1536]{2,1,0:T(8,128)(2,1)S(1)}, u32[]{:S(2)}, u32[]{:S(2)}) %all-to-all-start.2) | async-done | bytes 540704 | tf_op jit(solution)/shard_map/all_to_all | solution.py:57
  106.1 1.9 %collective-permute-start.10 = (bf16[15,192]{1,0:T(8,128)(2,1)S(1)}, bf16[15,192]{1,0:T(8,128)(2,1)S(1)}, u32[]{:S(2)}, u32[]{:S(2)}) collective-permute-start(bf16[15,192]{1,0:T(8,128)(2,1)S(1)} %get-tuple-element.22), channel_id=1, source_target_pairs={{0,8},{8,16},{16,24},{24,32},{32,40},{40,48},{48,56},{56,64},{64,7... | collective-permute-start | bytes 17288 | tf_op jit(solution)/shard_map/ppermute | solution.py:140
  108.0 6.7 %collective-permute-start.11 = (bf16[15,192]{1,0:T(8,128)(2,1)S(1)}, bf16[15,192]{1,0:T(8,128)(2,1)S(1)}, u32[]{:S(2)}, u32[]{:S(2)}) collective-permute-start(bf16[15,192]{1,0:T(8,128)(2,1)S(1)} %get-tuple-element.23), channel_id=1, source_target_pairs={{8,0},{16,8},{24,16},{32,24},{40,32},{48,40},{56,48},{64,56},{72,6... | collective-permute-start | bytes 17288 | tf_op jit(solution)/shard_map/ppermute | solution.py:141
  114.7 1.3 %collective-permute-done.11 = bf16[15,192]{1,0:T(8,128)(2,1)S(1)} collective-permute-done((bf16[15,192]{1,0:T(8,128)(2,1)S(1)}, bf16[15,192]{1,0:T(8,128)(2,1)S(1)}, u32[]{:S(2)}, u32[]{:S(2)}) %collective-permute-start.11) | collective-permute-done | bytes 5792 | tf_op jit(solution)/shard_map/ppermute | solution.py:141
  116.0 1.0 convolution_convert_fusion
  117.2 12.2 %all_to_all.21 = bf16[8,22,1536]{2,1,0:T(8,128)(2,1)S(1)} all-to-all(bf16[8,22,1536]{2,1,0:T(8,128)(2,1)S(1)} %reshape.179), channel_id=1, replica_groups=mesh['seq'=32,'mp'=8] {'mp'}, dimensions={0} | all-to-all | bytes 1081344 | tf_op jit(solution)/shard_map/all_to_all | solution.py:62
  129.5 0.7 fusion.44
  (95 shorter events, 6.3 us)
Async XLA Ops:
  0.0 75.6 %copy-start = (bf16[192,1536]{1,0:T(8,128)(2,1)S(1)}, bf16[192,1536]{1,0:T(8,128)(2,1)}, u32[]{:S(2)}) copy-start(bf16[192,1536]{1,0:T(8,128)(2,1)} %param.16) | copy-start | bytes 1769476
  4.0 15.7 %all-to-all-start = ((bf16[8,22,1536]{2,1,0:T(8,128)(2,1)}), bf16[8,22,1536]{2,1,0:T(8,128)(2,1)S(1)}, u32[]{:S(2)}, u32[]{:S(2)}) async-start(bf16[8,22,1536]{2,1,0:T(8,128)(2,1)} %broadcast_in_dim.4), calls=%async_computation | async-start | bytes 1179648 | tf_op jit(solution)/shard_map/all_to_all | solution.py:57
  19.9 0.9 copy-start.4
  19.9 0.9 copy-start.5
  21.5 14.5 %collective-permute-start.2 = (bf16[88,384]{1,0:T(8,128)(2,1)S(1)}, bf16[88,384]{1,0:T(8,128)(2,1)S(1)}, u32[]{:S(2)}, u32[]{:S(2)}) collective-permute-start(bf16[88,384]{1,0:T(8,128)(2,1)S(1)} %pad_maximum_fusion.8), channel_id=1, source_target_pairs={{0,48},{8,56},{16,0},{24,8},{32,16},{40,24},{48,32},{56,40},{64,11... | collective-permute-start | bytes 202760 | tf_op jit(solution)/shard_map/ppermute | solution.py:20
  27.0 8.7 %collective-permute-start.1 = (bf16[88,384]{1,0:T(8,128)(2,1)S(1)}, bf16[88,384]{1,0:T(8,128)(2,1)S(1)}, u32[]{:S(2)}, u32[]{:S(2)}) collective-permute-start(bf16[88,384]{1,0:T(8,128)(2,1)S(1)} %pad_maximum_fusion.8), channel_id=1, source_target_pairs={{0,16},{8,24},{16,32},{24,40},{32,48},{40,56},{48,0},{56,8},{64,80... | collective-permute-start | bytes 202760 | tf_op jit(solution)/shard_map/ppermute | solution.py:20
  27.0 8.9 %collective-permute-start = (bf16[88,384]{1,0:T(8,128)(2,1)S(1)}, bf16[88,384]{1,0:T(8,128)(2,1)S(1)}, u32[]{:S(2)}, u32[]{:S(2)}) collective-permute-start(bf16[88,384]{1,0:T(8,128)(2,1)S(1)} %pad_maximum_fusion.8), channel_id=1, source_target_pairs={{0,32},{8,40},{16,48},{24,56},{32,0},{40,8},{48,16},{56,24},{64,96... | collective-permute-start | bytes 202760 | tf_op jit(solution)/shard_map/ppermute | solution.py:20
  32.3 7.4 %collective-permute-start.5 = (bf16[176,384]{1,0:T(8,128)(2,1)S(1)}, bf16[176,384]{1,0:T(8,128)(2,1)S(1)}, u32[]{:S(2)}, u32[]{:S(2)}) collective-permute-start(bf16[176,384]{1,0:T(8,128)(2,1)S(1)} %get-tuple-element.8), channel_id=1, source_target_pairs={{0,192},{8,200},{16,208},{24,216},{32,224},{40,232},{48,240},{56,2... | collective-permute-start | bytes 405512 | tf_op jit(solution)/shard_map/ppermute | solution.py:20
  33.1 6.5 %collective-permute-start.4 = (bf16[176,384]{1,0:T(8,128)(2,1)S(1)}, bf16[176,384]{1,0:T(8,128)(2,1)S(1)}, u32[]{:S(2)}, u32[]{:S(2)}) collective-permute-start(bf16[176,384]{1,0:T(8,128)(2,1)S(1)} %get-tuple-element.8), channel_id=1, source_target_pairs={{0,64},{8,72},{16,80},{24,88},{32,96},{40,104},{48,112},{56,120},{... | collective-permute-start | bytes 405512 | tf_op jit(solution)/shard_map/ppermute | solution.py:20
  35.7 6.6 %collective-permute-start.3 = (bf16[176,384]{1,0:T(8,128)(2,1)S(1)}, bf16[176,384]{1,0:T(8,128)(2,1)S(1)}, u32[]{:S(2)}, u32[]{:S(2)}) collective-permute-start(bf16[176,384]{1,0:T(8,128)(2,1)S(1)} %get-tuple-element.8), channel_id=1, source_target_pairs={{0,128},{8,136},{16,144},{24,152},{32,160},{40,168},{48,176},{56,1... | collective-permute-start | bytes 405512 | tf_op jit(solution)/shard_map/ppermute | solution.py:20
  42.4 2.2 %collective-permute-start.6 = (bf16[4,176,384]{2,1,0:T(8,128)(2,1)S(1)}, bf16[4,176,384]{2,1,0:T(8,128)(2,1)S(1)}, u32[]{:S(2)}, u32[]{:S(2)}) collective-permute-start(bf16[4,176,384]{2,1,0:T(8,128)(2,1)S(1)} %pad_maximum_fusion), channel_id=1, source_target_pairs={{0,8},{8,0},{16,24},{24,16},{32,40},{40,32},{48,56},{56,48},{64,72... | collective-permute-start | bytes 1622024 | tf_op jit(solution)/shard_map/ppermute | solution.py:20
  46.9 2.1 %copy-start.2 = (bf16[704,2,96]{2,1,0:T(2,128)(2,1)S(1)}, bf16[704,2,96]{2,1,0:T(2,128)(2,1)}, u32[]{:S(2)}) copy-start(bf16[704,2,96]{2,1,0:T(2,128)(2,1)} %reshape.184) | copy-start | bytes 811012
  50.2 3.1 %copy-start.1 = (f32[2,704,1408]{2,1,0:T(8,128)}, f32[2,704,1408]{2,1,0:T(8,128)S(1)}, u32[]{:S(2)}) copy-start(f32[2,704,1408]{2,1,0:T(8,128)S(1)} %get-tuple-element.69) | copy-start | bytes 23789572
  59.8 8.8 %collective-permute-start.9 = (bf16[176,198]{1,0:T(8,128)(2,1)S(1)}, bf16[176,198]{1,0:T(8,128)(2,1)S(1)}, u32[]{:S(2)}, u32[]{:S(2)}) collective-permute-start(bf16[176,198]{1,0:T(8,128)(2,1)S(1)} %bitcast.108), channel_id=1, source_target_pairs={{0,16},{8,24},{16,32},{24,40},{32,48},{40,56},{48,0},{56,8},{64,80... | collective-permute-start | bytes 209096 | tf_op jit(solution)/shard_map/ppermute | solution.py:20
  62.5 7.6 %collective-permute-start.8 = (bf16[176,198]{1,0:T(8,128)(2,1)S(1)}, bf16[176,198]{1,0:T(8,128)(2,1)S(1)}, u32[]{:S(2)}, u32[]{:S(2)}) collective-permute-start(bf16[176,198]{1,0:T(8,128)(2,1)S(1)} %bitcast.107), channel_id=1, source_target_pairs={{0,48},{8,56},{16,0},{24,8},{32,16},{40,24},{48,32},{56,40},{64,11... | collective-permute-start | bytes 209096 | tf_op jit(solution)/shard_map/ppermute | solution.py:20
  64.1 9.6 %collective-permute-start.7 = (bf16[176,198]{1,0:T(8,128)(2,1)S(1)}, bf16[176,198]{1,0:T(8,128)(2,1)S(1)}, u32[]{:S(2)}, u32[]{:S(2)}) collective-permute-start(bf16[176,198]{1,0:T(8,128)(2,1)S(1)} %bitcast.110), channel_id=1, source_target_pairs={{0,32},{8,40},{16,48},{24,56},{32,0},{40,8},{48,16},{56,24},{64,96... | collective-permute-start | bytes 209096 | tf_op jit(solution)/shard_map/ppermute | solution.py:20
  76.1 15.4 %copy-start.3 = (bf16[22,1536]{1,0:T(8,128)(2,1)S(1)}, bf16[22,1536]{1,0:T(8,128)(2,1)}, u32[]{:S(2)}) copy-start(bf16[22,1536]{1,0:T(8,128)(2,1)} %param.12) | copy-start | bytes 202756
  76.1 15.8 %copy-start.7 = (f32[1536]{0:T(1024)S(1)}, f32[1536]{0:T(1024)}, u32[]{:S(2)}) copy-start(f32[1536]{0:T(1024)} %param.18) | copy-start | bytes 18436
  76.1 15.8 %copy-start.8 = (f32[1536]{0:T(1024)S(1)}, f32[1536]{0:T(1024)}, u32[]{:S(2)}) copy-start(f32[1536]{0:T(1024)} %param.17) | copy-start | bytes 18436
  91.5 5.0 %copy-start.6 = (f32[31,192]{1,0:T(8,128)S(1)}, f32[31,192]{1,0:T(8,128)}, u32[]{:S(2)}) copy-start(f32[31,192]{1,0:T(8,128)} %param.20) | copy-start | bytes 71428
  92.9 12.5 %copy-start.9 = (bf16[2,192,1536]{2,1,0:T(8,128)(2,1)S(1)}, bf16[2,192,1536]{2,1,0:T(8,128)(2,1)}, u32[]{:S(2)}) copy-start(bf16[2,192,1536]{2,1,0:T(8,128)(2,1)} %param.19) | copy-start | bytes 3538948
  92.9 12.3 %all-to-all-start.2 = ((bf16[8,22,1536]{2,1,0:T(8,128)(2,1)}), bf16[8,22,1536]{2,1,0:T(8,128)(2,1)S(1)}, u32[]{:S(2)}, u32[]{:S(2)}) async-start(bf16[8,22,1536]{2,1,0:T(8,128)(2,1)} %broadcast_in_dim.5), calls=%async_computation.2 | async-start | bytes 1179648 | tf_op jit(solution)/shard_map/all_to_all | solution.py:57
  105.7 10.3 %copy-start.10 = (bf16[192,1536]{1,0:T(8,128)(2,1)S(1)}, bf16[192,1536]{1,0:T(8,128)(2,1)}, u32[]{:S(2)}) copy-start(bf16[192,1536]{1,0:T(8,128)(2,1)} %param.23) | copy-start | bytes 1769476
  105.7 10.3 %copy-start.11 = (f32[192]{0:T(256)S(1)}, f32[192]{0:T(256)}, u32[]{:S(2)}) copy-start(f32[192]{0:T(256)} %param.22) | copy-start | bytes 2308
  105.7 10.3 %copy-start.12 = (f32[192]{0:T(256)S(1)}, f32[192]{0:T(256)}, u32[]{:S(2)}) copy-start(f32[192]{0:T(256)} %param.21) | copy-start | bytes 2308
  106.1 8.6 %collective-permute-start.10 = (bf16[15,192]{1,0:T(8,128)(2,1)S(1)}, bf16[15,192]{1,0:T(8,128)(2,1)S(1)}, u32[]{:S(2)}, u32[]{:S(2)}) collective-permute-start(bf16[15,192]{1,0:T(8,128)(2,1)S(1)} %get-tuple-element.22), channel_id=1, source_target_pairs={{0,8},{8,16},{16,24},{24,32},{32,40},{40,48},{48,56},{56,64},{64,7... | collective-permute-start | bytes 17288 | tf_op jit(solution)/shard_map/ppermute | solution.py:140
  108.0 8.0 %collective-permute-start.11 = (bf16[15,192]{1,0:T(8,128)(2,1)S(1)}, bf16[15,192]{1,0:T(8,128)(2,1)S(1)}, u32[]{:S(2)}, u32[]{:S(2)}) collective-permute-start(bf16[15,192]{1,0:T(8,128)(2,1)S(1)} %get-tuple-element.23), channel_id=1, source_target_pairs={{8,0},{16,8},{24,16},{32,24},{40,32},{48,40},{56,48},{64,56},{72,6... | collective-permute-start | bytes 17288 | tf_op jit(solution)/shard_map/ppermute | solution.py:141

commit v2 on v1

v2 whole, which is shorter than its diff:
```python
import functools

import jax
import jax.numpy as jnp
from jax import lax
from jax.experimental import pallas as pl
from jax.experimental.pallas import tpu as pltpu
from jax.sharding import PartitionSpec as P

D = 1536
HEADS = 16
HEAD = D // HEADS
HALF = HEAD // 2
WIDTH = 192
ROWS = 22
SLOT = 24
PEERS = 8
BLOCK = ROWS * PEERS
TAPS = 31
REACH = TAPS // 2
LOG2E = 1.4426950408889634
F32 = jnp.float32
BF16 = jnp.bfloat16
VMEM = pl.BlockSpec(memory_space=pltpu.VMEM)


def hop(array, place):
    count = lax.axis_size("seq")
    return lax.ppermute(array, "seq", [(i, place(i)) for i in range(count)])


def along_y(step):
    return lambda i: (i + 8 * step) % 32


def along_z(step):
    return lambda i: (i // 8) * 8 + (i % 8 + 2 * step) % 8


def other_core(i):
    return i ^ 1


def call(body, outs, scratch=(), flops=1_000_000, size=1_000_000):
    single = isinstance(outs, jax.ShapeDtypeStruct)
    return lambda *args: pl.pallas_call(
        body,
        out_shape=outs,
        in_specs=[VMEM] * len(args),
        out_specs=VMEM if single else tuple(VMEM for _ in outs),
        scratch_shapes=list(scratch),
        cost_estimate=pl.CostEstimate(flops=flops, bytes_accessed=size, transcendentals=0),
        compiler_params=pltpu.CompilerParams(vmem_limit_bytes=48 * 2**20),
    )(*args)


def dot_t(a, b):
    return lax.dot_general(a, b, (((1,), (1,)), ((), ())), preferred_element_type=F32)


def dot(a, b):
    return jnp.dot(a, b, preferred_element_type=F32)


def norm_rows(vf, gain, shift):
    center = vf - jnp.mean(vf, axis=-1, keepdims=True)
    spread = jnp.mean(center * center, axis=-1, keepdims=True)
    return (center * lax.rsqrt(spread + 1e-05) * gain + shift).astype(BF16)


def norm_body(x_ref, gain_ref, shift_ref, out_ref):
    normed = norm_rows(x_ref[...].astype(F32), gain_ref[...], shift_ref[...])
    for peer in range(PEERS):
        out_ref[peer, 0:ROWS, :] = normed


def pack_rows(out, tight):
    for peer in range(PEERS):
        tight[peer * ROWS : peer * ROWS + ROWS, :] = out[peer * SLOT : peer * SLOT + ROWS]


def swapped(w):
    parts = [
        w[head * HEAD + part * HALF : head * HEAD + part * HALF + HALF]
        for head in range(2)
        for part in (1, 0)
    ]
    return jnp.concatenate(parts, axis=0)


def query_body(x_ref, w_ref, cos_ref, sin_ref, out_ref, tight):
    x = x_ref[...].reshape(PEERS * SLOT, D)
    w = w_ref[0]
    zero = jnp.zeros((64, D), BF16)
    plain = dot_t(x, jnp.concatenate([w, zero], axis=0))
    cross = dot_t(x, jnp.concatenate([swapped(w), zero], axis=0))
    pack_rows(plain * cos_ref[:, 0:256] + cross * sin_ref[...], tight)
    first = tight[0:96, :]
    second = pltpu.roll(tight[80:176, :], 64, 1)
    lane = lax.broadcasted_iota(jnp.int32, (96, 128), 1)
    middle = jnp.where(lane < 64, first[:, 128:256], second[:, 0:128])
    out_ref[:, 0:128] = first[:, 0:128].astype(BF16)
    out_ref[:, 128:256] = middle.astype(BF16)
    out_ref[:, 256:384] = second[:, 128:256].astype(BF16)


def pair_body(x_ref, w_ref, cos_ref, sin_ref, out_ref, tight):
    x = x_ref[...].reshape(PEERS * SLOT, D)
    wk, wv = w_ref[1], w_ref[2]
    plain = dot_t(x, jnp.concatenate([wk, wv], axis=0))
    cross = dot_t(x, jnp.concatenate([swapped(wk), wv[0:64]], axis=0))
    left = plain[:, 0:256] * cos_ref[:, 0:256] + cross * sin_ref[...]
    pack_rows(jnp.concatenate([left, plain[:, 256:384]], axis=1), tight)
    out_ref[...] = tight[...].astype(BF16)


def attend_body(*refs):
    q_refs, kv_refs = refs[0:4], refs[4:12]
    out_refs = refs[12:16]
    q_all, kv_all, o_all = refs[16:19]
    for n, ref in enumerate(q_refs):
        q_all[n * BLOCK : n * BLOCK + 96, :] = ref[:, 0:256]
        second = pltpu.roll(ref[:, 128:384].astype(F32), 192, 1).astype(BF16)
        q_all[n * BLOCK + 80 : n * BLOCK + 176, :] = second
    for n, ref in enumerate(kv_refs):
        kv_all[n * BLOCK : n * BLOCK + BLOCK, :] = ref[...]
    factor = LOG2E / HEAD**0.5
    lane = lax.broadcasted_iota(jnp.int32, (BLOCK, 256), 1)

    def step(n, unused):
        q = q_all[pl.ds(pl.multiple_of(n * BLOCK, 16), BLOCK), :].astype(F32)
        result, stats = None, jnp.zeros((BLOCK, 256), F32)
        for head in range(2):
            own = (lane >= head * HEAD) & (lane < head * HEAD + HEAD)
            scores = dot_t(jnp.where(own, q, 0.0).astype(BF16), kv_all[:, 0:256])
            top = jnp.max(scores, axis=1, keepdims=True)
            weights = jnp.exp2((scores - top) * factor)
            total = jnp.sum(weights, axis=1, keepdims=True)
            mixed = dot(weights.astype(BF16), kv_all[:, 128:384]) * (1.0 / total)
            level = top * factor + jnp.log2(total)
            high = level.astype(BF16).astype(F32)
            middle = (level - high).astype(BF16).astype(F32)
            low = level - high - middle
            for place, piece in enumerate((high, middle, low)):
                stats = jnp.where(lane == head * 3 + place, piece, stats)
            result = mixed if head == 0 else jnp.where(lane < 160, result, mixed)
        o_all[pl.ds(pl.multiple_of(n * BLOCK, 16), BLOCK), :] = jnp.where(
            lane < 64, stats, result
        ).astype(BF16)
        return unused

    lax.fori_loop(0, 4, step, 0)
    for n, ref in enumerate(out_refs):
        ref[...] = o_all[n * BLOCK : n * BLOCK + BLOCK, :]


def merge_body(a_ref, b_ref, c_ref, d_ref, w_ref, out_ref, spread):
    parts = [ref[...].astype(F32) for ref in (a_ref, b_ref, c_ref, d_ref)]
    lane = lax.broadcasted_iota(jnp.int32, (BLOCK, 256), 1)
    context = jnp.zeros((BLOCK, 256), F32)
    shares = []
    for head in range(2):
        levels = [
            part[:, 3 * head : 3 * head + 1]
            + part[:, 3 * head + 1 : 3 * head + 2]
            + part[:, 3 * head + 2 : 3 * head + 3]
            for part in parts
        ]
        top = functools.reduce(jnp.maximum, levels)
        scaled = [jnp.exp2(level - top) for level in levels]
        total = functools.reduce(jnp.add, scaled)
        shares.append([value / total for value in scaled])
    for part, first, second in zip(parts, *shares):
        context += part * jnp.where(lane < 160, first, second)
    context = jnp.where(lane < 64, 0.0, context)
    spread[...] = jnp.zeros_like(spread)
    for peer in range(PEERS):
        spread[peer * SLOT : peer * SLOT + ROWS, :] = context[peer * ROWS : peer * ROWS + ROWS]
    w = jnp.concatenate([jnp.zeros((64, D), BF16), w_ref[...]], axis=0)
    out_ref[...] = dot(spread[...].astype(BF16), w).astype(BF16).reshape(PEERS, SLOT, D)


def middle_body(got_ref, x_ref, gain_ref, shift_ref, mid_ref, out_ref):
    total = jnp.sum(got_ref[...].astype(F32), axis=0)[0:ROWS]
    mid = (x_ref[...].astype(F32) + total).astype(BF16)
    mid_ref[...] = mid
    normed = norm_rows(mid.astype(F32), gain_ref[...], shift_ref[...])
    for peer in range(PEERS):
        out_ref[peer, 0:ROWS, :] = normed


def exchange(array):
    return lax.all_to_all(array, "mp", 0, 0, tiled=False)


def shape(dims, dtype=BF16):
    return jax.ShapeDtypeStruct(dims, dtype)


def tables():
    slot = jnp.arange(PEERS * SLOT)
    place = lax.axis_index("seq") * BLOCK + slot // SLOT * ROWS + slot % SLOT
    freq = 10000.0 ** (-jnp.arange(HALF).astype(F32) / HALF)
    angle = place.astype(F32)[:, None] * freq[None, :]
    cosine, sine = jnp.cos(angle), jnp.sin(angle)
    rest = (PEERS * SLOT, 64)
    wide_cos = jnp.concatenate([cosine] * 4 + [jnp.ones(rest, F32)], axis=1)
    wide_sin = jnp.concatenate([-sine, sine] * 2 + [jnp.zeros(rest, F32)], axis=1)
    return wide_cos, wide_sin


def local(
    frames_in,
    attn_gain,
    attn_shift,
    w_qkv,
    w_attn_out,
    conv_gain,
    conv_shift,
    w_pointwise_in,
    depth_kernel,
    norm_scale,
    norm_offset,
    w_pointwise_out,
):
    slots = shape((PEERS, SLOT, D))
    attn_in = exchange(
        call(norm_body, slots)(frames_in, attn_gain.reshape(1, D), attn_shift.reshape(1, D))
    )
    cosine, sine = tables()
    scratch = [pltpu.VMEM((BLOCK, 256), F32)]
    queries = call(query_body, shape((96, 384)), scratch)(attn_in, w_qkv, cosine, sine)
    scratch = [pltpu.VMEM((BLOCK, 384), F32)]
    pair = call(pair_body, shape((BLOCK, 384)), scratch)(attn_in, w_qkv, cosine, sine)

    steps = (2, 1, -1)
    q_got = [queries] + [hop(queries, along_z(step)) for step in steps]
    kv_got = [pair] + [hop(pair, along_y(step)) for step in steps]
    kv_got += [hop(kv, other_core) for kv in kv_got]
    scratch = [
        pltpu.VMEM((4 * BLOCK, 256), BF16),
        pltpu.VMEM((8 * BLOCK, 384), BF16),
        pltpu.VMEM((4 * BLOCK, 256), BF16),
    ]
    parts = call(attend_body, (shape((BLOCK, 256)),) * 4, scratch)(*q_got, *kv_got)
    back = [parts[0]] + [hop(parts[n + 1], along_z(-step)) for n, step in enumerate(steps)]
    scratch = [pltpu.VMEM((PEERS * SLOT, 256), F32)]
    sums = exchange(call(merge_body, slots, scratch)(*back, w_attn_out))
    mid, conv_in = call(middle_body, (shape((ROWS, D)), slots))(
        sums, frames_in, conv_gain.reshape(1, D), conv_shift.reshape(1, D)
    )
    conv_in = exchange(conv_in)[:, :ROWS].reshape(BLOCK, D)
    value_half = dot_t(conv_in, w_pointwise_in[0])
    gate_half = dot_t(conv_in, w_pointwise_in[1])
    glu = (value_half * jax.nn.sigmoid(gate_half)).astype(BF16)
    count = lax.axis_size("seq")
    ahead = lax.ppermute(glu[-REACH:], "seq", [(i, i + 1) for i in range(count - 1)])
    behind = lax.ppermute(glu[:REACH], "seq", [(i + 1, i) for i in range(count - 1)])
    padded = jnp.concatenate([ahead, glu, behind], axis=0)
    depth = jnp.zeros((BLOCK, WIDTH), F32)
    for tap in range(TAPS):
        depth = depth + padded[tap : tap + BLOCK].astype(F32) * depth_kernel[tap]
    normed = depth * norm_scale + norm_offset
    swish = (normed * jax.nn.sigmoid(normed)).astype(BF16)
    partial = dot(swish, w_pointwise_out).astype(BF16).reshape(PEERS, ROWS, D)
    conv = jnp.sum(exchange(partial).astype(F32), axis=0)
    return (mid.astype(F32) + conv).astype(BF16)


def solution(mesh):
    placed = (
        P(("seq", "mp"), None),
        P(),
        P(),
        P(None, "mp", None),
        P("mp", None),
        P(),
        P(),
        P(None, "mp", None),
        P(None, "mp"),
        P("mp"),
        P("mp"),
        P("mp", None),
    )
    return jax.shard_map(
        local, mesh=mesh, in_specs=placed, out_specs=P(("seq", "mp"), None), check_vma=False
    )
```

time: 131 us -> 123 us (0.939)
  waiting for transfers between devices: 31.2 us -> 46.5 us
  blocking collectives: 27.4 us -> 14.4 us
  Pallas kernels: 0 us -> 11.6 us
  local copies, waits for them, and re-layouts: 14.2 us -> 4.7 us
  other arithmetic: 10.1 us -> 1.2 us
  matrix products: 9.25 us -> 1.75 us
  starting transfers between devices: 37.4 us -> 41.7 us
    all_to_all x2 -> x1, blocking collectives: 27.4 us -> 14.4 us  [exchange(): return lax.all_to_all(array, 'mp', 0, 0, tiled=False)]
    pallas_call x0 -> x6, Pallas kernels: none -> 11.6 us  [call(): pl.pallas_call(body, out_shape=outs, in_specs=[VMEM] * len(args), out_spe...]
    all_to_all x2 -> x3, waiting for transfers between devices: 16 us -> 27.1 us  [exchange(): return lax.all_to_all(array, 'mp', 0, 0, tiled=False)]
    dot_general x9 -> x3, matrix products: 9.25 us -> 1.75 us  [the longest x1 1.06 us: dot(): return jnp.dot(a, b, preferred_element_type=F32)]
    ppermute x1, waiting for transfers between devices: 0.01 us -> 6.02 us  [local(): lax.ppermute(glu[-REACH:], 'seq', [(i, i + 1) for i in range(count - 1)])]
    reduce_sum x9 -> x1, other arithmetic: 4.85 us -> 0.1 us  [local(): conv = jnp.sum(exchange(partial).astype(F32), axis=0)]
    ppermute x10 -> x13, starting transfers between devices: 19.5 us -> 23.7 us  [hop(): return lax.ppermute(array, 'seq', [(i, place(i)) for i in range(count)])]
    slice x14 -> x0, local copies, waits for them, and re-layouts: 4.09 us -> none  [the longest x1 1.53 us: local(): w_qkv[slot]]
  transfers between devices with their start and end apart: 14 -> 18, of which waited for: 9 -> 10; matrix products, arithmetic and copies ran while one was open for 5% -> 2% of each run, Pallas kernels for 0% -> 0%
where the time goes in v2:
time: 123 us; the launch traced here: 122 us
  waiting for transfers between devices  46.5 us (38%)
  starting transfers between devices  41.7 us (34%)
  blocking collectives  14.4 us (12%)
  Pallas kernels  11.6 us (9%)
  local copies, waits for them, and re-layouts  4.7 us (4%)
  matrix products  1.75 us (1%)
    all_to_all x3, waiting for transfers between devices, exchange(): return lax.all_to_all(array, 'mp', 0, 0, tiled=False)  27.1 us
    ppermute x13, starting transfers between devices, hop(): return lax.ppermute(array, 'seq', [(i, place(i)) for i in range(count)])  23.7 us
    all_to_all x1, blocking collectives, exchange(): return lax.all_to_all(array, 'mp', 0, 0, tiled=False)  14.4 us
    ppermute x13, waiting for transfers between devices, hop(): return lax.ppermute(array, 'seq', [(i, place(i)) for i in range(count)])  13.3 us
    all_to_all x3, starting transfers between devices, exchange(): return lax.all_to_all(array, 'mp', 0, 0, tiled=False)  13.1 us
    pallas_call x6, Pallas kernels, call(): pl.pallas_call(body, out_shape=outs, in_specs=[VMEM] * len(args), out_spe...  11.6 us
    ppermute x1, waiting for transfers between devices, local(): lax.ppermute(glu[-REACH:], 'seq', [(i, i + 1) for i in range(count - 1)])  6.02 us
    ppermute x1, starting transfers between devices, local(): lax.ppermute(glu[:REACH], 'seq', [(i + 1, i) for i in range(count - 1)])  2.97 us
  transfers between devices with their start and end apart: 18, of which 10 were waited for; matrix products, arithmetic and copies ran while one was open for 2% of the time, Pallas kernels for 0%

profile of v2, /device:TPU:24, one launch (start us, length us, event | category | flops | bytes accessed | tf_op | source)
XLA Modules:
  0.0 122.1 jit_solution(10059329195082237977)
XLA Ops:
  0.0 0.8 reshape.48.gain_ref
  0.8 0.7 reshape.49.shift_ref
  1.5 0.9 copy-done.3
  2.4 1.0 shard_map.118
  3.4 5.7 %all-to-all-start = ((bf16[8,24,1536]{2,1,0:T(8,128)(2,1)}), bf16[8,24,1536]{2,1,0:T(8,128)(2,1)S(1)}, u32[]{:S(2)}, u32[]{:S(2)}) async-start(bf16[8,24,1536]{2,1,0:T(8,128)(2,1)} %shard_map.118), calls=%async_computation | async-start | bytes 1179648 | tf_op jit(solution)/shard_map/all_to_all | solution.py:193
  9.1 0.4 multiply_sine_fusion
  9.5 0.2 concatenate.41.cos_ref
  9.7 0.6 broadcast_in_dim.5
  10.4 1.1 concatenate.42.sin_ref
  11.5 7.6 %all-to-all-done.x_ref = bf16[8,24,1536]{2,1,0:T(8,128)(2,1)S(1)} async-done(((bf16[8,24,1536]{2,1,0:T(8,128)(2,1)}), bf16[8,24,1536]{2,1,0:T(8,128)(2,1)S(1)}, u32[]{:S(2)}, u32[]{:S(2)}) %all-to-all-start) | async-done | bytes 589856 | tf_op jit(solution)/shard_map/all_to_all | solution.py:193
  19.1 0.8 shard_map.120.refs_4_
  19.9 1.3 %collective-permute-start.3 = (bf16[176,384]{1,0:T(8,128)(2,1)S(1)}, bf16[176,384]{1,0:T(8,128)(2,1)S(1)}, u32[]{:S(2)}, u32[]{:S(2)}) collective-permute-start(bf16[176,384]{1,0:T(8,128)(2,1)S(1)} %shard_map.120.refs_4_), channel_id=1, source_target_pairs={{0,128},{8,136},{16,144},{24,152},{32,160},{40,168},{48,176},{56,1... | collective-permute-start | bytes 405512 | tf_op jit(solution)/shard_map/ppermute | solution.py:29
  21.2 2.2 %collective-permute-start.4 = (bf16[176,384]{1,0:T(8,128)(2,1)S(1)}, bf16[176,384]{1,0:T(8,128)(2,1)S(1)}, u32[]{:S(2)}, u32[]{:S(2)}) collective-permute-start(bf16[176,384]{1,0:T(8,128)(2,1)S(1)} %shard_map.120.refs_4_), channel_id=1, source_target_pairs={{0,64},{8,72},{16,80},{24,88},{32,96},{40,104},{48,112},{56,120},{... | collective-permute-start | bytes 405512 | tf_op jit(solution)/shard_map/ppermute | solution.py:29
  23.4 0.6 shard_map.119.refs_0_
  23.9 0.0 copy-start.2
  24.0 6.4 %collective-permute-start = (bf16[96,384]{1,0:T(8,128)(2,1)S(1)}, bf16[96,384]{1,0:T(8,128)(2,1)S(1)}, u32[]{:S(2)}, u32[]{:S(2)}) collective-permute-start(bf16[96,384]{1,0:T(8,128)(2,1)S(1)} %shard_map.119.refs_0_), channel_id=1, source_target_pairs={{0,32},{8,40},{16,48},{24,56},{32,0},{40,8},{48,16},{56,24},{64,96... | collective-permute-start | bytes 221192 | tf_op jit(solution)/shard_map/ppermute | solution.py:29
  30.3 1.5 %collective-permute-start.1 = (bf16[96,384]{1,0:T(8,128)(2,1)S(1)}, bf16[96,384]{1,0:T(8,128)(2,1)S(1)}, u32[]{:S(2)}, u32[]{:S(2)}) collective-permute-start(bf16[96,384]{1,0:T(8,128)(2,1)S(1)} %shard_map.119.refs_0_), channel_id=1, source_target_pairs={{0,16},{8,24},{16,32},{24,40},{32,48},{40,56},{48,0},{56,8},{64,80... | collective-permute-start | bytes 221192 | tf_op jit(solution)/shard_map/ppermute | solution.py:29
  31.8 0.9 collective-permute-done.refs_1_
  32.8 0.5 collective-permute-start.7
  33.3 0.1 collective-permute-start.8
  33.4 0.4 collective-permute-start.9
  33.8 3.0 %collective-permute-done.1.refs_2_ = bf16[96,384]{1,0:T(8,128)(2,1)S(1)} collective-permute-done((bf16[96,384]{1,0:T(8,128)(2,1)S(1)}, bf16[96,384]{1,0:T(8,128)(2,1)S(1)}, u32[]{:S(2)}, u32[]{:S(2)}) %collective-permute-start.1) | collective-permute-done | bytes 73760 | tf_op jit(solution)/shard_map/ppermute | solution.py:29
  36.8 4.3 %collective-permute-start.2 = (bf16[96,384]{1,0:T(8,128)(2,1)S(1)}, bf16[96,384]{1,0:T(8,128)(2,1)S(1)}, u32[]{:S(2)}, u32[]{:S(2)}) collective-permute-start(bf16[96,384]{1,0:T(8,128)(2,1)S(1)} %shard_map.119.refs_0_), channel_id=1, source_target_pairs={{0,48},{8,56},{16,0},{24,8},{32,16},{40,24},{48,32},{56,40},{64,11... | collective-permute-start | bytes 221192 | tf_op jit(solution)/shard_map/ppermute | solution.py:29
  41.1 2.8 %collective-permute-done.2.refs_3_ = bf16[96,384]{1,0:T(8,128)(2,1)S(1)} collective-permute-done((bf16[96,384]{1,0:T(8,128)(2,1)S(1)}, bf16[96,384]{1,0:T(8,128)(2,1)S(1)}, u32[]{:S(2)}, u32[]{:S(2)}) %collective-permute-start.2) | collective-permute-done | bytes 73760 | tf_op jit(solution)/shard_map/ppermute | solution.py:29
  43.9 6.5 %shard_map.121 = (bf16[176,256]{1,0:T(8,128)(2,1)S(1)}, bf16[176,256]{1,0:T(8,128)(2,1)S(1)}, bf16[176,256]{1,0:T(8,128)(2,1)S(1)}, bf16[176,256]{1,0:T(8,128)(2,1)S(1)}) custom-call(bf16[96,384]{1,0:T(8,128)(2,1)S(1)} %shard_map.119.refs_0_, bf16[96,384]{1,0:T(8,128)(2,1)S(1)} %collective-permute-done.refs_1_, ...), custom_call_target="tpu_custom_call" | custom-call | flops 1000000 | bytes 1000000 | tf_op jit(solution)/shard_map/pallas_call | solution.py:46
  50.4 3.6 %collective-permute-start.10 = (bf16[176,256]{1,0:T(8,128)(2,1)S(1)}, bf16[176,256]{1,0:T(8,128)(2,1)S(1)}, u32[]{:S(2)}, u32[]{:S(2)}) collective-permute-start(bf16[176,256]{1,0:T(8,128)(2,1)S(1)} %get-tuple-element.12), channel_id=1, source_target_pairs={{0,32},{8,40},{16,48},{24,56},{32,0},{40,8},{48,16},{56,24},{64,96... | collective-permute-start | bytes 270344 | tf_op jit(solution)/shard_map/ppermute | solution.py:29
  54.0 2.1 %collective-permute-start.11 = (bf16[176,256]{1,0:T(8,128)(2,1)S(1)}, bf16[176,256]{1,0:T(8,128)(2,1)S(1)}, u32[]{:S(2)}, u32[]{:S(2)}) collective-permute-start(bf16[176,256]{1,0:T(8,128)(2,1)S(1)} %get-tuple-element.13), channel_id=1, source_target_pairs={{0,48},{8,56},{16,0},{24,8},{32,16},{40,24},{48,32},{56,40},{64,11... | collective-permute-start | bytes 270344 | tf_op jit(solution)/shard_map/ppermute | solution.py:29
  56.1 1.3 %collective-permute-start.12 = (bf16[176,256]{1,0:T(8,128)(2,1)S(1)}, bf16[176,256]{1,0:T(8,128)(2,1)S(1)}, u32[]{:S(2)}, u32[]{:S(2)}) collective-permute-start(bf16[176,256]{1,0:T(8,128)(2,1)S(1)} %get-tuple-element.14), channel_id=1, source_target_pairs={{0,16},{8,24},{16,32},{24,40},{32,48},{40,56},{48,0},{56,8},{64,80... | collective-permute-start | bytes 270344 | tf_op jit(solution)/shard_map/ppermute | solution.py:29
  57.5 1.6 %collective-permute-done.10.b_ref = bf16[176,256]{1,0:T(8,128)(2,1)S(1)} collective-permute-done((bf16[176,256]{1,0:T(8,128)(2,1)S(1)}, bf16[176,256]{1,0:T(8,128)(2,1)S(1)}, u32[]{:S(2)}, u32[]{:S(2)}) %collective-permute-start.10) | collective-permute-done | bytes 90144 | tf_op jit(solution)/shard_map/ppermute | solution.py:29
  59.1 4.1 %collective-permute-done.11.c_ref = bf16[176,256]{1,0:T(8,128)(2,1)S(1)} collective-permute-done((bf16[176,256]{1,0:T(8,128)(2,1)S(1)}, bf16[176,256]{1,0:T(8,128)(2,1)S(1)}, u32[]{:S(2)}, u32[]{:S(2)}) %collective-permute-start.11) | collective-permute-done | bytes 90144 | tf_op jit(solution)/shard_map/ppermute | solution.py:29
  63.1 0.9 collective-permute-done.12.d_ref
  64.0 1.6 %shard_map.122 = bf16[8,24,1536]{2,1,0:T(8,128)(2,1)} custom-call(bf16[176,256]{1,0:T(8,128)(2,1)S(1)} %get-tuple-element.11.a_ref, bf16[176,256]{1,0:T(8,128)(2,1)S(1)} %collective-permute-done.10.b_ref, bf16[176,256]{1,0:T(8,128)(2,1)S(1)} %collective-permute-done.11.c_ref, bf16[176,256]{1,0:T(8,128)(2,1)S(1)} %collective-permute-done.12.d_ref, ...), custom_call_target="tpu_custom_call" | custom-call | flops 1000000 | bytes 1000000 | tf_op jit(solution)/shard_map/pallas_call | solution.py:46
  65.7 3.7 %all-to-all-start.1 = ((bf16[8,24,1536]{2,1,0:T(8,128)(2,1)}), bf16[8,24,1536]{2,1,0:T(8,128)(2,1)S(1)}, u32[]{:S(2)}, u32[]{:S(2)}) async-start(bf16[8,24,1536]{2,1,0:T(8,128)(2,1)} %shard_map.122), calls=%async_computation.1 | async-start | bytes 1179648 | tf_op jit(solution)/shard_map/all_to_all | solution.py:193
  69.5 9.7 %all-to-all-done.1.got_ref = bf16[8,24,1536]{2,1,0:T(8,128)(2,1)S(1)} async-done(((bf16[8,24,1536]{2,1,0:T(8,128)(2,1)}), bf16[8,24,1536]{2,1,0:T(8,128)(2,1)S(1)}, u32[]{:S(2)}, u32[]{:S(2)}) %all-to-all-start.1) | async-done | bytes 589856 | tf_op jit(solution)/shard_map/all_to_all | solution.py:193
  79.2 1.1 shard_map.123
  80.3 3.7 %all-to-all-start.2 = ((bf16[8,24,1536]{2,1,0:T(8,128)(2,1)}), bf16[8,24,1536]{2,1,0:T(8,128)(2,1)S(1)}, u32[]{:S(2)}, u32[]{:S(2)}) async-start(bf16[8,24,1536]{2,1,0:T(8,128)(2,1)} %get-tuple-element.16), calls=%async_computation.2 | async-start | bytes 1179648 | tf_op jit(solution)/shard_map/all_to_all | solution.py:193
  84.1 9.8 %all-to-all-done.2 = bf16[8,24,1536]{2,1,0:T(8,128)(2,1)S(1)} async-done(((bf16[8,24,1536]{2,1,0:T(8,128)(2,1)}), bf16[8,24,1536]{2,1,0:T(8,128)(2,1)S(1)}, u32[]{:S(2)}, u32[]{:S(2)}) %all-to-all-start.2) | async-done | bytes 589856 | tf_op jit(solution)/shard_map/all_to_all | solution.py:193
  93.8 0.2 reshape.52
  94.0 0.3 fusion.2
  94.4 0.3 fusion.3
  94.7 3.0 %collective-permute-start.14 = (bf16[15,192]{1,0:T(8,128)(2,1)S(1)}, bf16[15,192]{1,0:T(8,128)(2,1)S(1)}, u32[]{:S(2)}, u32[]{:S(2)}) collective-permute-start(bf16[15,192]{1,0:T(8,128)(2,1)S(1)} %get-tuple-element.18), channel_id=1, source_target_pairs={{8,0},{16,8},{24,16},{32,24},{40,32},{48,40},{56,48},{64,56},{72,6... | collective-permute-start | bytes 17288 | tf_op jit(solution)/shard_map/ppermute | solution.py:258
  97.7 1.9 %collective-permute-start.13 = (bf16[15,192]{1,0:T(8,128)(2,1)S(1)}, bf16[15,192]{1,0:T(8,128)(2,1)S(1)}, u32[]{:S(2)}, u32[]{:S(2)}) collective-permute-start(bf16[15,192]{1,0:T(8,128)(2,1)S(1)} %get-tuple-element.17), channel_id=1, source_target_pairs={{0,8},{8,16},{16,24},{24,32},{32,40},{40,48},{48,56},{56,64},{64,7... | collective-permute-start | bytes 17288 | tf_op jit(solution)/shard_map/ppermute | solution.py:257
  99.7 6.0 %collective-permute-done.13 = bf16[15,192]{1,0:T(8,128)(2,1)S(1)} collective-permute-done((bf16[15,192]{1,0:T(8,128)(2,1)S(1)}, bf16[15,192]{1,0:T(8,128)(2,1)S(1)}, u32[]{:S(2)}, u32[]{:S(2)}) %collective-permute-start.13) | collective-permute-done | bytes 5792 | tf_op jit(solution)/shard_map/ppermute | solution.py:257
  105.7 1.1 convolution_convert_fusion
  106.8 0.2 reshape.53
  106.9 14.4 %all_to_all.20 = bf16[8,22,1536]{2,1,0:T(8,128)(2,1)S(1)} all-to-all(bf16[8,22,1536]{2,1,0:T(8,128)(2,1)S(1)} %reshape.53), channel_id=1, replica_groups=mesh['seq'=32,'mp'=8] {'mp'}, dimensions={0} | all-to-all | bytes 1081344 | tf_op jit(solution)/shard_map/all_to_all | solution.py:193
  121.3 0.1 convert_reduce_fusion
  121.4 0.7 add_convert_fusion
  (38 shorter events, 0.2 us)
Async XLA Ops:
  0.0 105.7 %copy-start = (bf16[192,1536]{1,0:T(8,128)(2,1)S(1)}, bf16[192,1536]{1,0:T(8,128)(2,1)}, u32[]{:S(2)}) copy-start(bf16[192,1536]{1,0:T(8,128)(2,1)} %param.23) | copy-start | bytes 1769476
  1.5 0.9 copy-start.3
  3.4 15.7 %all-to-all-start = ((bf16[8,24,1536]{2,1,0:T(8,128)(2,1)}), bf16[8,24,1536]{2,1,0:T(8,128)(2,1)S(1)}, u32[]{:S(2)}, u32[]{:S(2)}) async-start(bf16[8,24,1536]{2,1,0:T(8,128)(2,1)} %shard_map.118), calls=%async_computation | async-start | bytes 1179648 | tf_op jit(solution)/shard_map/all_to_all | solution.py:193
  9.0 10.0 %copy-start.1 = (bf16[3,192,1536]{2,1,0:T(8,128)(2,1)S(1)}, bf16[3,192,1536]{2,1,0:T(8,128)(2,1)}, u32[]{:S(2)}) copy-start(bf16[3,192,1536]{2,1,0:T(8,128)(2,1)} %w_ref.4) | copy-start | bytes 5308420
  19.9 12.9 %collective-permute-start.3 = (bf16[176,384]{1,0:T(8,128)(2,1)S(1)}, bf16[176,384]{1,0:T(8,128)(2,1)S(1)}, u32[]{:S(2)}, u32[]{:S(2)}) collective-permute-start(bf16[176,384]{1,0:T(8,128)(2,1)S(1)} %shard_map.120.refs_4_), channel_id=1, source_target_pairs={{0,128},{8,136},{16,144},{24,152},{32,160},{40,168},{48,176},{56,1... | collective-permute-start | bytes 405512 | tf_op jit(solution)/shard_map/ppermute | solution.py:29
  21.2 12.1 %collective-permute-start.4 = (bf16[176,384]{1,0:T(8,128)(2,1)S(1)}, bf16[176,384]{1,0:T(8,128)(2,1)S(1)}, u32[]{:S(2)}, u32[]{:S(2)}) collective-permute-start(bf16[176,384]{1,0:T(8,128)(2,1)S(1)} %shard_map.120.refs_4_), channel_id=1, source_target_pairs={{0,64},{8,72},{16,80},{24,88},{32,96},{40,104},{48,112},{56,120},{... | collective-permute-start | bytes 405512 | tf_op jit(solution)/shard_map/ppermute | solution.py:29
  23.4 10.0 %collective-permute-start.5 = (bf16[176,384]{1,0:T(8,128)(2,1)S(1)}, bf16[176,384]{1,0:T(8,128)(2,1)S(1)}, u32[]{:S(2)}, u32[]{:S(2)}) collective-permute-start(bf16[176,384]{1,0:T(8,128)(2,1)S(1)} %shard_map.120.refs_4_), channel_id=1, source_target_pairs={{0,192},{8,200},{16,208},{24,216},{32,224},{40,232},{48,240},{56,2... | collective-permute-start | bytes 405512 | tf_op jit(solution)/shard_map/ppermute | solution.py:29
  23.9 40.1 %copy-start.2 = (bf16[192,1536]{1,0:T(8,128)(2,1)S(1)}, bf16[192,1536]{1,0:T(8,128)(2,1)}, u32[]{:S(2)}) copy-start(bf16[192,1536]{1,0:T(8,128)(2,1)} %w_ref.5) | copy-start | bytes 1769476
  24.0 8.8 %collective-permute-start = (bf16[96,384]{1,0:T(8,128)(2,1)S(1)}, bf16[96,384]{1,0:T(8,128)(2,1)S(1)}, u32[]{:S(2)}, u32[]{:S(2)}) collective-permute-start(bf16[96,384]{1,0:T(8,128)(2,1)S(1)} %shard_map.119.refs_0_), channel_id=1, source_target_pairs={{0,32},{8,40},{16,48},{24,56},{32,0},{40,8},{48,16},{56,24},{64,96... | collective-permute-start | bytes 221192 | tf_op jit(solution)/shard_map/ppermute | solution.py:29
  30.3 6.5 %collective-permute-start.1 = (bf16[96,384]{1,0:T(8,128)(2,1)S(1)}, bf16[96,384]{1,0:T(8,128)(2,1)S(1)}, u32[]{:S(2)}, u32[]{:S(2)}) collective-permute-start(bf16[96,384]{1,0:T(8,128)(2,1)S(1)} %shard_map.119.refs_0_), channel_id=1, source_target_pairs={{0,16},{8,24},{16,32},{24,40},{32,48},{40,56},{48,0},{56,8},{64,80... | collective-permute-start | bytes 221192 | tf_op jit(solution)/shard_map/ppermute | solution.py:29
  32.7 11.1 %collective-permute-start.6 = (bf16[176,384]{1,0:T(8,128)(2,1)S(1)}, bf16[176,384]{1,0:T(8,128)(2,1)S(1)}, u32[]{:S(2)}, u32[]{:S(2)}) collective-permute-start(bf16[176,384]{1,0:T(8,128)(2,1)S(1)} %shard_map.120.refs_4_), channel_id=1, source_target_pairs={{0,8},{8,0},{16,24},{24,16},{32,40},{40,32},{48,56},{56,48},{64,72... | collective-permute-start | bytes 405512 | tf_op jit(solution)/shard_map/ppermute | solution.py:29
  32.8 11.1 %collective-permute-start.7 = (bf16[176,384]{1,0:T(8,128)(2,1)S(1)}, bf16[176,384]{1,0:T(8,128)(2,1)S(1)}, u32[]{:S(2)}, u32[]{:S(2)}) collective-permute-start(bf16[176,384]{1,0:T(8,128)(2,1)S(1)} %collective-permute-done.3.refs_5_), channel_id=1, source_target_pairs={{0,8},{8,0},{16,24},{24,16},{32,40},{40,32},{48,56},{56,48},{64,72... | collective-permute-start | bytes 405512 | tf_op jit(solution)/shard_map/ppermute | solution.py:29
  33.3 10.6 %collective-permute-start.8 = (bf16[176,384]{1,0:T(8,128)(2,1)S(1)}, bf16[176,384]{1,0:T(8,128)(2,1)S(1)}, u32[]{:S(2)}, u32[]{:S(2)}) collective-permute-start(bf16[176,384]{1,0:T(8,128)(2,1)S(1)} %collective-permute-done.4.refs_6_), channel_id=1, source_target_pairs={{0,8},{8,0},{16,24},{24,16},{32,40},{40,32},{48,56},{56,48},{64,72... | collective-permute-start | bytes 405512 | tf_op jit(solution)/shard_map/ppermute | solution.py:29
  33.4 10.5 %collective-permute-start.9 = (bf16[176,384]{1,0:T(8,128)(2,1)S(1)}, bf16[176,384]{1,0:T(8,128)(2,1)S(1)}, u32[]{:S(2)}, u32[]{:S(2)}) collective-permute-start(bf16[176,384]{1,0:T(8,128)(2,1)S(1)} %collective-permute-done.5.refs_7_), channel_id=1, source_target_pairs={{0,8},{8,0},{16,24},{24,16},{32,40},{40,32},{48,56},{56,48},{64,72... | collective-permute-start | bytes 405512 | tf_op jit(solution)/shard_map/ppermute | solution.py:29
  36.8 7.1 %collective-permute-start.2 = (bf16[96,384]{1,0:T(8,128)(2,1)S(1)}, bf16[96,384]{1,0:T(8,128)(2,1)S(1)}, u32[]{:S(2)}, u32[]{:S(2)}) collective-permute-start(bf16[96,384]{1,0:T(8,128)(2,1)S(1)} %shard_map.119.refs_0_), channel_id=1, source_target_pairs={{0,48},{8,56},{16,0},{24,8},{32,16},{40,24},{48,32},{56,40},{64,11... | collective-permute-start | bytes 221192 | tf_op jit(solution)/shard_map/ppermute | solution.py:29
  50.4 8.6 %collective-permute-start.10 = (bf16[176,256]{1,0:T(8,128)(2,1)S(1)}, bf16[176,256]{1,0:T(8,128)(2,1)S(1)}, u32[]{:S(2)}, u32[]{:S(2)}) collective-permute-start(bf16[176,256]{1,0:T(8,128)(2,1)S(1)} %get-tuple-element.12), channel_id=1, source_target_pairs={{0,32},{8,40},{16,48},{24,56},{32,0},{40,8},{48,16},{56,24},{64,96... | collective-permute-start | bytes 270344 | tf_op jit(solution)/shard_map/ppermute | solution.py:29
  54.0 9.1 %collective-permute-start.11 = (bf16[176,256]{1,0:T(8,128)(2,1)S(1)}, bf16[176,256]{1,0:T(8,128)(2,1)S(1)}, u32[]{:S(2)}, u32[]{:S(2)}) collective-permute-start(bf16[176,256]{1,0:T(8,128)(2,1)S(1)} %get-tuple-element.13), channel_id=1, source_target_pairs={{0,48},{8,56},{16,0},{24,8},{32,16},{40,24},{48,32},{56,40},{64,11... | collective-permute-start | bytes 270344 | tf_op jit(solution)/shard_map/ppermute | solution.py:29
  56.1 7.9 %collective-permute-start.12 = (bf16[176,256]{1,0:T(8,128)(2,1)S(1)}, bf16[176,256]{1,0:T(8,128)(2,1)S(1)}, u32[]{:S(2)}, u32[]{:S(2)}) collective-permute-start(bf16[176,256]{1,0:T(8,128)(2,1)S(1)} %get-tuple-element.14), channel_id=1, source_target_pairs={{0,16},{8,24},{16,32},{24,40},{32,48},{40,56},{48,0},{56,8},{64,80... | collective-permute-start | bytes 270344 | tf_op jit(solution)/shard_map/ppermute | solution.py:29
  64.0 5.4 %copy-start.6 = (f32[1536]{0:T(1024)S(1)}, f32[1536]{0:T(1024)}, u32[]{:S(2)}) copy-start(f32[1536]{0:T(1024)} %param.17) | copy-start | bytes 18436
  64.0 5.4 %copy-start.7 = (f32[1536]{0:T(1024)S(1)}, f32[1536]{0:T(1024)}, u32[]{:S(2)}) copy-start(f32[1536]{0:T(1024)} %param.18) | copy-start | bytes 18436
  64.0 15.2 %copy-start.4 = (bf16[22,1536]{1,0:T(8,128)(2,1)S(1)}, bf16[22,1536]{1,0:T(8,128)(2,1)}, u32[]{:S(2)}) copy-start(bf16[22,1536]{1,0:T(8,128)(2,1)} %x_ref.3) | copy-start | bytes 202756
  65.7 13.5 %all-to-all-start.1 = ((bf16[8,24,1536]{2,1,0:T(8,128)(2,1)}), bf16[8,24,1536]{2,1,0:T(8,128)(2,1)S(1)}, u32[]{:S(2)}, u32[]{:S(2)}) async-start(bf16[8,24,1536]{2,1,0:T(8,128)(2,1)} %shard_map.122), calls=%async_computation.1 | async-start | bytes 1179648 | tf_op jit(solution)/shard_map/all_to_all | solution.py:193
  69.4 14.6 %copy-start.5 = (f32[31,192]{1,0:T(8,128)S(1)}, f32[31,192]{1,0:T(8,128)}, u32[]{:S(2)}) copy-start(f32[31,192]{1,0:T(8,128)} %param.20) | copy-start | bytes 71428
  80.3 13.6 %copy-start.8 = (bf16[2,192,1536]{2,1,0:T(8,128)(2,1)S(1)}, bf16[2,192,1536]{2,1,0:T(8,128)(2,1)}, u32[]{:S(2)}) copy-start(bf16[2,192,1536]{2,1,0:T(8,128)(2,1)} %param.19) | copy-start | bytes 3538948
  80.3 13.5 %all-to-all-start.2 = ((bf16[8,24,1536]{2,1,0:T(8,128)(2,1)}), bf16[8,24,1536]{2,1,0:T(8,128)(2,1)S(1)}, u32[]{:S(2)}, u32[]{:S(2)}) async-start(bf16[8,24,1536]{2,1,0:T(8,128)(2,1)} %get-tuple-element.16), calls=%async_computation.2 | async-start | bytes 1179648 | tf_op jit(solution)/shard_map/all_to_all | solution.py:193
  94.3 11.3 %copy-start.9 = (f32[192]{0:T(256)S(1)}, f32[192]{0:T(256)}, u32[]{:S(2)}) copy-start(f32[192]{0:T(256)} %param.22) | copy-start | bytes 2308
  94.3 11.3 %copy-start.10 = (f32[192]{0:T(256)S(1)}, f32[192]{0:T(256)}, u32[]{:S(2)}) copy-start(f32[192]{0:T(256)} %param.21) | copy-start | bytes 2308
  94.7 4.9 %collective-permute-start.14 = (bf16[15,192]{1,0:T(8,128)(2,1)S(1)}, bf16[15,192]{1,0:T(8,128)(2,1)S(1)}, u32[]{:S(2)}, u32[]{:S(2)}) collective-permute-start(bf16[15,192]{1,0:T(8,128)(2,1)S(1)} %get-tuple-element.18), channel_id=1, source_target_pairs={{8,0},{16,8},{24,16},{32,24},{40,32},{48,40},{56,48},{64,56},{72,6... | collective-permute-start | bytes 17288 | tf_op jit(solution)/shard_map/ppermute | solution.py:258
  97.7 8.0 %collective-permute-start.13 = (bf16[15,192]{1,0:T(8,128)(2,1)S(1)}, bf16[15,192]{1,0:T(8,128)(2,1)S(1)}, u32[]{:S(2)}, u32[]{:S(2)}) collective-permute-start(bf16[15,192]{1,0:T(8,128)(2,1)S(1)} %get-tuple-element.17), channel_id=1, source_target_pairs={{0,8},{8,16},{16,24},{24,32},{32,40},{40,48},{48,56},{56,64},{64,7... | collective-permute-start | bytes 17288 | tf_op jit(solution)/shard_map/ppermute | solution.py:257

commit v3 on v2

--- a/solution.py
+++ b/solution.py
@@ -50,7 +50,7 @@
         out_specs=VMEM if single else tuple(VMEM for _ in outs),
         scratch_shapes=list(scratch),
         cost_estimate=pl.CostEstimate(flops=flops, bytes_accessed=size, transcendentals=0),
-        compiler_params=pltpu.CompilerParams(vmem_limit_bytes=48 * 2**20),
+        compiler_params=pltpu.CompilerParams(vmem_limit_bytes=16 * 2**20),
     )(*args)
 
 
@@ -69,7 +69,7 @@
 
 
 def norm_body(x_ref, gain_ref, shift_ref, out_ref):
-    normed = norm_rows(x_ref[...].astype(F32), gain_ref[...], shift_ref[...])
+    normed = norm_rows(x_ref[...].astype(F32), gain_ref[...].reshape(1, D), shift_ref[...].reshape(1, D))
     for peer in range(PEERS):
         out_ref[peer, 0:ROWS, :] = normed
 
@@ -114,44 +114,32 @@
     out_ref[...] = tight[...].astype(BF16)
 
 
-def attend_body(*refs):
-    q_refs, kv_refs = refs[0:4], refs[4:12]
-    out_refs = refs[12:16]
-    q_all, kv_all, o_all = refs[16:19]
-    for n, ref in enumerate(q_refs):
-        q_all[n * BLOCK : n * BLOCK + 96, :] = ref[:, 0:256]
-        second = pltpu.roll(ref[:, 128:384].astype(F32), 192, 1).astype(BF16)
-        q_all[n * BLOCK + 80 : n * BLOCK + 176, :] = second
-    for n, ref in enumerate(kv_refs):
-        kv_all[n * BLOCK : n * BLOCK + BLOCK, :] = ref[...]
+def attend_body(q_ref, near_ref, far_ref, out_ref, q_all):
+    q_all[0:96, :] = q_ref[:, 0:256].astype(F32)
+    q_all[80:176, :] = pltpu.roll(q_ref[:, 128:384].astype(F32), 192, 1)
+    near = near_ref[...].reshape(4 * BLOCK, 2 * WIDTH)
+    far = far_ref[...].reshape(4 * BLOCK, 2 * WIDTH)
     factor = LOG2E / HEAD**0.5
     lane = lax.broadcasted_iota(jnp.int32, (BLOCK, 256), 1)
-
-    def step(n, unused):
-        q = q_all[pl.ds(pl.multiple_of(n * BLOCK, 16), BLOCK), :].astype(F32)
-        result, stats = None, jnp.zeros((BLOCK, 256), F32)
-        for head in range(2):
-            own = (lane >= head * HEAD) & (lane < head * HEAD + HEAD)
-            scores = dot_t(jnp.where(own, q, 0.0).astype(BF16), kv_all[:, 0:256])
-            top = jnp.max(scores, axis=1, keepdims=True)
-            weights = jnp.exp2((scores - top) * factor)
-            total = jnp.sum(weights, axis=1, keepdims=True)
-            mixed = dot(weights.astype(BF16), kv_all[:, 128:384]) * (1.0 / total)
-            level = top * factor + jnp.log2(total)
-            high = level.astype(BF16).astype(F32)
-            middle = (level - high).astype(BF16).astype(F32)
-            low = level - high - middle
-            for place, piece in enumerate((high, middle, low)):
-                stats = jnp.where(lane == head * 3 + place, piece, stats)
-            result = mixed if head == 0 else jnp.where(lane < 160, result, mixed)
-        o_all[pl.ds(pl.multiple_of(n * BLOCK, 16), BLOCK), :] = jnp.where(
-            lane < 64, stats, result
-        ).astype(BF16)
-        return unused
-
-    lax.fori_loop(0, 4, step, 0)
-    for n, ref in enumerate(out_refs):
-        ref[...] = o_all[n * BLOCK : n * BLOCK + BLOCK, :]
+    q = q_all[...]
+    result, stats = None, jnp.zeros((BLOCK, 256), F32)
+    for head in range(2):
+        own = (lane >= head * HEAD) & (lane < head * HEAD + HEAD)
+        q_head = jnp.where(own, q, 0.0).astype(BF16)
+        scores = [dot_t(q_head, kv[:, 0:256]) for kv in (near, far)]
+        top = jnp.maximum(*[jnp.max(part, axis=1, keepdims=True) for part in scores])
+        weights = [jnp.exp2((part - top) * factor) for part in scores]
+        total = sum(jnp.sum(part, axis=1, keepdims=True) for part in weights)
+        mixed = sum(dot(w.astype(BF16), kv[:, 128:384]) for w, kv in zip(weights, (near, far)))
+        mixed = mixed * (1.0 / total)
+        level = top * factor + jnp.log2(total)
+        high = level.astype(BF16).astype(F32)
+        middle = (level - high).astype(BF16).astype(F32)
+        low = level - high - middle
+        for place, piece in enumerate((high, middle, low)):
+            stats = jnp.where(lane == head * 3 + place, piece, stats)
+        result = mixed if head == 0 else jnp.where(lane < 160, result, mixed)
+    out_ref[...] = jnp.where(lane < 64, stats, result).astype(BF16)
 
 
 def merge_body(a_ref, b_ref, c_ref, d_ref, w_ref, out_ref, spread):
@@ -184,7 +172,7 @@
     total = jnp.sum(got_ref[...].astype(F32), axis=0)[0:ROWS]
     mid = (x_ref[...].astype(F32) + total).astype(BF16)
     mid_ref[...] = mid
-    normed = norm_rows(mid.astype(F32), gain_ref[...], shift_ref[...])
+    normed = norm_rows(mid.astype(F32), gain_ref[...].reshape(1, D), shift_ref[...].reshape(1, D))
     for peer in range(PEERS):
         out_ref[peer, 0:ROWS, :] = normed
 
@@ -225,37 +213,39 @@
 ):
     slots = shape((PEERS, SLOT, D))
     attn_in = exchange(
-        call(norm_body, slots)(frames_in, attn_gain.reshape(1, D), attn_shift.reshape(1, D))
+        call(norm_body, slots)(frames_in, attn_gain, attn_shift)
     )
     cosine, sine = tables()
-    scratch = [pltpu.VMEM((BLOCK, 256), F32)]
-    queries = call(query_body, shape((96, 384)), scratch)(attn_in, w_qkv, cosine, sine)
+    tight = pltpu.VMEM((BLOCK, 256), F32)
+    queries = call(query_body, shape((96, 384)), [tight])(attn_in, w_qkv, cosine, sine)
+    attn_in, queries = lax.optimization_barrier((attn_in, queries))
+    steps = (2, 1, -1)
+    q_got = [hop(queries, along_z(step)) for step in steps]
     scratch = [pltpu.VMEM((BLOCK, 384), F32)]
     pair = call(pair_body, shape((BLOCK, 384)), scratch)(attn_in, w_qkv, cosine, sine)
-
-    steps = (2, 1, -1)
-    q_got = [queries] + [hop(queries, along_z(step)) for step in steps]
-    kv_got = [pair] + [hop(pair, along_y(step)) for step in steps]
-    kv_got += [hop(kv, other_core) for kv in kv_got]
-    scratch = [
-        pltpu.VMEM((4 * BLOCK, 256), BF16),
-        pltpu.VMEM((8 * BLOCK, 384), BF16),
-        pltpu.VMEM((4 * BLOCK, 256), BF16),
-    ]
-    parts = call(attend_body, (shape((BLOCK, 256)),) * 4, scratch)(*q_got, *kv_got)
-    back = [parts[0]] + [hop(parts[n + 1], along_z(-step)) for n, step in enumerate(steps)]
+    near = [pair] + [hop(pair, along_y(step)) for step in steps]
+    *near, q_got[0], q_got[1], q_got[2] = lax.optimization_barrier((*near, *q_got))
+    near = jnp.stack(near)
+    far = hop(near, other_core)
+    attend = call(attend_body, shape((BLOCK, 256)), [tight])
+    back = [attend(queries, near, far)]
+    back += [hop(attend(q, near, far), along_z(-step)) for q, step in zip(q_got, steps)]
     scratch = [pltpu.VMEM((PEERS * SLOT, 256), F32)]
     sums = exchange(call(merge_body, slots, scratch)(*back, w_attn_out))
     mid, conv_in = call(middle_body, (shape((ROWS, D)), slots))(
-        sums, frames_in, conv_gain.reshape(1, D), conv_shift.reshape(1, D)
+        sums, frames_in, conv_gain, conv_shift
     )
     conv_in = exchange(conv_in)[:, :ROWS].reshape(BLOCK, D)
     value_half = dot_t(conv_in, w_pointwise_in[0])
     gate_half = dot_t(conv_in, w_pointwise_in[1])
     glu = (value_half * jax.nn.sigmoid(gate_half)).astype(BF16)
-    count = lax.axis_size("seq")
-    ahead = lax.ppermute(glu[-REACH:], "seq", [(i, i + 1) for i in range(count - 1)])
-    behind = lax.ppermute(glu[:REACH], "seq", [(i + 1, i) for i in range(count - 1)])
+    even = lax.axis_index("seq") % 2 == 0
+    head, tail = glu[:16], glu[-16:]
+    inner = hop(jnp.where(even, tail, head), other_core)
+    links = [(i, i + 1) for i in range(1, 31, 2)] + [(i + 1, i) for i in range(1, 31, 2)]
+    outer = lax.ppermute(jnp.where(even, head, tail), "seq", links)
+    ahead = jnp.where(even, outer, inner)[1:]
+    behind = jnp.where(even, inner, outer)[:REACH]
     padded = jnp.concatenate([ahead, glu, behind], axis=0)
     depth = jnp.zeros((BLOCK, WIDTH), F32)
     for tap in range(TAPS):

time: 123 us -> 111 us (0.902)
  waiting for transfers between devices: 46.5 us -> 28.7 us
  blocking collectives: 14.4 us -> 28 us
  starting transfers between devices: 41.7 us -> 34.2 us
    all_to_all x1 -> x2, blocking collectives: 14.4 us -> 28 us  [exchange(): return lax.all_to_all(array, 'mp', 0, 0, tiled=False)]
    all_to_all x3 -> x2, waiting for transfers between devices: 27.1 us -> 16.2 us  [exchange(): return lax.all_to_all(array, 'mp', 0, 0, tiled=False)]
    ppermute x13 -> x11, waiting for transfers between devices: 13.3 us -> 8.64 us  [hop(): return lax.ppermute(array, 'seq', [(i, place(i)) for i in range(count)])]
    all_to_all x3 -> x2, starting transfers between devices: 13.1 us -> 9.32 us  [exchange(): return lax.all_to_all(array, 'mp', 0, 0, tiled=False)]
    ppermute x13 -> x11, starting transfers between devices: 23.7 us -> 20.9 us  [hop(): return lax.ppermute(array, 'seq', [(i, place(i)) for i in range(count)])]
    ppermute x2 -> x1, waiting for transfers between devices: 6.02 us -> 3.92 us  [local(): outer = lax.ppermute(jnp.where(even, head, tail), 'seq', links)]
    reshape x4 -> x0, local copies, waits for them, and re-layouts: 1.48 us -> none  [the longest x1 0.76 us: local(): attn_gain.reshape(1, D)]
    unnamed x22 -> x26, local copies, waits for them, and re-layouts: 0.93 us -> 2.39 us
  transfers between devices with their start and end apart: 18 -> 14, of which waited for: 10 -> 7; matrix products, arithmetic and copies ran while one was open for 2% -> 2% of each run, Pallas kernels for 0% -> 5%
where the time goes in v3:
time: 111 us; the launch traced here: 110 us
  starting transfers between devices  34.2 us (31%)
  waiting for transfers between devices  28.7 us (26%)
  blocking collectives  28 us (25%)
  Pallas kernels  10.6 us (10%)
  local copies, waits for them, and re-layouts  4.67 us (4%)
  matrix products  1.74 us (2%)
  other arithmetic  1.3 us (1%)
    all_to_all x2, blocking collectives, exchange(): return lax.all_to_all(array, 'mp', 0, 0, tiled=False)  28 us
    ppermute x11, starting transfers between devices, hop(): return lax.ppermute(array, 'seq', [(i, place(i)) for i in range(count)])  20.9 us
    all_to_all x2, waiting for transfers between devices, exchange(): return lax.all_to_all(array, 'mp', 0, 0, tiled=False)  16.2 us
    pallas_call x9, Pallas kernels, call(): pl.pallas_call(body, out_shape=outs, in_specs=[VMEM] * len(args), out_spe...  10.6 us
    all_to_all x2, starting transfers between devices, exchange(): return lax.all_to_all(array, 'mp', 0, 0, tiled=False)  9.32 us
    ppermute x11, waiting for transfers between devices, hop(): return lax.ppermute(array, 'seq', [(i, place(i)) for i in range(count)])  8.64 us
    ppermute x1, starting transfers between devices, local(): outer = lax.ppermute(jnp.where(even, head, tail), 'seq', links)  4.01 us
    ppermute x1, waiting for transfers between devices, local(): outer = lax.ppermute(jnp.where(even, head, tail), 'seq', links)  3.92 us
  transfers between devices with their start and end apart: 14, of which 7 were waited for; matrix products, arithmetic and copies ran while one was open for 2% of the time, Pallas kernels for 5%

profile of v3, /device:TPU:24, one launch (start us, length us, event | category | flops | bytes accessed | tf_op | source)
XLA Modules:
  0.0 109.6 jit_solution(11770332665950128920)
XLA Ops:
  0.0 0.9 copy-done.3
  1.0 0.7 copy-done.5
  1.6 0.7 copy-done.6
  2.3 1.1 shard_map.118
  3.4 5.7 %all-to-all-start = ((bf16[8,24,1536]{2,1,0:T(8,128)(2,1)}), bf16[8,24,1536]{2,1,0:T(8,128)(2,1)S(1)}, u32[]{:S(2)}, u32[]{:S(2)}) async-start(bf16[8,24,1536]{2,1,0:T(8,128)(2,1)} %shard_map.118), calls=%async_computation | async-start | bytes 1179648 | tf_op jit(solution)/shard_map/all_to_all | solution.py:181
  9.1 0.4 multiply_sine_fusion
  9.5 0.2 concatenate.41.cos_ref
  9.7 0.6 broadcast_in_dim.5
  10.4 1.1 %concatenate.42.sin_ref = f32[192,256]{1,0:T(8,128)S(1)} concatenate(f32[192,48]{1,0:T(8,128)S(1)} %get-tuple-element.63, f32[192,48]{1,0:T(8,128)S(1)} %get-tuple-element.62, f32[192,48]{1,0:T(8,128)S(1)} %get-tuple-element.63, f32[192,48]{1,0:T(8,128)S(1)} %get-tuple-element.62, f32[192,64]{1,0:T(8,128)} %broadcast_in_dim.5), dimensions={1} | concatenate | bytes 393216 | tf_op jit(solution)/shard_map/concatenate | solution.py:196
  11.5 7.6 %all-to-all-done.x_ref = bf16[8,24,1536]{2,1,0:T(8,128)(2,1)S(1)} async-done(((bf16[8,24,1536]{2,1,0:T(8,128)(2,1)}), bf16[8,24,1536]{2,1,0:T(8,128)(2,1)S(1)}, u32[]{:S(2)}, u32[]{:S(2)}) %all-to-all-start) | async-done | bytes 589856 | tf_op jit(solution)/shard_map/all_to_all | solution.py:181
  19.1 0.6 shard_map.119.q_ref
  19.7 6.4 %collective-permute-start.3 = (bf16[96,384]{1,0:T(8,128)(2,1)S(1)}, bf16[96,384]{1,0:T(8,128)(2,1)S(1)}, u32[]{:S(2)}, u32[]{:S(2)}) collective-permute-start(bf16[96,384]{1,0:T(8,128)(2,1)S(1)} %shard_map.119.q_ref), channel_id=1, source_target_pairs={{0,32},{8,40},{16,48},{24,56},{32,0},{40,8},{48,16},{56,24},{64,96... | collective-permute-start | bytes 221192 | tf_op jit(solution)/shard_map/ppermute | solution.py:29
  26.1 0.8 shard_map.120
  26.8 1.3 %collective-permute-start = (bf16[176,384]{1,0:T(8,128)(2,1)S(1)}, bf16[176,384]{1,0:T(8,128)(2,1)S(1)}, u32[]{:S(2)}, u32[]{:S(2)}) collective-permute-start(bf16[176,384]{1,0:T(8,128)(2,1)S(1)} %shard_map.120), channel_id=1, source_target_pairs={{0,128},{8,136},{16,144},{24,152},{32,160},{40,168},{48,176},{56,1... | collective-permute-start | bytes 405512 | tf_op jit(solution)/shard_map/ppermute | solution.py:29
  28.1 2.2 %collective-permute-start.1 = (bf16[176,384]{1,0:T(8,128)(2,1)S(1)}, bf16[176,384]{1,0:T(8,128)(2,1)S(1)}, u32[]{:S(2)}, u32[]{:S(2)}) collective-permute-start(bf16[176,384]{1,0:T(8,128)(2,1)S(1)} %shard_map.120), channel_id=1, source_target_pairs={{0,64},{8,72},{16,80},{24,88},{32,96},{40,104},{48,112},{56,120},{... | collective-permute-start | bytes 405512 | tf_op jit(solution)/shard_map/ppermute | solution.py:29
  30.3 1.5 %collective-permute-start.4 = (bf16[96,384]{1,0:T(8,128)(2,1)S(1)}, bf16[96,384]{1,0:T(8,128)(2,1)S(1)}, u32[]{:S(2)}, u32[]{:S(2)}) collective-permute-start(bf16[96,384]{1,0:T(8,128)(2,1)S(1)} %shard_map.119.q_ref), channel_id=1, source_target_pairs={{0,16},{8,24},{16,32},{24,40},{32,48},{40,56},{48,0},{56,8},{64,80... | collective-permute-start | bytes 221192 | tf_op jit(solution)/shard_map/ppermute | solution.py:29
  31.8 2.7 %collective-permute-start.5 = (bf16[96,384]{1,0:T(8,128)(2,1)S(1)}, bf16[96,384]{1,0:T(8,128)(2,1)S(1)}, u32[]{:S(2)}, u32[]{:S(2)}) collective-permute-start(bf16[96,384]{1,0:T(8,128)(2,1)S(1)} %shard_map.119.q_ref), channel_id=1, source_target_pairs={{0,48},{8,56},{16,0},{24,8},{32,16},{40,24},{48,32},{56,40},{64,11... | collective-permute-start | bytes 221192 | tf_op jit(solution)/shard_map/ppermute | solution.py:29
  34.5 2.4 %collective-permute-done.4.q_ref = bf16[96,384]{1,0:T(8,128)(2,1)S(1)} collective-permute-done((bf16[96,384]{1,0:T(8,128)(2,1)S(1)}, bf16[96,384]{1,0:T(8,128)(2,1)S(1)}, u32[]{:S(2)}, u32[]{:S(2)}) %collective-permute-start.4) | collective-permute-done | bytes 73760 | tf_op jit(solution)/shard_map/ppermute | solution.py:29
  36.9 0.2 collective-permute-done.5.q_ref
  37.1 0.1 pad_maximum_fusion.near_ref
  37.2 0.1 collective-permute-start.6
  37.3 1.9 %collective-permute-done.6.far_ref = bf16[4,176,384]{2,1,0:T(8,128)(2,1)S(1)} collective-permute-done((bf16[4,176,384]{2,1,0:T(8,128)(2,1)S(1)}, bf16[4,176,384]{2,1,0:T(8,128)(2,1)S(1)}, u32[]{:S(2)}, u32[]{:S(2)}) %collective-permute-start.6) | collective-permute-done | bytes 540704 | tf_op jit(solution)/shard_map/ppermute | solution.py:29
  39.2 1.5 %shard_map.122 = bf16[176,256]{1,0:T(8,128)(2,1)S(1)} custom-call(bf16[96,384]{1,0:T(8,128)(2,1)S(1)} %collective-permute-done.3.q_ref, bf16[4,176,384]{2,1,0:T(8,128)(2,1)S(1)} %pad_maximum_fusion.near_ref, bf16[4,176,384]{2,1,0:T(8,128)(2,1)S(1)} %collective-permute-done.6.far_ref), custom_call_target="tpu_custom_call" | custom-call | flops 1000000 | bytes 1000000 | tf_op jit(solution)/shard_map/pallas_call | solution.py:46
  40.7 3.4 %collective-permute-start.7 = (bf16[176,256]{1,0:T(8,128)(2,1)S(1)}, bf16[176,256]{1,0:T(8,128)(2,1)S(1)}, u32[]{:S(2)}, u32[]{:S(2)}) collective-permute-start(bf16[176,256]{1,0:T(8,128)(2,1)S(1)} %shard_map.122), channel_id=1, source_target_pairs={{0,32},{8,40},{16,48},{24,56},{32,0},{40,8},{48,16},{56,24},{64,96... | collective-permute-start | bytes 270344 | tf_op jit(solution)/shard_map/ppermute | solution.py:29
  44.2 1.6 %shard_map.123 = bf16[176,256]{1,0:T(8,128)(2,1)S(1)} custom-call(bf16[96,384]{1,0:T(8,128)(2,1)S(1)} %collective-permute-done.4.q_ref, bf16[4,176,384]{2,1,0:T(8,128)(2,1)S(1)} %pad_maximum_fusion.near_ref, bf16[4,176,384]{2,1,0:T(8,128)(2,1)S(1)} %collective-permute-done.6.far_ref), custom_call_target="tpu_custom_call" | custom-call | flops 1000000 | bytes 1000000 | tf_op jit(solution)/shard_map/pallas_call | solution.py:46
  45.7 1.7 %collective-permute-start.8 = (bf16[176,256]{1,0:T(8,128)(2,1)S(1)}, bf16[176,256]{1,0:T(8,128)(2,1)S(1)}, u32[]{:S(2)}, u32[]{:S(2)}) collective-permute-start(bf16[176,256]{1,0:T(8,128)(2,1)S(1)} %shard_map.123), channel_id=1, source_target_pairs={{0,48},{8,56},{16,0},{24,8},{32,16},{40,24},{48,32},{56,40},{64,11... | collective-permute-start | bytes 270344 | tf_op jit(solution)/shard_map/ppermute | solution.py:29
  47.4 1.6 %shard_map.124 = bf16[176,256]{1,0:T(8,128)(2,1)S(1)} custom-call(bf16[96,384]{1,0:T(8,128)(2,1)S(1)} %collective-permute-done.5.q_ref, bf16[4,176,384]{2,1,0:T(8,128)(2,1)S(1)} %pad_maximum_fusion.near_ref, bf16[4,176,384]{2,1,0:T(8,128)(2,1)S(1)} %collective-permute-done.6.far_ref), custom_call_target="tpu_custom_call" | custom-call | flops 1000000 | bytes 1000000 | tf_op jit(solution)/shard_map/pallas_call | solution.py:46
  49.0 1.6 %collective-permute-start.9 = (bf16[176,256]{1,0:T(8,128)(2,1)S(1)}, bf16[176,256]{1,0:T(8,128)(2,1)S(1)}, u32[]{:S(2)}, u32[]{:S(2)}) collective-permute-start(bf16[176,256]{1,0:T(8,128)(2,1)S(1)} %shard_map.124), channel_id=1, source_target_pairs={{0,16},{8,24},{16,32},{24,40},{32,48},{40,56},{48,0},{56,8},{64,80... | collective-permute-start | bytes 270344 | tf_op jit(solution)/shard_map/ppermute | solution.py:29
  50.6 1.6 %shard_map.121.a_ref = bf16[176,256]{1,0:T(8,128)(2,1)S(1)} custom-call(bf16[96,384]{1,0:T(8,128)(2,1)S(1)} %shard_map.119.q_ref, bf16[4,176,384]{2,1,0:T(8,128)(2,1)S(1)} %pad_maximum_fusion.near_ref, bf16[4,176,384]{2,1,0:T(8,128)(2,1)S(1)} %collective-permute-done.6.far_ref), custom_call_target="tpu_custom_call" | custom-call | flops 1000000 | bytes 1000000 | tf_op jit(solution)/shard_map/pallas_call | solution.py:46
  52.1 0.0 copy-start.7
  52.2 0.0 copy-start.8
  52.2 4.1 %collective-permute-done.8.c_ref = bf16[176,256]{1,0:T(8,128)(2,1)S(1)} collective-permute-done((bf16[176,256]{1,0:T(8,128)(2,1)S(1)}, bf16[176,256]{1,0:T(8,128)(2,1)S(1)}, u32[]{:S(2)}, u32[]{:S(2)}) %collective-permute-start.8) | collective-permute-done | bytes 90144 | tf_op jit(solution)/shard_map/ppermute | solution.py:29
  56.3 0.8 shard_map.125
  57.1 15.5 %all_to_all.20.got_ref = bf16[8,24,1536]{2,1,0:T(8,128)(2,1)S(1)} all-to-all(bf16[8,24,1536]{2,1,0:T(8,128)(2,1)S(1)} %shard_map.125), channel_id=1, replica_groups=mesh['seq'=32,'mp'=8] {'mp'}, dimensions={0} | all-to-all | bytes 1179648 | tf_op jit(solution)/shard_map/all_to_all | solution.py:181
  72.7 1.2 %shard_map.126 = (bf16[22,1536]{1,0:T(8,128)(2,1)S(1)}, bf16[8,24,1536]{2,1,0:T(8,128)(2,1)}) custom-call(bf16[8,24,1536]{2,1,0:T(8,128)(2,1)S(1)} %all_to_all.20.got_ref, bf16[22,1536]{1,0:T(8,128)(2,1)S(1)} %copy-done.4, f32[1536]{0:T(1024)S(1)} %copy-done.7, f32[1536]{0:T(1024)S(1)} %copy-done.8), custom_call_target="tpu_custom_call" | custom-call | flops 1000000 | bytes 1000000 | tf_op jit(solution)/shard_map/pallas_call | solution.py:46
  73.8 3.7 %all-to-all-start.2 = ((bf16[8,24,1536]{2,1,0:T(8,128)(2,1)}), bf16[8,24,1536]{2,1,0:T(8,128)(2,1)S(1)}, u32[]{:S(2)}, u32[]{:S(2)}) async-start(bf16[8,24,1536]{2,1,0:T(8,128)(2,1)} %get-tuple-element.26), calls=%async_computation.2 | async-start | bytes 1179648 | tf_op jit(solution)/shard_map/all_to_all | solution.py:181
  77.5 8.6 %all-to-all-done.2 = bf16[8,24,1536]{2,1,0:T(8,128)(2,1)S(1)} async-done(((bf16[8,24,1536]{2,1,0:T(8,128)(2,1)}), bf16[8,24,1536]{2,1,0:T(8,128)(2,1)S(1)}, u32[]{:S(2)}, u32[]{:S(2)}) %all-to-all-start.2) | async-done | bytes 589856 | tf_op jit(solution)/shard_map/all_to_all | solution.py:181
  86.1 0.2 reshape.36
  86.3 0.3 fusion.2
  86.7 0.3 fusion.3
  87.0 0.1 collective-permute-start.11
  87.1 4.0 %collective-permute-start.10 = (bf16[16,192]{1,0:T(8,128)(2,1)S(1)}, bf16[16,192]{1,0:T(8,128)(2,1)S(1)}, u32[]{:S(2)}, u32[]{:S(2)}) collective-permute-start(bf16[16,192]{1,0:T(8,128)(2,1)S(1)} %get-tuple-element.28), channel_id=1, source_target_pairs={{8,16},{24,32},{40,48},{56,64},{72,80},{88,96},{104,112},{120,128}... | collective-permute-start | bytes 18440 | tf_op jit(solution)/shard_map/ppermute | solution.py:246
  91.2 3.9 %collective-permute-done.10 = bf16[16,192]{1,0:T(8,128)(2,1)S(1)} collective-permute-done((bf16[16,192]{1,0:T(8,128)(2,1)S(1)}, bf16[16,192]{1,0:T(8,128)(2,1)S(1)}, u32[]{:S(2)}, u32[]{:S(2)}) %collective-permute-start.10) | collective-permute-done | bytes 6176 | tf_op jit(solution)/shard_map/ppermute | solution.py:246
  95.1 1.1 convolution_convert_fusion
  96.2 0.2 reshape.37
  96.4 12.5 %all_to_all.21 = bf16[8,22,1536]{2,1,0:T(8,128)(2,1)S(1)} all-to-all(bf16[8,22,1536]{2,1,0:T(8,128)(2,1)S(1)} %reshape.37), channel_id=1, replica_groups=mesh['seq'=32,'mp'=8] {'mp'}, dimensions={0} | all-to-all | bytes 1081344 | tf_op jit(solution)/shard_map/all_to_all | solution.py:181
  108.8 0.1 convert_reduce_fusion
  108.9 0.7 add_convert_fusion
  (36 shorter events, 0.2 us)
Async XLA Ops:
  0.0 95.1 %copy-start = (bf16[192,1536]{1,0:T(8,128)(2,1)S(1)}, bf16[192,1536]{1,0:T(8,128)(2,1)}, u32[]{:S(2)}) copy-start(bf16[192,1536]{1,0:T(8,128)(2,1)} %param.23) | copy-start | bytes 1769476
  0.0 0.9 copy-start.3
  1.0 0.7 copy-start.5
  1.6 0.7 copy-start.6
  3.4 15.7 %all-to-all-start = ((bf16[8,24,1536]{2,1,0:T(8,128)(2,1)}), bf16[8,24,1536]{2,1,0:T(8,128)(2,1)S(1)}, u32[]{:S(2)}, u32[]{:S(2)}) async-start(bf16[8,24,1536]{2,1,0:T(8,128)(2,1)} %shard_map.118), calls=%async_computation | async-start | bytes 1179648 | tf_op jit(solution)/shard_map/all_to_all | solution.py:181
  9.1 10.0 %copy-start.1 = (bf16[3,192,1536]{2,1,0:T(8,128)(2,1)S(1)}, bf16[3,192,1536]{2,1,0:T(8,128)(2,1)}, u32[]{:S(2)}) copy-start(bf16[3,192,1536]{2,1,0:T(8,128)(2,1)} %w_ref.4) | copy-start | bytes 5308420
  19.7 12.1 %collective-permute-start.3 = (bf16[96,384]{1,0:T(8,128)(2,1)S(1)}, bf16[96,384]{1,0:T(8,128)(2,1)S(1)}, u32[]{:S(2)}, u32[]{:S(2)}) collective-permute-start(bf16[96,384]{1,0:T(8,128)(2,1)S(1)} %shard_map.119.q_ref), channel_id=1, source_target_pairs={{0,32},{8,40},{16,48},{24,56},{32,0},{40,8},{48,16},{56,24},{64,96... | collective-permute-start | bytes 221192 | tf_op jit(solution)/shard_map/ppermute | solution.py:29
  26.8 10.2 %collective-permute-start = (bf16[176,384]{1,0:T(8,128)(2,1)S(1)}, bf16[176,384]{1,0:T(8,128)(2,1)S(1)}, u32[]{:S(2)}, u32[]{:S(2)}) collective-permute-start(bf16[176,384]{1,0:T(8,128)(2,1)S(1)} %shard_map.120), channel_id=1, source_target_pairs={{0,128},{8,136},{16,144},{24,152},{32,160},{40,168},{48,176},{56,1... | collective-permute-start | bytes 405512 | tf_op jit(solution)/shard_map/ppermute | solution.py:29
  28.1 8.9 %collective-permute-start.1 = (bf16[176,384]{1,0:T(8,128)(2,1)S(1)}, bf16[176,384]{1,0:T(8,128)(2,1)S(1)}, u32[]{:S(2)}, u32[]{:S(2)}) collective-permute-start(bf16[176,384]{1,0:T(8,128)(2,1)S(1)} %shard_map.120), channel_id=1, source_target_pairs={{0,64},{8,72},{16,80},{24,88},{32,96},{40,104},{48,112},{56,120},{... | collective-permute-start | bytes 405512 | tf_op jit(solution)/shard_map/ppermute | solution.py:29
  30.3 6.7 %collective-permute-start.2 = (bf16[176,384]{1,0:T(8,128)(2,1)S(1)}, bf16[176,384]{1,0:T(8,128)(2,1)S(1)}, u32[]{:S(2)}, u32[]{:S(2)}) collective-permute-start(bf16[176,384]{1,0:T(8,128)(2,1)S(1)} %shard_map.120), channel_id=1, source_target_pairs={{0,192},{8,200},{16,208},{24,216},{32,224},{40,232},{48,240},{56,2... | collective-permute-start | bytes 405512 | tf_op jit(solution)/shard_map/ppermute | solution.py:29
  30.3 6.6 %collective-permute-start.4 = (bf16[96,384]{1,0:T(8,128)(2,1)S(1)}, bf16[96,384]{1,0:T(8,128)(2,1)S(1)}, u32[]{:S(2)}, u32[]{:S(2)}) collective-permute-start(bf16[96,384]{1,0:T(8,128)(2,1)S(1)} %shard_map.119.q_ref), channel_id=1, source_target_pairs={{0,16},{8,24},{16,32},{24,40},{32,48},{40,56},{48,0},{56,8},{64,80... | collective-permute-start | bytes 221192 | tf_op jit(solution)/shard_map/ppermute | solution.py:29
  31.8 5.3 %collective-permute-start.5 = (bf16[96,384]{1,0:T(8,128)(2,1)S(1)}, bf16[96,384]{1,0:T(8,128)(2,1)S(1)}, u32[]{:S(2)}, u32[]{:S(2)}) collective-permute-start(bf16[96,384]{1,0:T(8,128)(2,1)S(1)} %shard_map.119.q_ref), channel_id=1, source_target_pairs={{0,48},{8,56},{16,0},{24,8},{32,16},{40,24},{48,32},{56,40},{64,11... | collective-permute-start | bytes 221192 | tf_op jit(solution)/shard_map/ppermute | solution.py:29
  37.2 2.0 %collective-permute-start.6 = (bf16[4,176,384]{2,1,0:T(8,128)(2,1)S(1)}, bf16[4,176,384]{2,1,0:T(8,128)(2,1)S(1)}, u32[]{:S(2)}, u32[]{:S(2)}) collective-permute-start(bf16[4,176,384]{2,1,0:T(8,128)(2,1)S(1)} %pad_maximum_fusion.near_ref), channel_id=1, source_target_pairs={{0,8},{8,0},{16,24},{24,16},{32,40},{40,32},{48,56},{56,48},{64,72... | collective-permute-start | bytes 1622024 | tf_op jit(solution)/shard_map/ppermute | solution.py:29
  40.7 11.4 %collective-permute-start.7 = (bf16[176,256]{1,0:T(8,128)(2,1)S(1)}, bf16[176,256]{1,0:T(8,128)(2,1)S(1)}, u32[]{:S(2)}, u32[]{:S(2)}) collective-permute-start(bf16[176,256]{1,0:T(8,128)(2,1)S(1)} %shard_map.122), channel_id=1, source_target_pairs={{0,32},{8,40},{16,48},{24,56},{32,0},{40,8},{48,16},{56,24},{64,96... | collective-permute-start | bytes 270344 | tf_op jit(solution)/shard_map/ppermute | solution.py:29
  45.7 10.6 %copy-start.2 = (bf16[192,1536]{1,0:T(8,128)(2,1)S(1)}, bf16[192,1536]{1,0:T(8,128)(2,1)}, u32[]{:S(2)}) copy-start(bf16[192,1536]{1,0:T(8,128)(2,1)} %w_ref.5) | copy-start | bytes 1769476
  45.7 10.6 %collective-permute-start.8 = (bf16[176,256]{1,0:T(8,128)(2,1)S(1)}, bf16[176,256]{1,0:T(8,128)(2,1)S(1)}, u32[]{:S(2)}, u32[]{:S(2)}) collective-permute-start(bf16[176,256]{1,0:T(8,128)(2,1)S(1)} %shard_map.123), channel_id=1, source_target_pairs={{0,48},{8,56},{16,0},{24,8},{32,16},{40,24},{48,32},{56,40},{64,11... | collective-permute-start | bytes 270344 | tf_op jit(solution)/shard_map/ppermute | solution.py:29
  49.0 7.3 %collective-permute-start.9 = (bf16[176,256]{1,0:T(8,128)(2,1)S(1)}, bf16[176,256]{1,0:T(8,128)(2,1)S(1)}, u32[]{:S(2)}, u32[]{:S(2)}) collective-permute-start(bf16[176,256]{1,0:T(8,128)(2,1)S(1)} %shard_map.124), channel_id=1, source_target_pairs={{0,16},{8,24},{16,32},{24,40},{32,48},{40,56},{48,0},{56,8},{64,80... | collective-permute-start | bytes 270344 | tf_op jit(solution)/shard_map/ppermute | solution.py:29
  52.1 20.5 %copy-start.4 = (bf16[22,1536]{1,0:T(8,128)(2,1)S(1)}, bf16[22,1536]{1,0:T(8,128)(2,1)}, u32[]{:S(2)}) copy-start(bf16[22,1536]{1,0:T(8,128)(2,1)} %x_ref.3) | copy-start | bytes 202756
  52.1 20.5 %copy-start.7 = (f32[1536]{0:T(1024)S(1)}, f32[1536]{0:T(1024)}, u32[]{:S(2)}) copy-start(f32[1536]{0:T(1024)} %gain_ref.3) | copy-start | bytes 18436
  52.2 20.5 %copy-start.8 = (f32[1536]{0:T(1024)S(1)}, f32[1536]{0:T(1024)}, u32[]{:S(2)}) copy-start(f32[1536]{0:T(1024)} %shift_ref.3) | copy-start | bytes 18436
  72.6 4.9 %copy-start.9 = (f32[31,192]{1,0:T(8,128)S(1)}, f32[31,192]{1,0:T(8,128)}, u32[]{:S(2)}) copy-start(f32[31,192]{1,0:T(8,128)} %param.20) | copy-start | bytes 71428
  73.8 12.5 %copy-start.10 = (bf16[2,192,1536]{2,1,0:T(8,128)(2,1)S(1)}, bf16[2,192,1536]{2,1,0:T(8,128)(2,1)}, u32[]{:S(2)}) copy-start(bf16[2,192,1536]{2,1,0:T(8,128)(2,1)} %param.19) | copy-start | bytes 3538948
  73.8 12.3 %all-to-all-start.2 = ((bf16[8,24,1536]{2,1,0:T(8,128)(2,1)}), bf16[8,24,1536]{2,1,0:T(8,128)(2,1)S(1)}, u32[]{:S(2)}, u32[]{:S(2)}) async-start(bf16[8,24,1536]{2,1,0:T(8,128)(2,1)} %get-tuple-element.26), calls=%async_computation.2 | async-start | bytes 1179648 | tf_op jit(solution)/shard_map/all_to_all | solution.py:181
  86.6 8.5 %copy-start.11 = (f32[192]{0:T(256)S(1)}, f32[192]{0:T(256)}, u32[]{:S(2)}) copy-start(f32[192]{0:T(256)} %param.22) | copy-start | bytes 2308
  86.6 8.5 %copy-start.12 = (f32[192]{0:T(256)S(1)}, f32[192]{0:T(256)}, u32[]{:S(2)}) copy-start(f32[192]{0:T(256)} %param.21) | copy-start | bytes 2308
  87.0 4.1 %collective-permute-start.11 = (bf16[16,192]{1,0:T(8,128)(2,1)S(1)}, bf16[16,192]{1,0:T(8,128)(2,1)S(1)}, u32[]{:S(2)}, u32[]{:S(2)}) collective-permute-start(bf16[16,192]{1,0:T(8,128)(2,1)S(1)} %get-tuple-element.27), channel_id=1, source_target_pairs={{0,8},{8,0},{16,24},{24,16},{32,40},{40,32},{48,56},{56,48},{64,72... | collective-permute-start | bytes 18440 | tf_op jit(solution)/shard_map/ppermute | solution.py:29
  87.1 8.0 %collective-permute-start.10 = (bf16[16,192]{1,0:T(8,128)(2,1)S(1)}, bf16[16,192]{1,0:T(8,128)(2,1)S(1)}, u32[]{:S(2)}, u32[]{:S(2)}) collective-permute-start(bf16[16,192]{1,0:T(8,128)(2,1)S(1)} %get-tuple-element.28), channel_id=1, source_target_pairs={{8,16},{24,32},{40,48},{56,64},{72,80},{88,96},{104,112},{120,128}... | collective-permute-start | bytes 18440 | tf_op jit(solution)/shard_map/ppermute | solution.py:246

commit v4 on v3

--- a/solution.py
+++ b/solution.py
@@ -41,16 +41,16 @@
     return i ^ 1
 
 
-def call(body, outs, scratch=(), flops=1_000_000, size=1_000_000):
+def call(body, outs, scratch=(), flops=1_000_000, size=1_000_000, specs=None, vmem=16):
     single = isinstance(outs, jax.ShapeDtypeStruct)
     return lambda *args: pl.pallas_call(
         body,
         out_shape=outs,
-        in_specs=[VMEM] * len(args),
+        in_specs=specs or [VMEM] * len(args),
         out_specs=VMEM if single else tuple(VMEM for _ in outs),
         scratch_shapes=list(scratch),
         cost_estimate=pl.CostEstimate(flops=flops, bytes_accessed=size, transcendentals=0),
-        compiler_params=pltpu.CompilerParams(vmem_limit_bytes=16 * 2**20),
+        compiler_params=pltpu.CompilerParams(vmem_limit_bytes=vmem * 2**20),
     )(*args)
 
 
@@ -68,8 +68,20 @@
     return (center * lax.rsqrt(spread + 1e-05) * gain + shift).astype(BF16)
 
 
-def norm_body(x_ref, gain_ref, shift_ref, out_ref):
-    normed = norm_rows(x_ref[...].astype(F32), gain_ref[...].reshape(1, D), shift_ref[...].reshape(1, D))
+def norm_body(x_any, gain_any, shift_any, out_ref, x_ref, gain_ref, shift_ref, done):
+    copies = [
+        pltpu.make_async_copy(source, target, done.at[n])
+        for n, (source, target) in enumerate(
+            ((x_any, x_ref), (gain_any, gain_ref), (shift_any, shift_ref))
+        )
+    ]
+    for copy in copies:
+        copy.start()
+    for copy in copies:
+        copy.wait()
+    normed = norm_rows(
+        x_ref[...].astype(F32), gain_ref[...].reshape(1, D), shift_ref[...].reshape(1, D)
+    )
     for peer in range(PEERS):
         out_ref[peer, 0:ROWS, :] = normed
 
@@ -114,32 +126,74 @@
     out_ref[...] = tight[...].astype(BF16)
 
 
-def attend_body(q_ref, near_ref, far_ref, out_ref, q_all):
-    q_all[0:96, :] = q_ref[:, 0:256].astype(F32)
-    q_all[80:176, :] = pltpu.roll(q_ref[:, 128:384].astype(F32), 192, 1)
-    near = near_ref[...].reshape(4 * BLOCK, 2 * WIDTH)
-    far = far_ref[...].reshape(4 * BLOCK, 2 * WIDTH)
+def unpack_queries(q_refs, q_all):
+    for n, ref in enumerate(q_refs):
+        q_all[n * BLOCK : n * BLOCK + 96, :] = ref[:, 0:256].astype(F32)
+        second = pltpu.roll(ref[:, 128:384].astype(F32), 192, 1)
+        q_all[n * BLOCK + 80 : n * BLOCK + 176, :] = second
+
+
+def softmax_rows(q, head, pieces):
+    lane = lax.broadcasted_iota(jnp.int32, q.shape, 1)
+    own = (lane >= head * HEAD) & (lane < head * HEAD + HEAD)
+    q_head = jnp.where(own, q, 0.0).astype(BF16)
     factor = LOG2E / HEAD**0.5
-    lane = lax.broadcasted_iota(jnp.int32, (BLOCK, 256), 1)
-    q = q_all[...]
-    result, stats = None, jnp.zeros((BLOCK, 256), F32)
-    for head in range(2):
-        own = (lane >= head * HEAD) & (lane < head * HEAD + HEAD)
-        q_head = jnp.where(own, q, 0.0).astype(BF16)
-        scores = [dot_t(q_head, kv[:, 0:256]) for kv in (near, far)]
-        top = jnp.maximum(*[jnp.max(part, axis=1, keepdims=True) for part in scores])
-        weights = [jnp.exp2((part - top) * factor) for part in scores]
-        total = sum(jnp.sum(part, axis=1, keepdims=True) for part in weights)
-        mixed = sum(dot(w.astype(BF16), kv[:, 128:384]) for w, kv in zip(weights, (near, far)))
-        mixed = mixed * (1.0 / total)
-        level = top * factor + jnp.log2(total)
+    scores = [dot_t(q_head, kv[:, 0:256]) for kv in pieces]
+    top = functools.reduce(jnp.maximum, [jnp.max(part, axis=1, keepdims=True) for part in scores])
+    weights = [jnp.exp2((part - top) * factor) for part in scores]
+    total = sum(jnp.sum(part, axis=1, keepdims=True) for part in weights)
+    mixed = sum(dot(w.astype(BF16), kv[:, 128:384]) for w, kv in zip(weights, pieces))
+    return mixed * (1.0 / total), top * factor + jnp.log2(total)
+
+
+def with_levels(first, second, levels):
+    lane = lax.broadcasted_iota(jnp.int32, first.shape, 1)
+    stats = jnp.zeros(first.shape, F32)
+    for head, level in enumerate(levels):
         high = level.astype(BF16).astype(F32)
         middle = (level - high).astype(BF16).astype(F32)
         low = level - high - middle
         for place, piece in enumerate((high, middle, low)):
             stats = jnp.where(lane == head * 3 + place, piece, stats)
-        result = mixed if head == 0 else jnp.where(lane < 160, result, mixed)
-    out_ref[...] = jnp.where(lane < 64, stats, result).astype(BF16)
+    return jnp.where(lane < 64, stats, jnp.where(lane < 160, first, second)).astype(BF16)
+
+
+def flat(ref):
+    return ref[...].reshape(4 * BLOCK, 2 * WIDTH)
+
+
+def own_body(q_ref, near_ref, far_ref, out_ref, q_all):
+    unpack_queries((q_ref,), q_all)
+    pieces = (flat(near_ref), flat(far_ref))
+    (first, level_0), (second, level_1) = [softmax_rows(q_all[...], h, pieces) for h in (0, 1)]
+    out_ref[...] = with_levels(first, second, (level_0, level_1))
+
+
+def near_body(a_ref, b_ref, c_ref, kv_ref, out_ref, level_ref, q_all):
+    unpack_queries((a_ref, b_ref, c_ref), q_all)
+    pieces = (flat(kv_ref),)
+    (first, level_0), (second, level_1) = [softmax_rows(q_all[...], h, pieces) for h in (0, 1)]
+    lane = lax.broadcasted_iota(jnp.int32, first.shape, 1)
+    out_ref[...] = jnp.where(lane < 160, first, second)
+    narrow = lax.broadcasted_iota(jnp.int32, (3 * BLOCK, 128), 1)
+    level_ref[...] = jnp.where(narrow == 0, level_0, level_1)
+
+
+def far_body(a_ref, b_ref, c_ref, kv_ref, near_ref, level_ref, x_ref, y_ref, z_ref, q_all):
+    unpack_queries((a_ref, b_ref, c_ref), q_all)
+    pieces = (flat(kv_ref),)
+    merged, levels = [], []
+    for head in (0, 1):
+        result, level = softmax_rows(q_all[...], head, pieces)
+        before = level_ref[:, head : head + 1]
+        top = jnp.maximum(level, before)
+        new, old = jnp.exp2(level - top), jnp.exp2(before - top)
+        total = new + old
+        merged.append(result * (new / total) + near_ref[...] * (old / total))
+        levels.append(top + jnp.log2(total))
+    sent = with_levels(merged[0], merged[1], levels)
+    for n, ref in enumerate((x_ref, y_ref, z_ref)):
+        ref[...] = sent[n * BLOCK : n * BLOCK + BLOCK]
 
 
 def merge_body(a_ref, b_ref, c_ref, d_ref, w_ref, out_ref, spread):
@@ -213,23 +267,37 @@
 ):
     slots = shape((PEERS, SLOT, D))
     attn_in = exchange(
-        call(norm_body, slots)(frames_in, attn_gain, attn_shift)
+        call(
+            norm_body,
+            slots,
+            [
+                pltpu.VMEM((ROWS, D), BF16),
+                pltpu.VMEM((D,), F32),
+                pltpu.VMEM((D,), F32),
+                pltpu.SemaphoreType.DMA((3,)),
+            ],
+            specs=[pl.BlockSpec(memory_space=pl.ANY)] * 3,
+            vmem=60,
+        )(frames_in, attn_gain, attn_shift)
     )
     cosine, sine = tables()
+    scratch = [pltpu.VMEM((BLOCK, 384), F32)]
+    pair = call(pair_body, shape((BLOCK, 384)), scratch)(attn_in, w_qkv, cosine, sine)
+    attn_in, pair = lax.optimization_barrier((attn_in, pair))
+    steps = (2, 1, -1)
+    near = [pair] + [hop(pair, along_z(step)) for step in steps]
     tight = pltpu.VMEM((BLOCK, 256), F32)
     queries = call(query_body, shape((96, 384)), [tight])(attn_in, w_qkv, cosine, sine)
-    attn_in, queries = lax.optimization_barrier((attn_in, queries))
-    steps = (2, 1, -1)
-    q_got = [hop(queries, along_z(step)) for step in steps]
-    scratch = [pltpu.VMEM((BLOCK, 384), F32)]
-    pair = call(pair_body, shape((BLOCK, 384)), scratch)(attn_in, w_qkv, cosine, sine)
-    near = [pair] + [hop(pair, along_y(step)) for step in steps]
+    q_got = [hop(queries, along_y(step)) for step in steps]
     *near, q_got[0], q_got[1], q_got[2] = lax.optimization_barrier((*near, *q_got))
     near = jnp.stack(near)
     far = hop(near, other_core)
-    attend = call(attend_body, shape((BLOCK, 256)), [tight])
-    back = [attend(queries, near, far)]
-    back += [hop(attend(q, near, far), along_z(-step)) for q, step in zip(q_got, steps)]
+    wide = 3 * BLOCK
+    room = [pltpu.VMEM((wide, 256), F32)]
+    partial = call(near_body, (shape((wide, 256), F32), shape((wide, 128), F32)), room)(*q_got, near)
+    sent = call(far_body, (shape((BLOCK, 256)),) * 3, room)(*q_got, far, *partial)
+    back = [hop(part, along_y(-step)) for part, step in zip(sent, steps)]
+    back.append(call(own_body, shape((BLOCK, 256)), [tight])(queries, near, far))
     scratch = [pltpu.VMEM((PEERS * SLOT, 256), F32)]
     sums = exchange(call(merge_body, slots, scratch)(*back, w_attn_out))
     mid, conv_in = call(middle_body, (shape((ROWS, D)), slots))(

time: 111 us -> 104 us (0.937)
  blocking collectives: 28 us -> 25.7 us
  local copies, waits for them, and re-layouts: 4.67 us -> 2.4 us
  starting transfers between devices: 34.2 us -> 32.4 us
    unnamed x26 -> x20, local copies, waits for them, and re-layouts: 2.39 us -> 0.05 us
    all_to_all x2, blocking collectives: 28 us -> 25.7 us  [exchange(): return lax.all_to_all(array, 'mp', 0, 0, tiled=False)]
    ppermute x1, starting transfers between devices: 4.01 us -> 1.92 us  [local(): outer = lax.ppermute(jnp.where(even, head, tail), 'seq', links)]
    pallas_call x9 -> x8, Pallas kernels: 10.6 us -> 10.9 us  [call(): pl.pallas_call(body, out_shape=outs, in_specs=specs or [VMEM] * len(args)...]
  transfers between devices with their start and end apart: 14 -> 14, of which waited for: 7 -> 8; matrix products, arithmetic and copies ran while one was open for 2% -> 3% of each run, Pallas kernels for 5% -> 3%
where the time goes in v4:
time: 104 us; the launch traced here: 103 us
  starting transfers between devices  32.4 us (31%)
  waiting for transfers between devices  27.8 us (27%)
  blocking collectives  25.7 us (25%)
  Pallas kernels  10.9 us (10%)
  local copies, waits for them, and re-layouts  2.4 us (2%)
  other arithmetic  1.94 us (2%)
  matrix products  1.74 us (2%)
    all_to_all x2, blocking collectives, exchange(): return lax.all_to_all(array, 'mp', 0, 0, tiled=False)  25.7 us
    ppermute x11, starting transfers between devices, hop(): return lax.ppermute(array, 'seq', [(i, place(i)) for i in range(count)])  21.2 us
    all_to_all x2, waiting for transfers between devices, exchange(): return lax.all_to_all(array, 'mp', 0, 0, tiled=False)  15.4 us
    pallas_call x8, Pallas kernels, call(): pl.pallas_call(body, out_shape=outs, in_specs=specs or [VMEM] * len(args)...  10.9 us
    all_to_all x2, starting transfers between devices, exchange(): return lax.all_to_all(array, 'mp', 0, 0, tiled=False)  9.33 us
    ppermute x11, waiting for transfers between devices, hop(): return lax.ppermute(array, 'seq', [(i, place(i)) for i in range(count)])  7.87 us
    ppermute x1, waiting for transfers between devices, local(): outer = lax.ppermute(jnp.where(even, head, tail), 'seq', links)  4.53 us
  transfers between devices with their start and end apart: 14, of which 8 were waited for; matrix products, arithmetic and copies ran while one was open for 3% of the time, Pallas kernels for 3%

profile of v4, /device:TPU:24, one launch (start us, length us, event | category | flops | bytes accessed | tf_op | source)
XLA Modules:
  0.0 103.2 jit_solution(614783889296015037)
XLA Ops:
  0.0 2.0 %shard_map.118 = bf16[8,24,1536]{2,1,0:T(8,128)(2,1)} custom-call(bf16[22,1536]{1,0:T(8,128)(2,1)} %x_ref.1, f32[1536]{0:T(1024)} %gain_any.1, f32[1536]{0:T(1024)} %shift_any.1), custom_call_target="tpu_custom_call" | custom-call | flops 1000000 | bytes 1000000 | tf_op jit(solution)/shard_map/pallas_call | solution.py:46
  2.0 5.7 %all-to-all-start = ((bf16[8,24,1536]{2,1,0:T(8,128)(2,1)}), bf16[8,24,1536]{2,1,0:T(8,128)(2,1)S(1)}, u32[]{:S(2)}, u32[]{:S(2)}) async-start(bf16[8,24,1536]{2,1,0:T(8,128)(2,1)} %shard_map.118), calls=%async_computation | async-start | bytes 1179648 | tf_op jit(solution)/shard_map/all_to_all | solution.py:235
  7.7 1.1 %multiply_sine_fusion = (f32[192,48]{1,0:T(8,128)S(1)}, f32[192,48]{1,0:T(8,128)}, f32[192,48]{1,0:T(8,128)S(1)}) fusion(f32[48]{0:T(128)S(1)} %multiply_power_fusion, f32[192]{0:T(256)S(1)} %fusion.40), kind=kLoop, calls=%fused_computation.43 | loop fusion | flops 18432 | bytes 111552 | tf_op jit(solution)/shard_map/sin | solution.py:247
  8.8 0.2 concatenate.41.cos_ref
  9.0 0.6 broadcast_in_dim.5
  9.6 1.2 %concatenate.42.sin_ref = f32[192,256]{1,0:T(8,128)S(1)} concatenate(f32[192,48]{1,0:T(8,128)} %get-tuple-element.73, f32[192,48]{1,0:T(8,128)S(1)} %get-tuple-element.72, f32[192,48]{1,0:T(8,128)} %get-tuple-element.73, f32[192,48]{1,0:T(8,128)S(1)} %get-tuple-element.72, f32[192,64]{1,0:T(8,128)} %broadcast_in_dim.5), dimensions={1} | concatenate | bytes 393216 | tf_op jit(solution)/shard_map/concatenate | solution.py:250
  10.8 6.9 %all-to-all-done.x_ref = bf16[8,24,1536]{2,1,0:T(8,128)(2,1)S(1)} async-done(((bf16[8,24,1536]{2,1,0:T(8,128)(2,1)}), bf16[8,24,1536]{2,1,0:T(8,128)(2,1)S(1)}, u32[]{:S(2)}, u32[]{:S(2)}) %all-to-all-start) | async-done | bytes 589856 | tf_op jit(solution)/shard_map/all_to_all | solution.py:235
  17.7 0.8 shard_map.119
  18.5 0.6 shard_map.120.q_ref
  19.1 1.3 %collective-permute-start.3 = (bf16[96,384]{1,0:T(8,128)(2,1)S(1)}, bf16[96,384]{1,0:T(8,128)(2,1)S(1)}, u32[]{:S(2)}, u32[]{:S(2)}) collective-permute-start(bf16[96,384]{1,0:T(8,128)(2,1)S(1)} %shard_map.120.q_ref), channel_id=1, source_target_pairs={{0,128},{8,136},{16,144},{24,152},{32,160},{40,168},{48,176},{56,1... | collective-permute-start | bytes 221192 | tf_op jit(solution)/shard_map/ppermute | solution.py:29
  20.4 6.3 %collective-permute-start = (bf16[176,384]{1,0:T(8,128)(2,1)S(1)}, bf16[176,384]{1,0:T(8,128)(2,1)S(1)}, u32[]{:S(2)}, u32[]{:S(2)}) collective-permute-start(bf16[176,384]{1,0:T(8,128)(2,1)S(1)} %shard_map.119), channel_id=1, source_target_pairs={{0,32},{8,40},{16,48},{24,56},{32,0},{40,8},{48,16},{56,24},{64,96... | collective-permute-start | bytes 405512 | tf_op jit(solution)/shard_map/ppermute | solution.py:29
  26.7 1.5 %collective-permute-start.1 = (bf16[176,384]{1,0:T(8,128)(2,1)S(1)}, bf16[176,384]{1,0:T(8,128)(2,1)S(1)}, u32[]{:S(2)}, u32[]{:S(2)}) collective-permute-start(bf16[176,384]{1,0:T(8,128)(2,1)S(1)} %shard_map.119), channel_id=1, source_target_pairs={{0,16},{8,24},{16,32},{24,40},{32,48},{40,56},{48,0},{56,8},{64,80... | collective-permute-start | bytes 405512 | tf_op jit(solution)/shard_map/ppermute | solution.py:29
  28.2 2.7 %collective-permute-start.2 = (bf16[176,384]{1,0:T(8,128)(2,1)S(1)}, bf16[176,384]{1,0:T(8,128)(2,1)S(1)}, u32[]{:S(2)}, u32[]{:S(2)}) collective-permute-start(bf16[176,384]{1,0:T(8,128)(2,1)S(1)} %shard_map.119), channel_id=1, source_target_pairs={{0,48},{8,56},{16,0},{24,8},{32,16},{40,24},{48,32},{56,40},{64,11... | collective-permute-start | bytes 405512 | tf_op jit(solution)/shard_map/ppermute | solution.py:29
  30.8 2.2 %collective-permute-start.4 = (bf16[96,384]{1,0:T(8,128)(2,1)S(1)}, bf16[96,384]{1,0:T(8,128)(2,1)S(1)}, u32[]{:S(2)}, u32[]{:S(2)}) collective-permute-start(bf16[96,384]{1,0:T(8,128)(2,1)S(1)} %shard_map.120.q_ref), channel_id=1, source_target_pairs={{0,64},{8,72},{16,80},{24,88},{32,96},{40,104},{48,112},{56,120},{... | collective-permute-start | bytes 221192 | tf_op jit(solution)/shard_map/ppermute | solution.py:29
  33.0 2.2 %collective-permute-done.4.b_ref = bf16[96,384]{1,0:T(8,128)(2,1)S(1)} collective-permute-done((bf16[96,384]{1,0:T(8,128)(2,1)S(1)}, bf16[96,384]{1,0:T(8,128)(2,1)S(1)}, u32[]{:S(2)}, u32[]{:S(2)}) %collective-permute-start.4) | collective-permute-done | bytes 73760 | tf_op jit(solution)/shard_map/ppermute | solution.py:29
  35.2 3.4 %collective-permute-done.5.c_ref = bf16[96,384]{1,0:T(8,128)(2,1)S(1)} collective-permute-done((bf16[96,384]{1,0:T(8,128)(2,1)S(1)}, bf16[96,384]{1,0:T(8,128)(2,1)S(1)}, u32[]{:S(2)}, u32[]{:S(2)}) %collective-permute-start.5) | collective-permute-done | bytes 73760 | tf_op jit(solution)/shard_map/ppermute | solution.py:29
  38.6 0.8 collective-permute-done.2
  39.4 0.1 pad_maximum_fusion.kv_ref.near_ref
  39.5 0.1 collective-permute-start.6
  39.6 1.7 %shard_map.121 = (f32[528,256]{1,0:T(8,128)S(1)}, f32[528,128]{1,0:T(8,128)S(1)}) custom-call(bf16[96,384]{1,0:T(8,128)(2,1)S(1)} %collective-permute-done.3.a_ref, bf16[96,384]{1,0:T(8,128)(2,1)S(1)} %collective-permute-done.4.b_ref, bf16[96,384]{1,0:T(8,128)(2,1)S(1)} %collective-permute-done.5.c_ref, bf16[4,176,384]{2,1,0:T(8,128)(2,1)S(1)} %pad_maximum_fusion.kv_ref.near_ref), custom_call_target="tpu_custom_call" | custom-call | flops 1000000 | bytes 1000000 | tf_op jit(solution)/shard_map/pallas_call | solution.py:46
  41.3 0.2 collective-permute-done.6.kv_ref.far_ref
  41.5 2.3 %shard_map.122 = (bf16[176,256]{1,0:T(8,128)(2,1)S(1)}, bf16[176,256]{1,0:T(8,128)(2,1)S(1)}, bf16[176,256]{1,0:T(8,128)(2,1)S(1)}) custom-call(bf16[96,384]{1,0:T(8,128)(2,1)S(1)} %collective-permute-done.3.a_ref, bf16[96,384]{1,0:T(8,128)(2,1)S(1)} %collective-permute-done.4.b_ref, bf16[96,384]{1,0:T(8,128)(2,1)S(1)} %collective-permute-done.5.c_ref, ...), custom_call_target="tpu_custom_call" | custom-call | flops 1000000 | bytes 1000000 | tf_op jit(solution)/shard_map/pallas_call | solution.py:46
  43.8 2.4 %collective-permute-start.7 = (bf16[176,256]{1,0:T(8,128)(2,1)S(1)}, bf16[176,256]{1,0:T(8,128)(2,1)S(1)}, u32[]{:S(2)}, u32[]{:S(2)}) collective-permute-start(bf16[176,256]{1,0:T(8,128)(2,1)S(1)} %get-tuple-element.32), channel_id=1, source_target_pairs={{0,128},{8,136},{16,144},{24,152},{32,160},{40,168},{48,176},{56,1... | collective-permute-start | bytes 270344 | tf_op jit(solution)/shard_map/ppermute | solution.py:29
  46.2 0.7 collective-permute-start.8
  47.0 2.5 %collective-permute-start.9 = (bf16[176,256]{1,0:T(8,128)(2,1)S(1)}, bf16[176,256]{1,0:T(8,128)(2,1)S(1)}, u32[]{:S(2)}, u32[]{:S(2)}) collective-permute-start(bf16[176,256]{1,0:T(8,128)(2,1)S(1)} %get-tuple-element.34), channel_id=1, source_target_pairs={{0,64},{8,72},{16,80},{24,88},{32,96},{40,104},{48,112},{56,120},{... | collective-permute-start | bytes 270344 | tf_op jit(solution)/shard_map/ppermute | solution.py:29
  49.5 1.6 %shard_map.123.d_ref = bf16[176,256]{1,0:T(8,128)(2,1)S(1)} custom-call(bf16[96,384]{1,0:T(8,128)(2,1)S(1)} %shard_map.120.q_ref, bf16[4,176,384]{2,1,0:T(8,128)(2,1)S(1)} %pad_maximum_fusion.kv_ref.near_ref, bf16[4,176,384]{2,1,0:T(8,128)(2,1)S(1)} %collective-permute-done.6.kv_ref.far_ref), custom_call_target="tpu_custom_call" | custom-call | flops 1000000 | bytes 1000000 | tf_op jit(solution)/shard_map/pallas_call | solution.py:46
  51.1 0.0 copy-start.3
  51.1 0.0 copy-start.4
  51.1 0.0 copy-start.5
  51.1 1.3 %collective-permute-done.8.b_ref = bf16[176,256]{1,0:T(8,128)(2,1)S(1)} collective-permute-done((bf16[176,256]{1,0:T(8,128)(2,1)S(1)}, bf16[176,256]{1,0:T(8,128)(2,1)S(1)}, u32[]{:S(2)}, u32[]{:S(2)}) %collective-permute-start.8) | collective-permute-done | bytes 90144 | tf_op jit(solution)/shard_map/ppermute | solution.py:29
  52.4 0.8 shard_map.124
  53.2 13.5 %all_to_all.20.got_ref = bf16[8,24,1536]{2,1,0:T(8,128)(2,1)S(1)} all-to-all(bf16[8,24,1536]{2,1,0:T(8,128)(2,1)S(1)} %shard_map.124), channel_id=1, replica_groups=mesh['seq'=32,'mp'=8] {'mp'}, dimensions={0} | all-to-all | bytes 1179648 | tf_op jit(solution)/shard_map/all_to_all | solution.py:235
  66.8 0.0 copy-start.6
  66.8 1.1 %shard_map.125 = (bf16[22,1536]{1,0:T(8,128)(2,1)S(1)}, bf16[8,24,1536]{2,1,0:T(8,128)(2,1)}) custom-call(bf16[8,24,1536]{2,1,0:T(8,128)(2,1)S(1)} %all_to_all.20.got_ref, bf16[22,1536]{1,0:T(8,128)(2,1)S(1)} %copy-done.3, f32[1536]{0:T(1024)S(1)} %copy-done.4, f32[1536]{0:T(1024)S(1)} %copy-done.5), custom_call_target="tpu_custom_call" | custom-call | flops 1000000 | bytes 1000000 | tf_op jit(solution)/shard_map/pallas_call | solution.py:46
  67.9 3.7 %all-to-all-start.2 = ((bf16[8,24,1536]{2,1,0:T(8,128)(2,1)}), bf16[8,24,1536]{2,1,0:T(8,128)(2,1)S(1)}, u32[]{:S(2)}, u32[]{:S(2)}) async-start(bf16[8,24,1536]{2,1,0:T(8,128)(2,1)} %get-tuple-element.36), calls=%async_computation.2 | async-start | bytes 1179648 | tf_op jit(solution)/shard_map/all_to_all | solution.py:235
  71.6 8.5 %all-to-all-done.2 = bf16[8,24,1536]{2,1,0:T(8,128)(2,1)S(1)} async-done(((bf16[8,24,1536]{2,1,0:T(8,128)(2,1)}), bf16[8,24,1536]{2,1,0:T(8,128)(2,1)S(1)}, u32[]{:S(2)}, u32[]{:S(2)}) %all-to-all-start.2) | async-done | bytes 589856 | tf_op jit(solution)/shard_map/all_to_all | solution.py:235
  80.2 0.2 reshape.36
  80.3 0.3 fusion.2
  80.7 0.0 copy-start.8
  80.7 0.3 fusion.3
  81.1 1.9 %collective-permute-start.10 = (bf16[16,192]{1,0:T(8,128)(2,1)S(1)}, bf16[16,192]{1,0:T(8,128)(2,1)S(1)}, u32[]{:S(2)}, u32[]{:S(2)}) collective-permute-start(bf16[16,192]{1,0:T(8,128)(2,1)S(1)} %get-tuple-element.38), channel_id=1, source_target_pairs={{8,16},{24,32},{40,48},{56,64},{72,80},{88,96},{104,112},{120,128}... | collective-permute-start | bytes 18440 | tf_op jit(solution)/shard_map/ppermute | solution.py:314
  83.0 1.5 %collective-permute-start.11 = (bf16[16,192]{1,0:T(8,128)(2,1)S(1)}, bf16[16,192]{1,0:T(8,128)(2,1)S(1)}, u32[]{:S(2)}, u32[]{:S(2)}) collective-permute-start(bf16[16,192]{1,0:T(8,128)(2,1)S(1)} %get-tuple-element.37), channel_id=1, source_target_pairs={{0,8},{8,0},{16,24},{24,16},{32,40},{40,32},{48,56},{56,48},{64,72... | collective-permute-start | bytes 18440 | tf_op jit(solution)/shard_map/ppermute | solution.py:29
  84.5 4.5 %collective-permute-done.10 = bf16[16,192]{1,0:T(8,128)(2,1)S(1)} collective-permute-done((bf16[16,192]{1,0:T(8,128)(2,1)S(1)}, bf16[16,192]{1,0:T(8,128)(2,1)S(1)}, u32[]{:S(2)}, u32[]{:S(2)}) %collective-permute-start.10) | collective-permute-done | bytes 6176 | tf_op jit(solution)/shard_map/ppermute | solution.py:314
  89.1 1.1 %convolution_convert_fusion = bf16[176,1536]{1,0:T(8,128)(2,1)S(1)} fusion(bf16[192,1536]{1,0:T(8,128)(2,1)S(1)} %copy-done, bf16[176,192]{1,0:T(8,128)(2,1)S(1)} %fusion.3, bf16[15,192]{1,0:T(8,128)(2,1)S(1)} %get-tuple-element.71, bf16[15,192]{1,0:T(8,128)(2,1)S(1)} %get-tuple-element.70, f32[192]{0:T(256)S(1)} %copy-done.8, f32[192]{0:T(256)S(1)} %copy-done.9, ...), kind=kOutput, calls=%fused_computation | convolution fusion | flops 110466048 | bytes 1234944 | tf_op jit(solution)/shard_map/dot_general | solution.py:62
  90.2 0.2 reshape.37
  90.3 12.2 %all_to_all.21 = bf16[8,22,1536]{2,1,0:T(8,128)(2,1)S(1)} all-to-all(bf16[8,22,1536]{2,1,0:T(8,128)(2,1)S(1)} %reshape.37), channel_id=1, replica_groups=mesh['seq'=32,'mp'=8] {'mp'}, dimensions={0} | all-to-all | bytes 1081344 | tf_op jit(solution)/shard_map/all_to_all | solution.py:235
  102.5 0.1 convert_reduce_fusion
  102.6 0.7 add_convert_fusion
  (29 shorter events, 0.1 us)
Async XLA Ops:
  0.0 89.1 %copy-start = (bf16[192,1536]{1,0:T(8,128)(2,1)S(1)}, bf16[192,1536]{1,0:T(8,128)(2,1)}, u32[]{:S(2)}) copy-start(bf16[192,1536]{1,0:T(8,128)(2,1)} %param.23) | copy-start | bytes 1769476
  2.0 15.7 %all-to-all-start = ((bf16[8,24,1536]{2,1,0:T(8,128)(2,1)}), bf16[8,24,1536]{2,1,0:T(8,128)(2,1)S(1)}, u32[]{:S(2)}, u32[]{:S(2)}) async-start(bf16[8,24,1536]{2,1,0:T(8,128)(2,1)} %shard_map.118), calls=%async_computation | async-start | bytes 1179648 | tf_op jit(solution)/shard_map/all_to_all | solution.py:235
  7.7 10.0 %copy-start.1 = (bf16[3,192,1536]{2,1,0:T(8,128)(2,1)S(1)}, bf16[3,192,1536]{2,1,0:T(8,128)(2,1)}, u32[]{:S(2)}) copy-start(bf16[3,192,1536]{2,1,0:T(8,128)(2,1)} %w_ref.4) | copy-start | bytes 5308420
  19.1 13.9 %collective-permute-start.3 = (bf16[96,384]{1,0:T(8,128)(2,1)S(1)}, bf16[96,384]{1,0:T(8,128)(2,1)S(1)}, u32[]{:S(2)}, u32[]{:S(2)}) collective-permute-start(bf16[96,384]{1,0:T(8,128)(2,1)S(1)} %shard_map.120.q_ref), channel_id=1, source_target_pairs={{0,128},{8,136},{16,144},{24,152},{32,160},{40,168},{48,176},{56,1... | collective-permute-start | bytes 221192 | tf_op jit(solution)/shard_map/ppermute | solution.py:29
  20.4 18.2 %collective-permute-start = (bf16[176,384]{1,0:T(8,128)(2,1)S(1)}, bf16[176,384]{1,0:T(8,128)(2,1)S(1)}, u32[]{:S(2)}, u32[]{:S(2)}) collective-permute-start(bf16[176,384]{1,0:T(8,128)(2,1)S(1)} %shard_map.119), channel_id=1, source_target_pairs={{0,32},{8,40},{16,48},{24,56},{32,0},{40,8},{48,16},{56,24},{64,96... | collective-permute-start | bytes 405512 | tf_op jit(solution)/shard_map/ppermute | solution.py:29
  26.7 11.9 %collective-permute-start.1 = (bf16[176,384]{1,0:T(8,128)(2,1)S(1)}, bf16[176,384]{1,0:T(8,128)(2,1)S(1)}, u32[]{:S(2)}, u32[]{:S(2)}) collective-permute-start(bf16[176,384]{1,0:T(8,128)(2,1)S(1)} %shard_map.119), channel_id=1, source_target_pairs={{0,16},{8,24},{16,32},{24,40},{32,48},{40,56},{48,0},{56,8},{64,80... | collective-permute-start | bytes 405512 | tf_op jit(solution)/shard_map/ppermute | solution.py:29
  28.2 11.2 %collective-permute-start.2 = (bf16[176,384]{1,0:T(8,128)(2,1)S(1)}, bf16[176,384]{1,0:T(8,128)(2,1)S(1)}, u32[]{:S(2)}, u32[]{:S(2)}) collective-permute-start(bf16[176,384]{1,0:T(8,128)(2,1)S(1)} %shard_map.119), channel_id=1, source_target_pairs={{0,48},{8,56},{16,0},{24,8},{32,16},{40,24},{48,32},{56,40},{64,11... | collective-permute-start | bytes 405512 | tf_op jit(solution)/shard_map/ppermute | solution.py:29
  30.8 4.4 %collective-permute-start.4 = (bf16[96,384]{1,0:T(8,128)(2,1)S(1)}, bf16[96,384]{1,0:T(8,128)(2,1)S(1)}, u32[]{:S(2)}, u32[]{:S(2)}) collective-permute-start(bf16[96,384]{1,0:T(8,128)(2,1)S(1)} %shard_map.120.q_ref), channel_id=1, source_target_pairs={{0,64},{8,72},{16,80},{24,88},{32,96},{40,104},{48,112},{56,120},{... | collective-permute-start | bytes 221192 | tf_op jit(solution)/shard_map/ppermute | solution.py:29
  33.0 5.6 %collective-permute-start.5 = (bf16[96,384]{1,0:T(8,128)(2,1)S(1)}, bf16[96,384]{1,0:T(8,128)(2,1)S(1)}, u32[]{:S(2)}, u32[]{:S(2)}) collective-permute-start(bf16[96,384]{1,0:T(8,128)(2,1)S(1)} %shard_map.120.q_ref), channel_id=1, source_target_pairs={{0,192},{8,200},{16,208},{24,216},{32,224},{40,232},{48,240},{56,2... | collective-permute-start | bytes 221192 | tf_op jit(solution)/shard_map/ppermute | solution.py:29
  39.5 2.0 %collective-permute-start.6 = (bf16[4,176,384]{2,1,0:T(8,128)(2,1)S(1)}, bf16[4,176,384]{2,1,0:T(8,128)(2,1)S(1)}, u32[]{:S(2)}, u32[]{:S(2)}) collective-permute-start(bf16[4,176,384]{2,1,0:T(8,128)(2,1)S(1)} %pad_maximum_fusion.kv_ref.near_ref), channel_id=1, source_target_pairs={{0,8},{8,0},{16,24},{24,16},{32,40},{40,32},{48,56},{56,48},{64,72... | collective-permute-start | bytes 1622024 | tf_op jit(solution)/shard_map/ppermute | solution.py:29
  41.5 10.9 %copy-start.2 = (bf16[192,1536]{1,0:T(8,128)(2,1)S(1)}, bf16[192,1536]{1,0:T(8,128)(2,1)}, u32[]{:S(2)}) copy-start(bf16[192,1536]{1,0:T(8,128)(2,1)} %w_ref.5) | copy-start | bytes 1769476
  43.8 7.3 %collective-permute-start.7 = (bf16[176,256]{1,0:T(8,128)(2,1)S(1)}, bf16[176,256]{1,0:T(8,128)(2,1)S(1)}, u32[]{:S(2)}, u32[]{:S(2)}) collective-permute-start(bf16[176,256]{1,0:T(8,128)(2,1)S(1)} %get-tuple-element.32), channel_id=1, source_target_pairs={{0,128},{8,136},{16,144},{24,152},{32,160},{40,168},{48,176},{56,1... | collective-permute-start | bytes 270344 | tf_op jit(solution)/shard_map/ppermute | solution.py:29
  46.2 6.2 %collective-permute-start.8 = (bf16[176,256]{1,0:T(8,128)(2,1)S(1)}, bf16[176,256]{1,0:T(8,128)(2,1)S(1)}, u32[]{:S(2)}, u32[]{:S(2)}) collective-permute-start(bf16[176,256]{1,0:T(8,128)(2,1)S(1)} %get-tuple-element.33), channel_id=1, source_target_pairs={{0,192},{8,200},{16,208},{24,216},{32,224},{40,232},{48,240},{56,2... | collective-permute-start | bytes 270344 | tf_op jit(solution)/shard_map/ppermute | solution.py:29
  47.0 5.4 %collective-permute-start.9 = (bf16[176,256]{1,0:T(8,128)(2,1)S(1)}, bf16[176,256]{1,0:T(8,128)(2,1)S(1)}, u32[]{:S(2)}, u32[]{:S(2)}) collective-permute-start(bf16[176,256]{1,0:T(8,128)(2,1)S(1)} %get-tuple-element.34), channel_id=1, source_target_pairs={{0,64},{8,72},{16,80},{24,88},{32,96},{40,104},{48,112},{56,120},{... | collective-permute-start | bytes 270344 | tf_op jit(solution)/shard_map/ppermute | solution.py:29
  51.1 15.7 %copy-start.3 = (bf16[22,1536]{1,0:T(8,128)(2,1)S(1)}, bf16[22,1536]{1,0:T(8,128)(2,1)}, u32[]{:S(2)}) copy-start(bf16[22,1536]{1,0:T(8,128)(2,1)} %x_ref.1) | copy-start | bytes 202756
  51.1 15.7 %copy-start.4 = (f32[1536]{0:T(1024)S(1)}, f32[1536]{0:T(1024)}, u32[]{:S(2)}) copy-start(f32[1536]{0:T(1024)} %gain_ref.1) | copy-start | bytes 18436
  51.1 15.7 %copy-start.5 = (f32[1536]{0:T(1024)S(1)}, f32[1536]{0:T(1024)}, u32[]{:S(2)}) copy-start(f32[1536]{0:T(1024)} %shift_ref.1) | copy-start | bytes 18436
  66.8 4.8 %copy-start.6 = (f32[31,192]{1,0:T(8,128)S(1)}, f32[31,192]{1,0:T(8,128)}, u32[]{:S(2)}) copy-start(f32[31,192]{1,0:T(8,128)} %param.20) | copy-start | bytes 71428
  67.9 12.4 %copy-start.7 = (bf16[2,192,1536]{2,1,0:T(8,128)(2,1)S(1)}, bf16[2,192,1536]{2,1,0:T(8,128)(2,1)}, u32[]{:S(2)}) copy-start(bf16[2,192,1536]{2,1,0:T(8,128)(2,1)} %param.19) | copy-start | bytes 3538948
  67.9 12.2 %all-to-all-start.2 = ((bf16[8,24,1536]{2,1,0:T(8,128)(2,1)}), bf16[8,24,1536]{2,1,0:T(8,128)(2,1)S(1)}, u32[]{:S(2)}, u32[]{:S(2)}) async-start(bf16[8,24,1536]{2,1,0:T(8,128)(2,1)} %get-tuple-element.36), calls=%async_computation.2 | async-start | bytes 1179648 | tf_op jit(solution)/shard_map/all_to_all | solution.py:235
  80.7 8.4 %copy-start.8 = (f32[192]{0:T(256)S(1)}, f32[192]{0:T(256)}, u32[]{:S(2)}) copy-start(f32[192]{0:T(256)} %param.22) | copy-start | bytes 2308
  80.7 8.4 %copy-start.9 = (f32[192]{0:T(256)S(1)}, f32[192]{0:T(256)}, u32[]{:S(2)}) copy-start(f32[192]{0:T(256)} %param.21) | copy-start | bytes 2308
  81.1 8.0 %collective-permute-start.10 = (bf16[16,192]{1,0:T(8,128)(2,1)S(1)}, bf16[16,192]{1,0:T(8,128)(2,1)S(1)}, u32[]{:S(2)}, u32[]{:S(2)}) collective-permute-start(bf16[16,192]{1,0:T(8,128)(2,1)S(1)} %get-tuple-element.38), channel_id=1, source_target_pairs={{8,16},{24,32},{40,48},{56,64},{72,80},{88,96},{104,112},{120,128}... | collective-permute-start | bytes 18440 | tf_op jit(solution)/shard_map/ppermute | solution.py:314
  83.0 6.1 %collective-permute-start.11 = (bf16[16,192]{1,0:T(8,128)(2,1)S(1)}, bf16[16,192]{1,0:T(8,128)(2,1)S(1)}, u32[]{:S(2)}, u32[]{:S(2)}) collective-permute-start(bf16[16,192]{1,0:T(8,128)(2,1)S(1)} %get-tuple-element.37), channel_id=1, source_target_pairs={{0,8},{8,0},{16,24},{24,16},{32,40},{40,32},{48,56},{56,48},{64,72... | collective-permute-start | bytes 18440 | tf_op jit(solution)/shard_map/ppermute | solution.py:29

commit v5 on v4

--- a/solution.py
+++ b/solution.py
@@ -229,6 +229,59 @@
     normed = norm_rows(mid.astype(F32), gain_ref[...].reshape(1, D), shift_ref[...].reshape(1, D))
     for peer in range(PEERS):
         out_ref[peer, 0:ROWS, :] = normed
+
+
+def gate(x, w_ref):
+    return (dot_t(x, w_ref[0]) * jax.nn.sigmoid(dot_t(x, w_ref[1]))).astype(BF16)
+
+
+def edge_body(odd_ref, got_ref, w_ref, inner_ref, outer_ref):
+    tail = got_ref[PEERS - 1].astype(F32)[ROWS - 16 : ROWS].astype(BF16)
+    glu = gate(jnp.concatenate([got_ref[0][0:16], tail], axis=0), w_ref).astype(F32)
+    odd = odd_ref[0] == 1
+    inner_ref[...] = jnp.where(odd, glu[0:16], glu[16:32]).astype(BF16)
+    outer_ref[...] = jnp.where(odd, glu[16:32], glu[0:16]).astype(BF16)
+
+
+def inside_body(got_ref, w_ref, taps_ref, depth_ref, padded):
+    glu = gate(got_ref[...].reshape(PEERS * SLOT, D), w_ref).astype(F32)
+    padded[0:16, :] = jnp.zeros((16, WIDTH), F32)
+    padded[BLOCK + 16 : BLOCK + 32, :] = jnp.zeros((16, WIDTH), F32)
+    for peer in range(PEERS):
+        start = 16 + peer * ROWS
+        padded[start : start + ROWS, :] = glu[peer * SLOT : peer * SLOT + ROWS]
+    depth = jnp.zeros((BLOCK, WIDTH), F32)
+    for tap in range(TAPS):
+        depth += padded[tap + 1 : tap + 1 + BLOCK, :] * taps_ref[tap : tap + 1, :]
+    depth_ref[...] = depth
+
+
+def close_body(*refs):
+    odd_ref, depth_ref, inner_ref, outer_ref, taps_ref, scale_ref, offset_ref, w_ref = refs[:8]
+    out_ref, padded, spread = refs[8:]
+    odd = odd_ref[0] == 1
+    inner, outer = inner_ref[...].astype(F32), outer_ref[...].astype(F32)
+    empty = jnp.zeros((32, WIDTH), F32)
+    padded[0:16, :] = jnp.where(odd, inner, outer)
+    padded[16:48, :] = empty
+    padded[48:80, :] = empty
+    padded[80:96, :] = jnp.where(odd, outer, inner)
+    first = jnp.zeros((16, WIDTH), F32)
+    last = jnp.zeros((16, WIDTH), F32)
+    for tap in range(TAPS):
+        weight = taps_ref[tap : tap + 1, :]
+        first += padded[tap + 1 : tap + 17, :] * weight
+        last += padded[tap + 49 : tap + 65, :] * weight
+    depth = depth_ref[...]
+    depth = jnp.concatenate(
+        [depth[0:16] + first, depth[16 : BLOCK - 16], depth[BLOCK - 16 :] + last], axis=0
+    )
+    normed = depth * scale_ref[...].reshape(1, WIDTH) + offset_ref[...].reshape(1, WIDTH)
+    swish = normed * jax.nn.sigmoid(normed)
+    spread[...] = jnp.zeros_like(spread)
+    for peer in range(PEERS):
+        spread[peer * SLOT : peer * SLOT + ROWS, :] = swish[peer * ROWS : peer * ROWS + ROWS]
+    out_ref[...] = dot(spread[...].astype(BF16), w_ref[...]).astype(BF16).reshape(PEERS, SLOT, D)
 
 
 def exchange(array):
@@ -285,10 +338,11 @@
     pair = call(pair_body, shape((BLOCK, 384)), scratch)(attn_in, w_qkv, cosine, sine)
     attn_in, pair = lax.optimization_barrier((attn_in, pair))
     steps = (2, 1, -1)
-    near = [pair] + [hop(pair, along_z(step)) for step in steps]
+    near = [pair] + [hop(pair, along_z(step)) for step in (-1, 1, 2)]
     tight = pltpu.VMEM((BLOCK, 256), F32)
     queries = call(query_body, shape((96, 384)), [tight])(attn_in, w_qkv, cosine, sine)
-    q_got = [hop(queries, along_y(step)) for step in steps]
+    q_got = [hop(queries, along_y(step)) for step in (1, -1, 2)]
+    q_got = [q_got[2], q_got[0], q_got[1]]
     *near, q_got[0], q_got[1], q_got[2] = lax.optimization_barrier((*near, *q_got))
     near = jnp.stack(near)
     far = hop(near, other_core)
@@ -303,25 +357,23 @@
     mid, conv_in = call(middle_body, (shape((ROWS, D)), slots))(
         sums, frames_in, conv_gain, conv_shift
     )
-    conv_in = exchange(conv_in)[:, :ROWS].reshape(BLOCK, D)
-    value_half = dot_t(conv_in, w_pointwise_in[0])
-    gate_half = dot_t(conv_in, w_pointwise_in[1])
-    glu = (value_half * jax.nn.sigmoid(gate_half)).astype(BF16)
-    even = lax.axis_index("seq") % 2 == 0
-    head, tail = glu[:16], glu[-16:]
-    inner = hop(jnp.where(even, tail, head), other_core)
+    conv_in = exchange(conv_in)
+    odd = (lax.axis_index("seq") % 2).astype(jnp.int32).reshape(1)
+    scalar = pl.BlockSpec(memory_space=pltpu.SMEM)
+    ends = call(edge_body, (shape((16, WIDTH)),) * 2, specs=[scalar, VMEM, VMEM])
+    inner, outer = ends(odd, conv_in, w_pointwise_in)
     links = [(i, i + 1) for i in range(1, 31, 2)] + [(i + 1, i) for i in range(1, 31, 2)]
-    outer = lax.ppermute(jnp.where(even, head, tail), "seq", links)
-    ahead = jnp.where(even, outer, inner)[1:]
-    behind = jnp.where(even, inner, outer)[:REACH]
-    padded = jnp.concatenate([ahead, glu, behind], axis=0)
-    depth = jnp.zeros((BLOCK, WIDTH), F32)
-    for tap in range(TAPS):
-        depth = depth + padded[tap : tap + BLOCK].astype(F32) * depth_kernel[tap]
-    normed = depth * norm_scale + norm_offset
-    swish = (normed * jax.nn.sigmoid(normed)).astype(BF16)
-    partial = dot(swish, w_pointwise_out).astype(BF16).reshape(PEERS, ROWS, D)
-    conv = jnp.sum(exchange(partial).astype(F32), axis=0)
+    inner = hop(inner, other_core)
+    outer = lax.ppermute(outer, "seq", links)
+    padded = [pltpu.VMEM((BLOCK + 32, WIDTH), F32)]
+    depth = call(inside_body, shape((BLOCK, WIDTH), F32), padded)(
+        conv_in, w_pointwise_in, depth_kernel
+    )
+    room = [pltpu.VMEM((96, WIDTH), F32), pltpu.VMEM((PEERS * SLOT, WIDTH), F32)]
+    sums = call(close_body, slots, room, specs=[scalar] + [VMEM] * 7)(
+        odd, depth, inner, outer, depth_kernel, norm_scale, norm_offset, w_pointwise_out
+    )
+    conv = jnp.sum(exchange(sums).astype(F32), axis=0)[:ROWS]
     return (mid.astype(F32) + conv).astype(BF16)
 
 

time: 104 us -> 104 us (level)
  Pallas kernels: 10.9 us -> 13.1 us
  local copies, waits for them, and re-layouts: 2.4 us -> 0.45 us
  matrix products: 1.74 us -> 0 us
    ppermute x1, starting transfers between devices: 1.92 us -> 5.14 us  [local(): outer = lax.ppermute(outer, 'seq', links)]
    ppermute x11, starting transfers between devices: 21.2 us -> 18.2 us  [hop(): return lax.ppermute(array, 'seq', [(i, place(i)) for i in range(count)])]
    ppermute x1, waiting for transfers between devices: 4.53 us -> 1.73 us  [local(): outer = lax.ppermute(outer, 'seq', links)]
    all_to_all x2, waiting for transfers between devices: 15.4 us -> 18.2 us  [exchange(): return lax.all_to_all(array, 'mp', 0, 0, tiled=False)]
    pallas_call x8 -> x11, Pallas kernels: 10.9 us -> 13.1 us  [call(): pl.pallas_call(body, out_shape=outs, in_specs=specs or [VMEM] * len(args)...]
    dot_general x3 -> x0, matrix products: 1.74 us -> none  [the longest x1 1.06 us: dot(): return jnp.dot(a, b, preferred_element_type=F32)]
  transfers between devices with their start and end apart: 14 -> 14, of which waited for: 8 -> 9; matrix products, arithmetic and copies ran while one was open for 3% -> 1% of each run, Pallas kernels for 3% -> 4%
where the time goes in v5:
time: 104 us; the launch traced here: 103 us
  starting transfers between devices  32.6 us (31%)
  waiting for transfers between devices  28.6 us (28%)
  blocking collectives  26.3 us (25%)
  Pallas kernels  13.1 us (13%)
  other arithmetic  1.27 us (1%)
    all_to_all x2, blocking collectives, exchange(): return lax.all_to_all(array, 'mp', 0, 0, tiled=False)  26.3 us
    ppermute x11, starting transfers between devices, hop(): return lax.ppermute(array, 'seq', [(i, place(i)) for i in range(count)])  18.2 us
    all_to_all x2, waiting for transfers between devices, exchange(): return lax.all_to_all(array, 'mp', 0, 0, tiled=False)  18.2 us
    pallas_call x11, Pallas kernels, call(): pl.pallas_call(body, out_shape=outs, in_specs=specs or [VMEM] * len(args)...  13.1 us
    all_to_all x2, starting transfers between devices, exchange(): return lax.all_to_all(array, 'mp', 0, 0, tiled=False)  9.2 us
    ppermute x11, waiting for transfers between devices, hop(): return lax.ppermute(array, 'seq', [(i, place(i)) for i in range(count)])  8.69 us
    ppermute x1, starting transfers between devices, local(): outer = lax.ppermute(outer, 'seq', links)  5.14 us
  transfers between devices with their start and end apart: 14, of which 9 were waited for; matrix products, arithmetic and copies ran while one was open for 1% of the time, Pallas kernels for 4%

profile of v5, /device:TPU:24, one launch (start us, length us, event | category | flops | bytes accessed | tf_op | source)
XLA Modules:
  0.0 102.6 jit_solution(615827918838958951)
XLA Ops:
  0.0 2.0 %shard_map.118 = bf16[8,24,1536]{2,1,0:T(8,128)(2,1)} custom-call(bf16[22,1536]{1,0:T(8,128)(2,1)} %x_ref.1, f32[1536]{0:T(1024)} %gain_any.1, f32[1536]{0:T(1024)} %shift_any.1), custom_call_target="tpu_custom_call" | custom-call | flops 1000000 | bytes 1000000 | tf_op jit(solution)/shard_map/pallas_call | solution.py:46
  2.0 5.7 %all-to-all-start = ((bf16[8,24,1536]{2,1,0:T(8,128)(2,1)}), bf16[8,24,1536]{2,1,0:T(8,128)(2,1)S(1)}, u32[]{:S(2)}, u32[]{:S(2)}) async-start(bf16[8,24,1536]{2,1,0:T(8,128)(2,1)} %shard_map.118), calls=%async_computation | async-start | bytes 1179648 | tf_op jit(solution)/shard_map/all_to_all | solution.py:288
  7.7 0.4 multiply_sine_fusion
  8.1 0.2 concatenate.6.cos_ref
  8.4 0.2 concatenate.7.sin_ref
  8.6 9.1 %all-to-all-done.x_ref = bf16[8,24,1536]{2,1,0:T(8,128)(2,1)S(1)} async-done(((bf16[8,24,1536]{2,1,0:T(8,128)(2,1)}), bf16[8,24,1536]{2,1,0:T(8,128)(2,1)S(1)}, u32[]{:S(2)}, u32[]{:S(2)}) %all-to-all-start) | async-done | bytes 589856 | tf_op jit(solution)/shard_map/all_to_all | solution.py:288
  17.7 0.8 shard_map.119
  18.5 0.6 shard_map.120.q_ref
  19.0 0.8 collective-permute-start.5
  19.9 6.3 %collective-permute-start.2 = (bf16[176,384]{1,0:T(8,128)(2,1)S(1)}, bf16[176,384]{1,0:T(8,128)(2,1)S(1)}, u32[]{:S(2)}, u32[]{:S(2)}) collective-permute-start(bf16[176,384]{1,0:T(8,128)(2,1)S(1)} %shard_map.119), channel_id=1, source_target_pairs={{0,32},{8,40},{16,48},{24,56},{32,0},{40,8},{48,16},{56,24},{64,96... | collective-permute-start | bytes 405512 | tf_op jit(solution)/shard_map/ppermute | solution.py:29
  26.2 1.5 %collective-permute-start.1 = (bf16[176,384]{1,0:T(8,128)(2,1)S(1)}, bf16[176,384]{1,0:T(8,128)(2,1)S(1)}, u32[]{:S(2)}, u32[]{:S(2)}) collective-permute-start(bf16[176,384]{1,0:T(8,128)(2,1)S(1)} %shard_map.119), channel_id=1, source_target_pairs={{0,16},{8,24},{16,32},{24,40},{32,48},{40,56},{48,0},{56,8},{64,80... | collective-permute-start | bytes 405512 | tf_op jit(solution)/shard_map/ppermute | solution.py:29
  27.6 2.7 %collective-permute-start = (bf16[176,384]{1,0:T(8,128)(2,1)S(1)}, bf16[176,384]{1,0:T(8,128)(2,1)S(1)}, u32[]{:S(2)}, u32[]{:S(2)}) collective-permute-start(bf16[176,384]{1,0:T(8,128)(2,1)S(1)} %shard_map.119), channel_id=1, source_target_pairs={{0,48},{8,56},{16,0},{24,8},{32,16},{40,24},{48,32},{56,40},{64,11... | collective-permute-start | bytes 405512 | tf_op jit(solution)/shard_map/ppermute | solution.py:29
  30.3 2.5 %collective-permute-start.4 = (bf16[96,384]{1,0:T(8,128)(2,1)S(1)}, bf16[96,384]{1,0:T(8,128)(2,1)S(1)}, u32[]{:S(2)}, u32[]{:S(2)}) collective-permute-start(bf16[96,384]{1,0:T(8,128)(2,1)S(1)} %shard_map.120.q_ref), channel_id=1, source_target_pairs={{0,64},{8,72},{16,80},{24,88},{32,96},{40,104},{48,112},{56,120},{... | collective-permute-start | bytes 221192 | tf_op jit(solution)/shard_map/ppermute | solution.py:29
  32.8 0.0 collective-permute-start.3
  32.8 2.7 %collective-permute-done.4.b_ref = bf16[96,384]{1,0:T(8,128)(2,1)S(1)} collective-permute-done((bf16[96,384]{1,0:T(8,128)(2,1)S(1)}, bf16[96,384]{1,0:T(8,128)(2,1)S(1)}, u32[]{:S(2)}, u32[]{:S(2)}) %collective-permute-start.4) | collective-permute-done | bytes 73760 | tf_op jit(solution)/shard_map/ppermute | solution.py:29
  35.5 3.2 %collective-permute-done.3.a_ref = bf16[96,384]{1,0:T(8,128)(2,1)S(1)} collective-permute-done((bf16[96,384]{1,0:T(8,128)(2,1)S(1)}, bf16[96,384]{1,0:T(8,128)(2,1)S(1)}, u32[]{:S(2)}, u32[]{:S(2)}) %collective-permute-start.3) | collective-permute-done | bytes 73760 | tf_op jit(solution)/shard_map/ppermute | solution.py:29
  38.7 0.2 collective-permute-done
  38.8 0.1 pad_maximum_fusion.kv_ref.near_ref
  38.9 0.1 collective-permute-start.6
  39.0 1.7 %shard_map.121 = (f32[528,256]{1,0:T(8,128)S(1)}, f32[528,128]{1,0:T(8,128)S(1)}) custom-call(bf16[96,384]{1,0:T(8,128)(2,1)S(1)} %collective-permute-done.3.a_ref, bf16[96,384]{1,0:T(8,128)(2,1)S(1)} %collective-permute-done.4.b_ref, bf16[96,384]{1,0:T(8,128)(2,1)S(1)} %collective-permute-done.5.c_ref, bf16[4,176,384]{2,1,0:T(8,128)(2,1)S(1)} %pad_maximum_fusion.kv_ref.near_ref), custom_call_target="tpu_custom_call" | custom-call | flops 1000000 | bytes 1000000 | tf_op jit(solution)/shard_map/pallas_call | solution.py:46
  40.7 0.2 collective-permute-done.6.kv_ref.far_ref
  41.0 2.3 %shard_map.122 = (bf16[176,256]{1,0:T(8,128)(2,1)S(1)}, bf16[176,256]{1,0:T(8,128)(2,1)S(1)}, bf16[176,256]{1,0:T(8,128)(2,1)S(1)}) custom-call(bf16[96,384]{1,0:T(8,128)(2,1)S(1)} %collective-permute-done.3.a_ref, bf16[96,384]{1,0:T(8,128)(2,1)S(1)} %collective-permute-done.4.b_ref, bf16[96,384]{1,0:T(8,128)(2,1)S(1)} %collective-permute-done.5.c_ref, ...), custom_call_target="tpu_custom_call" | custom-call | flops 1000000 | bytes 1000000 | tf_op jit(solution)/shard_map/pallas_call | solution.py:46
  43.3 1.0 %collective-permute-start.7 = (bf16[176,256]{1,0:T(8,128)(2,1)S(1)}, bf16[176,256]{1,0:T(8,128)(2,1)S(1)}, u32[]{:S(2)}, u32[]{:S(2)}) collective-permute-start(bf16[176,256]{1,0:T(8,128)(2,1)S(1)} %get-tuple-element.34), channel_id=1, source_target_pairs={{0,128},{8,136},{16,144},{24,152},{32,160},{40,168},{48,176},{56,1... | collective-permute-start | bytes 270344 | tf_op jit(solution)/shard_map/ppermute | solution.py:29
  44.3 2.4 %collective-permute-start.8 = (bf16[176,256]{1,0:T(8,128)(2,1)S(1)}, bf16[176,256]{1,0:T(8,128)(2,1)S(1)}, u32[]{:S(2)}, u32[]{:S(2)}) collective-permute-start(bf16[176,256]{1,0:T(8,128)(2,1)S(1)} %get-tuple-element.35), channel_id=1, source_target_pairs={{0,192},{8,200},{16,208},{24,216},{32,224},{40,232},{48,240},{56,2... | collective-permute-start | bytes 270344 | tf_op jit(solution)/shard_map/ppermute | solution.py:29
  46.7 0.8 collective-permute-start.9
  47.6 1.6 %shard_map.123.d_ref = bf16[176,256]{1,0:T(8,128)(2,1)S(1)} custom-call(bf16[96,384]{1,0:T(8,128)(2,1)S(1)} %shard_map.120.q_ref, bf16[4,176,384]{2,1,0:T(8,128)(2,1)S(1)} %pad_maximum_fusion.kv_ref.near_ref, bf16[4,176,384]{2,1,0:T(8,128)(2,1)S(1)} %collective-permute-done.6.kv_ref.far_ref), custom_call_target="tpu_custom_call" | custom-call | flops 1000000 | bytes 1000000 | tf_op jit(solution)/shard_map/pallas_call | solution.py:46
  49.2 0.0 copy-start.4
  49.2 0.0 copy-start.6
  49.2 0.0 copy-start.7
  49.2 1.1 %collective-permute-done.7.a_ref = bf16[176,256]{1,0:T(8,128)(2,1)S(1)} collective-permute-done((bf16[176,256]{1,0:T(8,128)(2,1)S(1)}, bf16[176,256]{1,0:T(8,128)(2,1)S(1)}, u32[]{:S(2)}, u32[]{:S(2)}) %collective-permute-start.7) | collective-permute-done | bytes 90144 | tf_op jit(solution)/shard_map/ppermute | solution.py:29
  50.3 1.3 %collective-permute-done.8.b_ref = bf16[176,256]{1,0:T(8,128)(2,1)S(1)} collective-permute-done((bf16[176,256]{1,0:T(8,128)(2,1)S(1)}, bf16[176,256]{1,0:T(8,128)(2,1)S(1)}, u32[]{:S(2)}, u32[]{:S(2)}) %collective-permute-start.8) | collective-permute-done | bytes 90144 | tf_op jit(solution)/shard_map/ppermute | solution.py:29
  51.6 0.8 shard_map.124
  52.5 14.0 %all_to_all.20.got_ref = bf16[8,24,1536]{2,1,0:T(8,128)(2,1)S(1)} all-to-all(bf16[8,24,1536]{2,1,0:T(8,128)(2,1)S(1)} %shard_map.124), channel_id=1, replica_groups=mesh['seq'=32,'mp'=8] {'mp'}, dimensions={0} | all-to-all | bytes 1179648 | tf_op jit(solution)/shard_map/all_to_all | solution.py:288
  66.5 0.0 copy-start.1
  66.5 1.2 %shard_map.125 = (bf16[22,1536]{1,0:T(8,128)(2,1)S(1)}, bf16[8,24,1536]{2,1,0:T(8,128)(2,1)}) custom-call(bf16[8,24,1536]{2,1,0:T(8,128)(2,1)S(1)} %all_to_all.20.got_ref, bf16[22,1536]{1,0:T(8,128)(2,1)S(1)} %copy-done.4, f32[1536]{0:T(1024)S(1)} %copy-done.6, f32[1536]{0:T(1024)S(1)} %copy-done.7), custom_call_target="tpu_custom_call" | custom-call | flops 1000000 | bytes 1000000 | tf_op jit(solution)/shard_map/pallas_call | solution.py:46
  67.7 3.5 %all-to-all-start.2 = ((bf16[8,24,1536]{2,1,0:T(8,128)(2,1)}), bf16[8,24,1536]{2,1,0:T(8,128)(2,1)S(1)}, u32[]{:S(2)}, u32[]{:S(2)}) async-start(bf16[8,24,1536]{2,1,0:T(8,128)(2,1)} %get-tuple-element.38), calls=%async_computation.2 | async-start | bytes 1179648 | tf_op jit(solution)/shard_map/all_to_all | solution.py:288
  71.2 0.0 copy-start.5
  71.3 9.0 %all-to-all-done.2.got_ref = bf16[8,24,1536]{2,1,0:T(8,128)(2,1)S(1)} async-done(((bf16[8,24,1536]{2,1,0:T(8,128)(2,1)}), bf16[8,24,1536]{2,1,0:T(8,128)(2,1)S(1)}, u32[]{:S(2)}, u32[]{:S(2)}) %all-to-all-start.2) | async-done | bytes 589856 | tf_op jit(solution)/shard_map/all_to_all | solution.py:288
  80.3 0.5 shard_map.127
  80.8 0.0 copy-start.9
  80.8 0.1 collective-permute-start.10
  80.9 5.1 %collective-permute-start.11 = (bf16[16,192]{1,0:T(8,128)(2,1)S(1)}, bf16[16,192]{1,0:T(8,128)(2,1)S(1)}, u32[]{:S(2)}, u32[]{:S(2)}) collective-permute-start(bf16[16,192]{1,0:T(8,128)(2,1)S(1)} %get-tuple-element.40), channel_id=1, source_target_pairs={{8,16},{24,32},{40,48},{56,64},{72,80},{88,96},{104,112},{120,128}... | collective-permute-start | bytes 18440 | tf_op jit(solution)/shard_map/ppermute | solution.py:367
  86.1 1.2 %shard_map.126.refs_1_ = f32[176,192]{1,0:T(8,128)S(1)} custom-call(bf16[8,24,1536]{2,1,0:T(8,128)(2,1)S(1)} %all-to-all-done.2.got_ref, bf16[2,192,1536]{2,1,0:T(8,128)(2,1)S(1)} %copy-done.1, f32[31,192]{1,0:T(8,128)S(1)} %copy-done.5), custom_call_target="tpu_custom_call" | custom-call | flops 1000000 | bytes 1000000 | tf_op jit(solution)/shard_map/pallas_call | solution.py:46
  87.3 1.7 %collective-permute-done.11.refs_3_ = bf16[16,192]{1,0:T(8,128)(2,1)S(1)} collective-permute-done((bf16[16,192]{1,0:T(8,128)(2,1)S(1)}, bf16[16,192]{1,0:T(8,128)(2,1)S(1)}, u32[]{:S(2)}, u32[]{:S(2)}) %collective-permute-start.11) | collective-permute-done | bytes 6176 | tf_op jit(solution)/shard_map/ppermute | solution.py:367
  89.1 0.5 shard_map.128
  89.6 12.3 %all_to_all.21 = bf16[8,24,1536]{2,1,0:T(8,128)(2,1)S(1)} all-to-all(bf16[8,24,1536]{2,1,0:T(8,128)(2,1)S(1)} %shard_map.128), channel_id=1, replica_groups=mesh['seq'=32,'mp'=8] {'mp'}, dimensions={0} | all-to-all | bytes 1179648 | tf_op jit(solution)/shard_map/all_to_all | solution.py:288
  101.9 0.1 convert_reduce_fusion
  102.0 0.7 fusion
  (23 shorter events, 0.1 us)
Async XLA Ops:
  2.0 15.7 %all-to-all-start = ((bf16[8,24,1536]{2,1,0:T(8,128)(2,1)}), bf16[8,24,1536]{2,1,0:T(8,128)(2,1)S(1)}, u32[]{:S(2)}, u32[]{:S(2)}) async-start(bf16[8,24,1536]{2,1,0:T(8,128)(2,1)} %shard_map.118), calls=%async_computation | async-start | bytes 1179648 | tf_op jit(solution)/shard_map/all_to_all | solution.py:288
  7.7 10.0 %copy-start = (bf16[3,192,1536]{2,1,0:T(8,128)(2,1)S(1)}, bf16[3,192,1536]{2,1,0:T(8,128)(2,1)}, u32[]{:S(2)}) copy-start(bf16[3,192,1536]{2,1,0:T(8,128)(2,1)} %w_ref.6) | copy-start | bytes 5308420
  19.0 13.7 %collective-permute-start.5 = (bf16[96,384]{1,0:T(8,128)(2,1)S(1)}, bf16[96,384]{1,0:T(8,128)(2,1)S(1)}, u32[]{:S(2)}, u32[]{:S(2)}) collective-permute-start(bf16[96,384]{1,0:T(8,128)(2,1)S(1)} %shard_map.120.q_ref), channel_id=1, source_target_pairs={{0,192},{8,200},{16,208},{24,216},{32,224},{40,232},{48,240},{56,2... | collective-permute-start | bytes 221192 | tf_op jit(solution)/shard_map/ppermute | solution.py:29
  19.9 18.8 %collective-permute-start.2 = (bf16[176,384]{1,0:T(8,128)(2,1)S(1)}, bf16[176,384]{1,0:T(8,128)(2,1)S(1)}, u32[]{:S(2)}, u32[]{:S(2)}) collective-permute-start(bf16[176,384]{1,0:T(8,128)(2,1)S(1)} %shard_map.119), channel_id=1, source_target_pairs={{0,32},{8,40},{16,48},{24,56},{32,0},{40,8},{48,16},{56,24},{64,96... | collective-permute-start | bytes 405512 | tf_op jit(solution)/shard_map/ppermute | solution.py:29
  26.2 12.5 %collective-permute-start.1 = (bf16[176,384]{1,0:T(8,128)(2,1)S(1)}, bf16[176,384]{1,0:T(8,128)(2,1)S(1)}, u32[]{:S(2)}, u32[]{:S(2)}) collective-permute-start(bf16[176,384]{1,0:T(8,128)(2,1)S(1)} %shard_map.119), channel_id=1, source_target_pairs={{0,16},{8,24},{16,32},{24,40},{32,48},{40,56},{48,0},{56,8},{64,80... | collective-permute-start | bytes 405512 | tf_op jit(solution)/shard_map/ppermute | solution.py:29
  27.6 11.2 %collective-permute-start = (bf16[176,384]{1,0:T(8,128)(2,1)S(1)}, bf16[176,384]{1,0:T(8,128)(2,1)S(1)}, u32[]{:S(2)}, u32[]{:S(2)}) collective-permute-start(bf16[176,384]{1,0:T(8,128)(2,1)S(1)} %shard_map.119), channel_id=1, source_target_pairs={{0,48},{8,56},{16,0},{24,8},{32,16},{40,24},{48,32},{56,40},{64,11... | collective-permute-start | bytes 405512 | tf_op jit(solution)/shard_map/ppermute | solution.py:29
  30.3 5.2 %collective-permute-start.4 = (bf16[96,384]{1,0:T(8,128)(2,1)S(1)}, bf16[96,384]{1,0:T(8,128)(2,1)S(1)}, u32[]{:S(2)}, u32[]{:S(2)}) collective-permute-start(bf16[96,384]{1,0:T(8,128)(2,1)S(1)} %shard_map.120.q_ref), channel_id=1, source_target_pairs={{0,64},{8,72},{16,80},{24,88},{32,96},{40,104},{48,112},{56,120},{... | collective-permute-start | bytes 221192 | tf_op jit(solution)/shard_map/ppermute | solution.py:29
  32.8 5.9 %collective-permute-start.3 = (bf16[96,384]{1,0:T(8,128)(2,1)S(1)}, bf16[96,384]{1,0:T(8,128)(2,1)S(1)}, u32[]{:S(2)}, u32[]{:S(2)}) collective-permute-start(bf16[96,384]{1,0:T(8,128)(2,1)S(1)} %shard_map.120.q_ref), channel_id=1, source_target_pairs={{0,128},{8,136},{16,144},{24,152},{32,160},{40,168},{48,176},{56,1... | collective-permute-start | bytes 221192 | tf_op jit(solution)/shard_map/ppermute | solution.py:29
  38.9 2.0 %collective-permute-start.6 = (bf16[4,176,384]{2,1,0:T(8,128)(2,1)S(1)}, bf16[4,176,384]{2,1,0:T(8,128)(2,1)S(1)}, u32[]{:S(2)}, u32[]{:S(2)}) collective-permute-start(bf16[4,176,384]{2,1,0:T(8,128)(2,1)S(1)} %pad_maximum_fusion.kv_ref.near_ref), channel_id=1, source_target_pairs={{0,8},{8,0},{16,24},{24,16},{32,40},{40,32},{48,56},{56,48},{64,72... | collective-permute-start | bytes 1622024 | tf_op jit(solution)/shard_map/ppermute | solution.py:29
  41.0 10.7 %copy-start.2 = (bf16[192,1536]{1,0:T(8,128)(2,1)S(1)}, bf16[192,1536]{1,0:T(8,128)(2,1)}, u32[]{:S(2)}) copy-start(bf16[192,1536]{1,0:T(8,128)(2,1)} %w_ref.7) | copy-start | bytes 1769476
  43.3 7.0 %collective-permute-start.7 = (bf16[176,256]{1,0:T(8,128)(2,1)S(1)}, bf16[176,256]{1,0:T(8,128)(2,1)S(1)}, u32[]{:S(2)}, u32[]{:S(2)}) collective-permute-start(bf16[176,256]{1,0:T(8,128)(2,1)S(1)} %get-tuple-element.34), channel_id=1, source_target_pairs={{0,128},{8,136},{16,144},{24,152},{32,160},{40,168},{48,176},{56,1... | collective-permute-start | bytes 270344 | tf_op jit(solution)/shard_map/ppermute | solution.py:29
  44.3 7.3 %collective-permute-start.8 = (bf16[176,256]{1,0:T(8,128)(2,1)S(1)}, bf16[176,256]{1,0:T(8,128)(2,1)S(1)}, u32[]{:S(2)}, u32[]{:S(2)}) collective-permute-start(bf16[176,256]{1,0:T(8,128)(2,1)S(1)} %get-tuple-element.35), channel_id=1, source_target_pairs={{0,192},{8,200},{16,208},{24,216},{32,224},{40,232},{48,240},{56,2... | collective-permute-start | bytes 270344 | tf_op jit(solution)/shard_map/ppermute | solution.py:29
  46.7 4.9 %collective-permute-start.9 = (bf16[176,256]{1,0:T(8,128)(2,1)S(1)}, bf16[176,256]{1,0:T(8,128)(2,1)S(1)}, u32[]{:S(2)}, u32[]{:S(2)}) collective-permute-start(bf16[176,256]{1,0:T(8,128)(2,1)S(1)} %get-tuple-element.36), channel_id=1, source_target_pairs={{0,64},{8,72},{16,80},{24,88},{32,96},{40,104},{48,112},{56,120},{... | collective-permute-start | bytes 270344 | tf_op jit(solution)/shard_map/ppermute | solution.py:29
  49.2 17.3 %copy-start.4 = (bf16[22,1536]{1,0:T(8,128)(2,1)S(1)}, bf16[22,1536]{1,0:T(8,128)(2,1)}, u32[]{:S(2)}) copy-start(bf16[22,1536]{1,0:T(8,128)(2,1)} %x_ref.1) | copy-start | bytes 202756
  49.2 17.3 %copy-start.6 = (f32[1536]{0:T(1024)S(1)}, f32[1536]{0:T(1024)}, u32[]{:S(2)}) copy-start(f32[1536]{0:T(1024)} %gain_ref.1) | copy-start | bytes 18436
  49.2 17.3 %copy-start.7 = (f32[1536]{0:T(1024)S(1)}, f32[1536]{0:T(1024)}, u32[]{:S(2)}) copy-start(f32[1536]{0:T(1024)} %shift_ref.1) | copy-start | bytes 18436
  66.5 13.8 %copy-start.1 = (bf16[2,192,1536]{2,1,0:T(8,128)(2,1)S(1)}, bf16[2,192,1536]{2,1,0:T(8,128)(2,1)}, u32[]{:S(2)}) copy-start(bf16[2,192,1536]{2,1,0:T(8,128)(2,1)} %w_ref.9) | copy-start | bytes 3538948
  67.7 12.6 %all-to-all-start.2 = ((bf16[8,24,1536]{2,1,0:T(8,128)(2,1)}), bf16[8,24,1536]{2,1,0:T(8,128)(2,1)S(1)}, u32[]{:S(2)}, u32[]{:S(2)}) async-start(bf16[8,24,1536]{2,1,0:T(8,128)(2,1)} %get-tuple-element.38), calls=%async_computation.2 | async-start | bytes 1179648 | tf_op jit(solution)/shard_map/all_to_all | solution.py:288
  71.2 14.8 %copy-start.5 = (f32[31,192]{1,0:T(8,128)S(1)}, f32[31,192]{1,0:T(8,128)}, u32[]{:S(2)}) copy-start(f32[31,192]{1,0:T(8,128)} %refs_4_.1) | copy-start | bytes 71428
  80.8 8.3 %copy-start.3 = (bf16[192,1536]{1,0:T(8,128)(2,1)S(1)}, bf16[192,1536]{1,0:T(8,128)(2,1)}, u32[]{:S(2)}) copy-start(bf16[192,1536]{1,0:T(8,128)(2,1)} %refs_7_.1) | copy-start | bytes 1769476
  80.8 8.3 %copy-start.8 = (f32[192]{0:T(256)S(1)}, f32[192]{0:T(256)}, u32[]{:S(2)}) copy-start(f32[192]{0:T(256)} %refs_5_.1) | copy-start | bytes 2308
  80.8 8.2 %copy-start.9 = (f32[192]{0:T(256)S(1)}, f32[192]{0:T(256)}, u32[]{:S(2)}) copy-start(f32[192]{0:T(256)} %refs_6_.1) | copy-start | bytes 2308
  80.8 6.5 %collective-permute-start.10 = (bf16[16,192]{1,0:T(8,128)(2,1)S(1)}, bf16[16,192]{1,0:T(8,128)(2,1)S(1)}, u32[]{:S(2)}, u32[]{:S(2)}) collective-permute-start(bf16[16,192]{1,0:T(8,128)(2,1)S(1)} %get-tuple-element.39), channel_id=1, source_target_pairs={{0,8},{8,0},{16,24},{24,16},{32,40},{40,32},{48,56},{56,48},{64,72... | collective-permute-start | bytes 18440 | tf_op jit(solution)/shard_map/ppermute | solution.py:29
  80.9 8.1 %collective-permute-start.11 = (bf16[16,192]{1,0:T(8,128)(2,1)S(1)}, bf16[16,192]{1,0:T(8,128)(2,1)S(1)}, u32[]{:S(2)}, u32[]{:S(2)}) collective-permute-start(bf16[16,192]{1,0:T(8,128)(2,1)S(1)} %get-tuple-element.40), channel_id=1, source_target_pairs={{8,16},{24,32},{40,48},{56,64},{72,80},{88,96},{104,112},{120,128}... | collective-permute-start | bytes 18440 | tf_op jit(solution)/shard_map/ppermute | solution.py:367

commit v6 on v4

--- a/solution.py
+++ b/solution.py
@@ -285,10 +285,11 @@
     pair = call(pair_body, shape((BLOCK, 384)), scratch)(attn_in, w_qkv, cosine, sine)
     attn_in, pair = lax.optimization_barrier((attn_in, pair))
     steps = (2, 1, -1)
-    near = [pair] + [hop(pair, along_z(step)) for step in steps]
+    near = [pair] + [hop(pair, along_z(step)) for step in (-1, 1, 2)]
     tight = pltpu.VMEM((BLOCK, 256), F32)
     queries = call(query_body, shape((96, 384)), [tight])(attn_in, w_qkv, cosine, sine)
-    q_got = [hop(queries, along_y(step)) for step in steps]
+    q_got = [hop(queries, along_y(step)) for step in (1, -1, 2)]
+    q_got = [q_got[2], q_got[0], q_got[1]]
     *near, q_got[0], q_got[1], q_got[2] = lax.optimization_barrier((*near, *q_got))
     near = jnp.stack(near)
     far = hop(near, other_core)

time: 104 us -> 105 us (level)
  waiting for transfers between devices: 27.8 us -> 26 us
  blocking collectives: 25.7 us -> 27.3 us
    ppermute x1, waiting for transfers between devices: 4.53 us -> 2.78 us  [local(): outer = lax.ppermute(jnp.where(even, head, tail), 'seq', links)]
    all_to_all x2, blocking collectives: 25.7 us -> 27.3 us  [exchange(): return lax.all_to_all(array, 'mp', 0, 0, tiled=False)]
  transfers between devices with their start and end apart: 14 -> 14, of which waited for: 8 -> 9; matrix products, arithmetic and copies ran while one was open for 3% -> 3% of each run, Pallas kernels for 3% -> 3%
where the time goes in v6:
time: 105 us; the launch traced here: 104 us
  starting transfers between devices  32.9 us (31%)
  blocking collectives  27.3 us (26%)
  waiting for transfers between devices  26 us (25%)
  Pallas kernels  10.9 us (10%)
  local copies, waits for them, and re-layouts  2.4 us (2%)
  other arithmetic  1.94 us (2%)
  matrix products  1.74 us (2%)
    all_to_all x2, blocking collectives, exchange(): return lax.all_to_all(array, 'mp', 0, 0, tiled=False)  27.3 us
    ppermute x11, starting transfers between devices, hop(): return lax.ppermute(array, 'seq', [(i, place(i)) for i in range(count)])  21.7 us
    all_to_all x2, waiting for transfers between devices, exchange(): return lax.all_to_all(array, 'mp', 0, 0, tiled=False)  15.4 us
    pallas_call x8, Pallas kernels, call(): pl.pallas_call(body, out_shape=outs, in_specs=specs or [VMEM] * len(args)...  10.9 us
    all_to_all x2, starting transfers between devices, exchange(): return lax.all_to_all(array, 'mp', 0, 0, tiled=False)  9.33 us
    ppermute x11, waiting for transfers between devices, hop(): return lax.ppermute(array, 'seq', [(i, place(i)) for i in range(count)])  7.76 us
    ppermute x1, waiting for transfers between devices, local(): outer = lax.ppermute(jnp.where(even, head, tail), 'seq', links)  2.78 us
  transfers between devices with their start and end apart: 14, of which 9 were waited for; matrix products, arithmetic and copies ran while one was open for 3% of the time, Pallas kernels for 3%

profile of v6, /device:TPU:24, one launch (start us, length us, event | category | flops | bytes accessed | tf_op | source)
XLA Modules:
  0.0 103.5 jit_solution(10520856733027329134)
XLA Ops:
  0.0 2.0 %shard_map.118 = bf16[8,24,1536]{2,1,0:T(8,128)(2,1)} custom-call(bf16[22,1536]{1,0:T(8,128)(2,1)} %x_ref.1, f32[1536]{0:T(1024)} %gain_any.1, f32[1536]{0:T(1024)} %shift_any.1), custom_call_target="tpu_custom_call" | custom-call | flops 1000000 | bytes 1000000 | tf_op jit(solution)/shard_map/pallas_call | solution.py:46
  2.0 5.7 %all-to-all-start = ((bf16[8,24,1536]{2,1,0:T(8,128)(2,1)}), bf16[8,24,1536]{2,1,0:T(8,128)(2,1)S(1)}, u32[]{:S(2)}, u32[]{:S(2)}) async-start(bf16[8,24,1536]{2,1,0:T(8,128)(2,1)} %shard_map.118), calls=%async_computation | async-start | bytes 1179648 | tf_op jit(solution)/shard_map/all_to_all | solution.py:235
  7.7 1.1 %multiply_sine_fusion = (f32[192,48]{1,0:T(8,128)S(1)}, f32[192,48]{1,0:T(8,128)}, f32[192,48]{1,0:T(8,128)S(1)}) fusion(f32[48]{0:T(128)S(1)} %multiply_power_fusion, f32[192]{0:T(256)S(1)} %fusion.40), kind=kLoop, calls=%fused_computation.43 | loop fusion | flops 18432 | bytes 111552 | tf_op jit(solution)/shard_map/sin | solution.py:247
  8.8 0.2 concatenate.41.cos_ref
  9.0 0.6 broadcast_in_dim.5
  9.6 1.2 %concatenate.42.sin_ref = f32[192,256]{1,0:T(8,128)S(1)} concatenate(f32[192,48]{1,0:T(8,128)} %get-tuple-element.73, f32[192,48]{1,0:T(8,128)S(1)} %get-tuple-element.72, f32[192,48]{1,0:T(8,128)} %get-tuple-element.73, f32[192,48]{1,0:T(8,128)S(1)} %get-tuple-element.72, f32[192,64]{1,0:T(8,128)} %broadcast_in_dim.5), dimensions={1} | concatenate | bytes 393216 | tf_op jit(solution)/shard_map/concatenate | solution.py:250
  10.8 6.9 %all-to-all-done.x_ref = bf16[8,24,1536]{2,1,0:T(8,128)(2,1)S(1)} async-done(((bf16[8,24,1536]{2,1,0:T(8,128)(2,1)}), bf16[8,24,1536]{2,1,0:T(8,128)(2,1)S(1)}, u32[]{:S(2)}, u32[]{:S(2)}) %all-to-all-start) | async-done | bytes 589856 | tf_op jit(solution)/shard_map/all_to_all | solution.py:235
  17.7 0.8 shard_map.119
  18.5 0.6 shard_map.120.q_ref
  19.1 1.3 %collective-permute-start.3 = (bf16[96,384]{1,0:T(8,128)(2,1)S(1)}, bf16[96,384]{1,0:T(8,128)(2,1)S(1)}, u32[]{:S(2)}, u32[]{:S(2)}) collective-permute-start(bf16[96,384]{1,0:T(8,128)(2,1)S(1)} %shard_map.120.q_ref), channel_id=1, source_target_pairs={{0,128},{8,136},{16,144},{24,152},{32,160},{40,168},{48,176},{56,1... | collective-permute-start | bytes 221192 | tf_op jit(solution)/shard_map/ppermute | solution.py:29
  20.4 5.4 %collective-permute-start = (bf16[176,384]{1,0:T(8,128)(2,1)S(1)}, bf16[176,384]{1,0:T(8,128)(2,1)S(1)}, u32[]{:S(2)}, u32[]{:S(2)}) collective-permute-start(bf16[176,384]{1,0:T(8,128)(2,1)S(1)} %shard_map.119), channel_id=1, source_target_pairs={{0,48},{8,56},{16,0},{24,8},{32,16},{40,24},{48,32},{56,40},{64,11... | collective-permute-start | bytes 405512 | tf_op jit(solution)/shard_map/ppermute | solution.py:29
  25.8 3.8 %collective-permute-start.2 = (bf16[176,384]{1,0:T(8,128)(2,1)S(1)}, bf16[176,384]{1,0:T(8,128)(2,1)S(1)}, u32[]{:S(2)}, u32[]{:S(2)}) collective-permute-start(bf16[176,384]{1,0:T(8,128)(2,1)S(1)} %shard_map.119), channel_id=1, source_target_pairs={{0,32},{8,40},{16,48},{24,56},{32,0},{40,8},{48,16},{56,24},{64,96... | collective-permute-start | bytes 405512 | tf_op jit(solution)/shard_map/ppermute | solution.py:29
  29.6 2.2 %collective-permute-start.4 = (bf16[96,384]{1,0:T(8,128)(2,1)S(1)}, bf16[96,384]{1,0:T(8,128)(2,1)S(1)}, u32[]{:S(2)}, u32[]{:S(2)}) collective-permute-start(bf16[96,384]{1,0:T(8,128)(2,1)S(1)} %shard_map.120.q_ref), channel_id=1, source_target_pairs={{0,64},{8,72},{16,80},{24,88},{32,96},{40,104},{48,112},{56,120},{... | collective-permute-start | bytes 221192 | tf_op jit(solution)/shard_map/ppermute | solution.py:29
  31.8 2.2 %collective-permute-done.4.b_ref = bf16[96,384]{1,0:T(8,128)(2,1)S(1)} collective-permute-done((bf16[96,384]{1,0:T(8,128)(2,1)S(1)}, bf16[96,384]{1,0:T(8,128)(2,1)S(1)}, u32[]{:S(2)}, u32[]{:S(2)}) %collective-permute-start.4) | collective-permute-done | bytes 73760 | tf_op jit(solution)/shard_map/ppermute | solution.py:29
  34.0 3.4 %collective-permute-done.5.c_ref = bf16[96,384]{1,0:T(8,128)(2,1)S(1)} collective-permute-done((bf16[96,384]{1,0:T(8,128)(2,1)S(1)}, bf16[96,384]{1,0:T(8,128)(2,1)S(1)}, u32[]{:S(2)}, u32[]{:S(2)}) %collective-permute-start.5) | collective-permute-done | bytes 73760 | tf_op jit(solution)/shard_map/ppermute | solution.py:29
  37.4 0.3 collective-permute-done.1
  37.7 0.4 collective-permute-done.2
  38.1 0.1 pad_maximum_fusion.kv_ref.near_ref
  38.1 0.1 collective-permute-start.6
  38.2 1.7 %shard_map.121 = (f32[528,256]{1,0:T(8,128)S(1)}, f32[528,128]{1,0:T(8,128)S(1)}) custom-call(bf16[96,384]{1,0:T(8,128)(2,1)S(1)} %collective-permute-done.3.a_ref, bf16[96,384]{1,0:T(8,128)(2,1)S(1)} %collective-permute-done.4.b_ref, bf16[96,384]{1,0:T(8,128)(2,1)S(1)} %collective-permute-done.5.c_ref, bf16[4,176,384]{2,1,0:T(8,128)(2,1)S(1)} %pad_maximum_fusion.kv_ref.near_ref), custom_call_target="tpu_custom_call" | custom-call | flops 1000000 | bytes 1000000 | tf_op jit(solution)/shard_map/pallas_call | solution.py:46
  39.9 0.2 collective-permute-done.6.kv_ref.far_ref
  40.2 2.3 %shard_map.122 = (bf16[176,256]{1,0:T(8,128)(2,1)S(1)}, bf16[176,256]{1,0:T(8,128)(2,1)S(1)}, bf16[176,256]{1,0:T(8,128)(2,1)S(1)}) custom-call(bf16[96,384]{1,0:T(8,128)(2,1)S(1)} %collective-permute-done.3.a_ref, bf16[96,384]{1,0:T(8,128)(2,1)S(1)} %collective-permute-done.4.b_ref, bf16[96,384]{1,0:T(8,128)(2,1)S(1)} %collective-permute-done.5.c_ref, ...), custom_call_target="tpu_custom_call" | custom-call | flops 1000000 | bytes 1000000 | tf_op jit(solution)/shard_map/pallas_call | solution.py:46
  42.5 2.4 %collective-permute-start.7 = (bf16[176,256]{1,0:T(8,128)(2,1)S(1)}, bf16[176,256]{1,0:T(8,128)(2,1)S(1)}, u32[]{:S(2)}, u32[]{:S(2)}) collective-permute-start(bf16[176,256]{1,0:T(8,128)(2,1)S(1)} %get-tuple-element.32), channel_id=1, source_target_pairs={{0,128},{8,136},{16,144},{24,152},{32,160},{40,168},{48,176},{56,1... | collective-permute-start | bytes 270344 | tf_op jit(solution)/shard_map/ppermute | solution.py:29
  44.9 0.7 collective-permute-start.8
  45.6 2.5 %collective-permute-start.9 = (bf16[176,256]{1,0:T(8,128)(2,1)S(1)}, bf16[176,256]{1,0:T(8,128)(2,1)S(1)}, u32[]{:S(2)}, u32[]{:S(2)}) collective-permute-start(bf16[176,256]{1,0:T(8,128)(2,1)S(1)} %get-tuple-element.34), channel_id=1, source_target_pairs={{0,64},{8,72},{16,80},{24,88},{32,96},{40,104},{48,112},{56,120},{... | collective-permute-start | bytes 270344 | tf_op jit(solution)/shard_map/ppermute | solution.py:29
  48.1 1.6 %shard_map.123.d_ref = bf16[176,256]{1,0:T(8,128)(2,1)S(1)} custom-call(bf16[96,384]{1,0:T(8,128)(2,1)S(1)} %shard_map.120.q_ref, bf16[4,176,384]{2,1,0:T(8,128)(2,1)S(1)} %pad_maximum_fusion.kv_ref.near_ref, bf16[4,176,384]{2,1,0:T(8,128)(2,1)S(1)} %collective-permute-done.6.kv_ref.far_ref), custom_call_target="tpu_custom_call" | custom-call | flops 1000000 | bytes 1000000 | tf_op jit(solution)/shard_map/pallas_call | solution.py:46
  49.7 0.0 copy-start.3
  49.8 0.0 copy-start.4
  49.8 0.0 copy-start.5
  49.8 1.3 %collective-permute-done.8.b_ref = bf16[176,256]{1,0:T(8,128)(2,1)S(1)} collective-permute-done((bf16[176,256]{1,0:T(8,128)(2,1)S(1)}, bf16[176,256]{1,0:T(8,128)(2,1)S(1)}, u32[]{:S(2)}, u32[]{:S(2)}) %collective-permute-start.8) | collective-permute-done | bytes 90144 | tf_op jit(solution)/shard_map/ppermute | solution.py:29
  51.1 0.8 shard_map.124
  51.9 14.8 %all_to_all.20.got_ref = bf16[8,24,1536]{2,1,0:T(8,128)(2,1)S(1)} all-to-all(bf16[8,24,1536]{2,1,0:T(8,128)(2,1)S(1)} %shard_map.124), channel_id=1, replica_groups=mesh['seq'=32,'mp'=8] {'mp'}, dimensions={0} | all-to-all | bytes 1179648 | tf_op jit(solution)/shard_map/all_to_all | solution.py:235
  66.7 0.0 copy-start.6
  66.7 1.1 %shard_map.125 = (bf16[22,1536]{1,0:T(8,128)(2,1)S(1)}, bf16[8,24,1536]{2,1,0:T(8,128)(2,1)}) custom-call(bf16[8,24,1536]{2,1,0:T(8,128)(2,1)S(1)} %all_to_all.20.got_ref, bf16[22,1536]{1,0:T(8,128)(2,1)S(1)} %copy-done.3, f32[1536]{0:T(1024)S(1)} %copy-done.4, f32[1536]{0:T(1024)S(1)} %copy-done.5), custom_call_target="tpu_custom_call" | custom-call | flops 1000000 | bytes 1000000 | tf_op jit(solution)/shard_map/pallas_call | solution.py:46
  67.8 3.7 %all-to-all-start.2 = ((bf16[8,24,1536]{2,1,0:T(8,128)(2,1)}), bf16[8,24,1536]{2,1,0:T(8,128)(2,1)S(1)}, u32[]{:S(2)}, u32[]{:S(2)}) async-start(bf16[8,24,1536]{2,1,0:T(8,128)(2,1)} %get-tuple-element.36), calls=%async_computation.2 | async-start | bytes 1179648 | tf_op jit(solution)/shard_map/all_to_all | solution.py:235
  71.6 8.5 %all-to-all-done.2 = bf16[8,24,1536]{2,1,0:T(8,128)(2,1)S(1)} async-done(((bf16[8,24,1536]{2,1,0:T(8,128)(2,1)}), bf16[8,24,1536]{2,1,0:T(8,128)(2,1)S(1)}, u32[]{:S(2)}, u32[]{:S(2)}) %all-to-all-start.2) | async-done | bytes 589856 | tf_op jit(solution)/shard_map/all_to_all | solution.py:235
  80.1 0.2 reshape.36
  80.3 0.3 fusion.2
  80.6 0.0 copy-start.8
  80.6 0.3 fusion.3
  81.0 1.9 %collective-permute-start.10 = (bf16[16,192]{1,0:T(8,128)(2,1)S(1)}, bf16[16,192]{1,0:T(8,128)(2,1)S(1)}, u32[]{:S(2)}, u32[]{:S(2)}) collective-permute-start(bf16[16,192]{1,0:T(8,128)(2,1)S(1)} %get-tuple-element.38), channel_id=1, source_target_pairs={{8,16},{24,32},{40,48},{56,64},{72,80},{88,96},{104,112},{120,128}... | collective-permute-start | bytes 18440 | tf_op jit(solution)/shard_map/ppermute | solution.py:315
  82.9 3.3 %collective-permute-start.11 = (bf16[16,192]{1,0:T(8,128)(2,1)S(1)}, bf16[16,192]{1,0:T(8,128)(2,1)S(1)}, u32[]{:S(2)}, u32[]{:S(2)}) collective-permute-start(bf16[16,192]{1,0:T(8,128)(2,1)S(1)} %get-tuple-element.37), channel_id=1, source_target_pairs={{0,8},{8,0},{16,24},{24,16},{32,40},{40,32},{48,56},{56,48},{64,72... | collective-permute-start | bytes 18440 | tf_op jit(solution)/shard_map/ppermute | solution.py:29
  86.2 2.8 %collective-permute-done.10 = bf16[16,192]{1,0:T(8,128)(2,1)S(1)} collective-permute-done((bf16[16,192]{1,0:T(8,128)(2,1)S(1)}, bf16[16,192]{1,0:T(8,128)(2,1)S(1)}, u32[]{:S(2)}, u32[]{:S(2)}) %collective-permute-start.10) | collective-permute-done | bytes 6176 | tf_op jit(solution)/shard_map/ppermute | solution.py:315
  89.0 1.1 %convolution_convert_fusion = bf16[176,1536]{1,0:T(8,128)(2,1)S(1)} fusion(bf16[192,1536]{1,0:T(8,128)(2,1)S(1)} %copy-done, bf16[176,192]{1,0:T(8,128)(2,1)S(1)} %fusion.3, bf16[15,192]{1,0:T(8,128)(2,1)S(1)} %get-tuple-element.71, bf16[15,192]{1,0:T(8,128)(2,1)S(1)} %get-tuple-element.70, f32[192]{0:T(256)S(1)} %copy-done.8, f32[192]{0:T(256)S(1)} %copy-done.9, ...), kind=kOutput, calls=%fused_computation | convolution fusion | flops 110466048 | bytes 1234944 | tf_op jit(solution)/shard_map/dot_general | solution.py:62
  90.1 0.2 reshape.37
  90.2 12.5 %all_to_all.21 = bf16[8,22,1536]{2,1,0:T(8,128)(2,1)S(1)} all-to-all(bf16[8,22,1536]{2,1,0:T(8,128)(2,1)S(1)} %reshape.37), channel_id=1, replica_groups=mesh['seq'=32,'mp'=8] {'mp'}, dimensions={0} | all-to-all | bytes 1081344 | tf_op jit(solution)/shard_map/all_to_all | solution.py:235
  102.7 0.1 convert_reduce_fusion
  102.8 0.7 add_convert_fusion
  (29 shorter events, 0.1 us)
Async XLA Ops:
  0.0 89.0 %copy-start = (bf16[192,1536]{1,0:T(8,128)(2,1)S(1)}, bf16[192,1536]{1,0:T(8,128)(2,1)}, u32[]{:S(2)}) copy-start(bf16[192,1536]{1,0:T(8,128)(2,1)} %param.23) | copy-start | bytes 1769476
  2.0 15.7 %all-to-all-start = ((bf16[8,24,1536]{2,1,0:T(8,128)(2,1)}), bf16[8,24,1536]{2,1,0:T(8,128)(2,1)S(1)}, u32[]{:S(2)}, u32[]{:S(2)}) async-start(bf16[8,24,1536]{2,1,0:T(8,128)(2,1)} %shard_map.118), calls=%async_computation | async-start | bytes 1179648 | tf_op jit(solution)/shard_map/all_to_all | solution.py:235
  7.7 10.0 %copy-start.1 = (bf16[3,192,1536]{2,1,0:T(8,128)(2,1)S(1)}, bf16[3,192,1536]{2,1,0:T(8,128)(2,1)}, u32[]{:S(2)}) copy-start(bf16[3,192,1536]{2,1,0:T(8,128)(2,1)} %w_ref.4) | copy-start | bytes 5308420
  19.1 12.7 %collective-permute-start.3 = (bf16[96,384]{1,0:T(8,128)(2,1)S(1)}, bf16[96,384]{1,0:T(8,128)(2,1)S(1)}, u32[]{:S(2)}, u32[]{:S(2)}) collective-permute-start(bf16[96,384]{1,0:T(8,128)(2,1)S(1)} %shard_map.120.q_ref), channel_id=1, source_target_pairs={{0,128},{8,136},{16,144},{24,152},{32,160},{40,168},{48,176},{56,1... | collective-permute-start | bytes 221192 | tf_op jit(solution)/shard_map/ppermute | solution.py:29
  20.4 17.0 %collective-permute-start = (bf16[176,384]{1,0:T(8,128)(2,1)S(1)}, bf16[176,384]{1,0:T(8,128)(2,1)S(1)}, u32[]{:S(2)}, u32[]{:S(2)}) collective-permute-start(bf16[176,384]{1,0:T(8,128)(2,1)S(1)} %shard_map.119), channel_id=1, source_target_pairs={{0,48},{8,56},{16,0},{24,8},{32,16},{40,24},{48,32},{56,40},{64,11... | collective-permute-start | bytes 405512 | tf_op jit(solution)/shard_map/ppermute | solution.py:29
  25.8 11.9 %collective-permute-start.1 = (bf16[176,384]{1,0:T(8,128)(2,1)S(1)}, bf16[176,384]{1,0:T(8,128)(2,1)S(1)}, u32[]{:S(2)}, u32[]{:S(2)}) collective-permute-start(bf16[176,384]{1,0:T(8,128)(2,1)S(1)} %shard_map.119), channel_id=1, source_target_pairs={{0,16},{8,24},{16,32},{24,40},{32,48},{40,56},{48,0},{56,8},{64,80... | collective-permute-start | bytes 405512 | tf_op jit(solution)/shard_map/ppermute | solution.py:29
  25.8 12.2 %collective-permute-start.2 = (bf16[176,384]{1,0:T(8,128)(2,1)S(1)}, bf16[176,384]{1,0:T(8,128)(2,1)S(1)}, u32[]{:S(2)}, u32[]{:S(2)}) collective-permute-start(bf16[176,384]{1,0:T(8,128)(2,1)S(1)} %shard_map.119), channel_id=1, source_target_pairs={{0,32},{8,40},{16,48},{24,56},{32,0},{40,8},{48,16},{56,24},{64,96... | collective-permute-start | bytes 405512 | tf_op jit(solution)/shard_map/ppermute | solution.py:29
  29.6 4.4 %collective-permute-start.4 = (bf16[96,384]{1,0:T(8,128)(2,1)S(1)}, bf16[96,384]{1,0:T(8,128)(2,1)S(1)}, u32[]{:S(2)}, u32[]{:S(2)}) collective-permute-start(bf16[96,384]{1,0:T(8,128)(2,1)S(1)} %shard_map.120.q_ref), channel_id=1, source_target_pairs={{0,64},{8,72},{16,80},{24,88},{32,96},{40,104},{48,112},{56,120},{... | collective-permute-start | bytes 221192 | tf_op jit(solution)/shard_map/ppermute | solution.py:29
  31.8 5.6 %collective-permute-start.5 = (bf16[96,384]{1,0:T(8,128)(2,1)S(1)}, bf16[96,384]{1,0:T(8,128)(2,1)S(1)}, u32[]{:S(2)}, u32[]{:S(2)}) collective-permute-start(bf16[96,384]{1,0:T(8,128)(2,1)S(1)} %shard_map.120.q_ref), channel_id=1, source_target_pairs={{0,192},{8,200},{16,208},{24,216},{32,224},{40,232},{48,240},{56,2... | collective-permute-start | bytes 221192 | tf_op jit(solution)/shard_map/ppermute | solution.py:29
  38.1 2.0 %collective-permute-start.6 = (bf16[4,176,384]{2,1,0:T(8,128)(2,1)S(1)}, bf16[4,176,384]{2,1,0:T(8,128)(2,1)S(1)}, u32[]{:S(2)}, u32[]{:S(2)}) collective-permute-start(bf16[4,176,384]{2,1,0:T(8,128)(2,1)S(1)} %pad_maximum_fusion.kv_ref.near_ref), channel_id=1, source_target_pairs={{0,8},{8,0},{16,24},{24,16},{32,40},{40,32},{48,56},{56,48},{64,72... | collective-permute-start | bytes 1622024 | tf_op jit(solution)/shard_map/ppermute | solution.py:29
  40.2 10.9 %copy-start.2 = (bf16[192,1536]{1,0:T(8,128)(2,1)S(1)}, bf16[192,1536]{1,0:T(8,128)(2,1)}, u32[]{:S(2)}) copy-start(bf16[192,1536]{1,0:T(8,128)(2,1)} %w_ref.5) | copy-start | bytes 1769476
  42.5 7.3 %collective-permute-start.7 = (bf16[176,256]{1,0:T(8,128)(2,1)S(1)}, bf16[176,256]{1,0:T(8,128)(2,1)S(1)}, u32[]{:S(2)}, u32[]{:S(2)}) collective-permute-start(bf16[176,256]{1,0:T(8,128)(2,1)S(1)} %get-tuple-element.32), channel_id=1, source_target_pairs={{0,128},{8,136},{16,144},{24,152},{32,160},{40,168},{48,176},{56,1... | collective-permute-start | bytes 270344 | tf_op jit(solution)/shard_map/ppermute | solution.py:29
  44.9 6.2 %collective-permute-start.8 = (bf16[176,256]{1,0:T(8,128)(2,1)S(1)}, bf16[176,256]{1,0:T(8,128)(2,1)S(1)}, u32[]{:S(2)}, u32[]{:S(2)}) collective-permute-start(bf16[176,256]{1,0:T(8,128)(2,1)S(1)} %get-tuple-element.33), channel_id=1, source_target_pairs={{0,192},{8,200},{16,208},{24,216},{32,224},{40,232},{48,240},{56,2... | collective-permute-start | bytes 270344 | tf_op jit(solution)/shard_map/ppermute | solution.py:29
  45.6 5.4 %collective-permute-start.9 = (bf16[176,256]{1,0:T(8,128)(2,1)S(1)}, bf16[176,256]{1,0:T(8,128)(2,1)S(1)}, u32[]{:S(2)}, u32[]{:S(2)}) collective-permute-start(bf16[176,256]{1,0:T(8,128)(2,1)S(1)} %get-tuple-element.34), channel_id=1, source_target_pairs={{0,64},{8,72},{16,80},{24,88},{32,96},{40,104},{48,112},{56,120},{... | collective-permute-start | bytes 270344 | tf_op jit(solution)/shard_map/ppermute | solution.py:29
  49.7 16.9 %copy-start.3 = (bf16[22,1536]{1,0:T(8,128)(2,1)S(1)}, bf16[22,1536]{1,0:T(8,128)(2,1)}, u32[]{:S(2)}) copy-start(bf16[22,1536]{1,0:T(8,128)(2,1)} %x_ref.1) | copy-start | bytes 202756
  49.8 16.9 %copy-start.4 = (f32[1536]{0:T(1024)S(1)}, f32[1536]{0:T(1024)}, u32[]{:S(2)}) copy-start(f32[1536]{0:T(1024)} %gain_ref.1) | copy-start | bytes 18436
  49.8 16.9 %copy-start.5 = (f32[1536]{0:T(1024)S(1)}, f32[1536]{0:T(1024)}, u32[]{:S(2)}) copy-start(f32[1536]{0:T(1024)} %shift_ref.1) | copy-start | bytes 18436
  66.7 4.8 %copy-start.6 = (f32[31,192]{1,0:T(8,128)S(1)}, f32[31,192]{1,0:T(8,128)}, u32[]{:S(2)}) copy-start(f32[31,192]{1,0:T(8,128)} %param.20) | copy-start | bytes 71428
  67.8 12.4 %copy-start.7 = (bf16[2,192,1536]{2,1,0:T(8,128)(2,1)S(1)}, bf16[2,192,1536]{2,1,0:T(8,128)(2,1)}, u32[]{:S(2)}) copy-start(bf16[2,192,1536]{2,1,0:T(8,128)(2,1)} %param.19) | copy-start | bytes 3538948
  67.8 12.3 %all-to-all-start.2 = ((bf16[8,24,1536]{2,1,0:T(8,128)(2,1)}), bf16[8,24,1536]{2,1,0:T(8,128)(2,1)S(1)}, u32[]{:S(2)}, u32[]{:S(2)}) async-start(bf16[8,24,1536]{2,1,0:T(8,128)(2,1)} %get-tuple-element.36), calls=%async_computation.2 | async-start | bytes 1179648 | tf_op jit(solution)/shard_map/all_to_all | solution.py:235
  80.6 8.4 %copy-start.8 = (f32[192]{0:T(256)S(1)}, f32[192]{0:T(256)}, u32[]{:S(2)}) copy-start(f32[192]{0:T(256)} %param.22) | copy-start | bytes 2308
  80.6 8.4 %copy-start.9 = (f32[192]{0:T(256)S(1)}, f32[192]{0:T(256)}, u32[]{:S(2)}) copy-start(f32[192]{0:T(256)} %param.21) | copy-start | bytes 2308
  81.0 8.0 %collective-permute-start.10 = (bf16[16,192]{1,0:T(8,128)(2,1)S(1)}, bf16[16,192]{1,0:T(8,128)(2,1)S(1)}, u32[]{:S(2)}, u32[]{:S(2)}) collective-permute-start(bf16[16,192]{1,0:T(8,128)(2,1)S(1)} %get-tuple-element.38), channel_id=1, source_target_pairs={{8,16},{24,32},{40,48},{56,64},{72,80},{88,96},{104,112},{120,128}... | collective-permute-start | bytes 18440 | tf_op jit(solution)/shard_map/ppermute | solution.py:315
  82.9 6.1 %collective-permute-start.11 = (bf16[16,192]{1,0:T(8,128)(2,1)S(1)}, bf16[16,192]{1,0:T(8,128)(2,1)S(1)}, u32[]{:S(2)}, u32[]{:S(2)}) collective-permute-start(bf16[16,192]{1,0:T(8,128)(2,1)S(1)} %get-tuple-element.37), channel_id=1, source_target_pairs={{0,8},{8,0},{16,24},{24,16},{32,40},{40,32},{48,56},{56,48},{64,72... | collective-permute-start | bytes 18440 | tf_op jit(solution)/shard_map/ppermute | solution.py:29
